TPU v7x, 32 devices: a whole 2x2x4 slice. The times are simulated.
32 devices in a mesh: span: 4 (over x, core), seq: 4 (over z), mp: 2 (over y).
Axes of the slice: x: 2, y: 2, z: 4, core: 2. Of those that a mesh axis runs over, the one named last changes fastest.
Arguments:
- queries: bfloat16 [4, 256, 3072], P('span', 'seq', 'mp'), may hold values from -256 to 256
- keys_values: bfloat16 [2, 4, 256, 512], P(None, 'span', 'seq', 'mp'), may hold values from -200 to 200
- clip_tokens: int32 [4], replicated, may hold values from 64 to 256, as said below
- noise_level: int32 [4], replicated, may hold values from 0 to 63
- level_gate: bfloat16 [64, 3072], P(None, 'mp'), may hold values from -3 to 3
- out_gain: bfloat16 [3072], P('mp'), may hold values from 0.099609375 to 1.8984375
Outputs:
- layer_out: bfloat16 [4, 256, 3072], P('span', 'seq', 'mp')
Inputs may be any that keep to these rules, and one draw needn't show every extreme that they name: `clip_tokens`: each clip's live slots are its first ones; some clip fills all 256 slots.
All inputs are finite; a program needn't handle non-finite values.
Results may differ from a plain program's by a relative error of at most 0.0065.
Values may be sent and summed in bfloat16 or wider, within the bound.
No kernel may reach another device: no remote copies, remote signals or barrier semaphores. Data moves between devices by JAX's collectives and lax.ppermute only.
A program may use at most 64 MiB of HBM per device.

v0:
```python
import math

import jax
import jax.numpy as jnp
from jax import lax
from jax.sharding import PartitionSpec as P

HEADS = 24
KVH = 4
HD = 128


def passed_along(shard, axis, by):
    peers = lax.axis_size(axis)
    pairs = [(i, i + by) for i in range(peers) if 0 <= i + by < peers]
    return lax.ppermute(shard, axis, pairs)


def per_device(queries, keys_values, clip_tokens, noise_level, level_gate, out_gain):
    tokens_here = queries.shape[1]
    slot_count = tokens_here * lax.axis_size("seq")
    clip_count = clip_tokens.shape[0]
    kv_heads_here = keys_values.shape[-1] // HD
    group_size = HEADS // KVH
    own_clip = lax.axis_index("span")
    own_seq = lax.axis_index("seq")
    query_heads = queries[0].reshape(tokens_here, kv_heads_here, group_size, HD)
    score_scale = 1.0 / math.sqrt(HD)
    clip_ids = jnp.arange(clip_count, dtype=jnp.int32)

    def clip_length(which):
        return jnp.sum(
            jnp.where(which[:, None] == clip_ids[None, :], clip_tokens[None, :], 0), axis=1
        )

    def block_step(running, key_block, first):
        key_count = key_block.shape[1]
        positions = first + jnp.arange(key_count, dtype=jnp.int32)
        holder = positions // slot_count
        slot_index = positions - holder * slot_count
        usable = (holder >= 0) & (holder <= own_clip) & (slot_index < clip_length(holder))

        def update(state):
            running_max, weight_sum, weighted = state
            key_rows = key_block[0].reshape(key_count, kv_heads_here, HD)
            value_rows = key_block[1].reshape(key_count, kv_heads_here, HD)
            scores = (
                jnp.einsum(
                    "tgrd,kgd->tgrk", query_heads, key_rows, preferred_element_type=jnp.float32
                )
                * score_scale
            )
            scores = jnp.where(usable[None, None, None, :], scores, -jnp.inf)
            new_max = jnp.maximum(running_max, jnp.max(scores, axis=-1))
            weights = jnp.exp(scores - new_max[..., None])
            shrink = jnp.exp(running_max - new_max)
            weight_sum = weight_sum * shrink + jnp.sum(weights, axis=-1)
            weighted = weighted * shrink[..., None] + jnp.einsum(
                "tgrk,kgd->tgrd",
                weights.astype(jnp.bfloat16),
                value_rows,
                preferred_element_type=jnp.float32,
            )
            return (new_max, weight_sum, weighted)

        def unchanged(state):
            return state

        return lax.cond(jnp.any(usable), update, unchanged, running)

    def fold_piece(running, kv_piece, first):
        key_count = kv_piece.shape[1]
        if key_count > 1024 and key_count % 1024 == 0:

            def loop_step(block_index, state):
                key_block = lax.dynamic_slice_in_dim(kv_piece, block_index * 1024, 1024, 1)
                return block_step(state, key_block, first + block_index * 1024)

            return lax.fori_loop(0, key_count // 1024, loop_step, running)
        return block_step(running, kv_piece, first)

    initial = (
        jnp.full((tokens_here, kv_heads_here, group_size), -jnp.inf, jnp.float32),
        jnp.zeros((tokens_here, kv_heads_here, group_size), jnp.float32),
        jnp.zeros((tokens_here, kv_heads_here, group_size, HD), jnp.float32),
    )
    local_kv = keys_values[:, 0]
    clip_kv = lax.all_gather(local_kv, "seq", axis=1, tiled=True)
    running = fold_piece(initial, clip_kv, own_clip * slot_count)
    for distance in range(1, clip_count):
        clip_kv = passed_along(clip_kv, "span", 1)
        running = fold_piece(running, clip_kv, (own_clip - distance) * slot_count)
    running_max, weight_sum, weighted = running
    attended = (weighted / weight_sum[..., None]).reshape(
        tokens_here, kv_heads_here * group_size * HD
    )
    squares = jnp.sum(attended * attended, axis=1)
    mean_square = lax.psum(squares, "mp") / (HEADS * HD)
    own_level = jnp.sum(jnp.where(clip_ids == own_clip, noise_level, 0))
    one_hot = (jnp.arange(level_gate.shape[0], dtype=jnp.int32) == own_level).astype(jnp.bfloat16)
    gate_row = jnp.dot(one_hot, level_gate, preferred_element_type=jnp.float32)
    own_length = jnp.sum(jnp.where(clip_ids == own_clip, clip_tokens, 0))
    usable_rows = own_seq * tokens_here + jnp.arange(tokens_here, dtype=jnp.int32) < own_length
    normed = (
        attended
        * lax.rsqrt(mean_square + 1e-06)[:, None]
        * out_gain.astype(jnp.float32)
        * (1.0 + gate_row)
    )
    return jnp.where(usable_rows[:, None], normed, 0.0).astype(jnp.bfloat16)[None]


def solution(mesh):
    placed = (
        P("span", "seq", "mp"),
        P(None, "span", "seq", "mp"),
        P(),
        P(),
        P(None, "mp"),
        P("mp"),
    )
    return jax.shard_map(
        per_device, mesh=mesh, in_specs=placed, out_specs=P("span", "seq", "mp"), check_vma=False
    )
```

profile of v0, /device:TPU:14, one launch (start us, length us, event | category | flops | bytes accessed | tf_op | source)
XLA Modules:
  0.0 54.9 jit_solution(6567961110237758740)
XLA Ops:
  0.0 0.9 %copy.49 = bf16[2,1,64,256]{3,0,1,2:T(2,128)(2,1)S(1)} copy(bf16[2,1,64,256]{3,2,1,0:T(8,128)(2,1)} %param.15) | data formatting | bytes 131072 | tf_op args[1]
  1.0 14.6 %all-gather = bf16[2,1,256,256]{3,0,1,2:T(2,128)(2,1)S(1)} all-gather(bf16[2,1,64,256]{3,0,1,2:T(2,128)(2,1)S(1)} %copy.49), channel_id=2, replica_groups=mesh['span'=4,'seq'=4,'mp'=2] {'seq'}, dimensions={2}, use_global_device_ids=true | all-gather | bytes 327680 | tf_op jit(solution)/shard_map/all_gather | solution.py:88
  15.6 2.0 %collective-permute-start = (bf16[2,256,256]{2,0,1:T(2,128)(2,1)S(1)}, bf16[2,256,256]{2,0,1:T(2,128)(2,1)S(1)}, u32[]{:S(2)}, u32[]{:S(2)}) collective-permute-start(bf16[2,256,256]{2,0,1:T(2,128)(2,1)S(1)} %bitcast.77), channel_id=1, source_target_pairs={{0,8},{8,16},{16,24},{1,9},{9,17},{17,25},{2,10},{10,18},{18,26},{... | collective-permute-start | bytes 786440 | tf_op jit(solution)/shard_map/ppermute | solution.py:16
  17.8 0.6 %fusion.42 = (pred[]{:T(512)}, pred[256]{0:T(512)(128)(4,1)S(1)}) fusion(s32[256]{0:T(256)S(1)} %get-tuple-element.172, s32[]{:T(128)S(6)} %axis_index.28, s32[]{:T(128)S(6)} %mul.131), kind=kLoop, calls=%fused_computation.98 | loop fusion | flops 6143 | bytes 1289 | tf_op jit(solution)/shard_map/reduce_or | solution.py:69
  18.4 0.7 %fusion.41 = (pred[]{:T(512)}, pred[256]{0:T(512)(128)(4,1)S(1)}) fusion(s32[256]{0:T(256)S(1)} %get-tuple-element.170, s32[]{:T(128)S(6)} %axis_index.28, s32[]{:T(128)S(6)} %mul.133), kind=kLoop, calls=%fused_computation.97 | loop fusion | flops 6143 | bytes 1289 | tf_op jit(solution)/shard_map/reduce_or | solution.py:69
  19.1 0.7 %fusion.36 = s32[]{:T(128)} fusion(s32[4]{0:T(128)S(1)} %copy-done.4, s32[]{:T(128)S(6)} %axis_index.28), kind=kLoop, calls=%fused_computation.90 | loop fusion | flops 11 | bytes 24 | tf_op jit(solution)/shard_map/reduce_sum | solution.py:99
  19.8 0.8 %convolution_reduce_fusion = f32[1536]{0:T(1024)S(1)} fusion(bf16[64,1536]{1,0:T(8,128)(2,1)S(1)} %copy-done, s32[]{:T(128)} %fusion.36), kind=kOutput, calls=%fused_computation.48 | convolution fusion | flops 196672 | bytes 202756 | tf_op jit(solution)/shard_map/dot_general | solution.py:101
  20.7 0.6 %fusion.40 = (pred[]{:T(512)}, pred[256]{0:T(512)(128)(4,1)S(1)}) fusion(s32[256]{0:T(256)S(1)} %get-tuple-element.171, s32[]{:T(128)S(6)} %axis_index.28, s32[]{:T(128)S(6)} %mul.135), kind=kLoop, calls=%fused_computation.96 | loop fusion | flops 6143 | bytes 1289 | tf_op jit(solution)/shard_map/reduce_or | solution.py:69
  21.3 2.1 %collective-permute-done = bf16[2,256,256]{2,0,1:T(2,128)(2,1)S(1)} collective-permute-done((bf16[2,256,256]{2,0,1:T(2,128)(2,1)S(1)}, bf16[2,256,256]{2,0,1:T(2,128)(2,1)S(1)}, u32[]{:S(2)}, u32[]{:S(2)}) %collective-permute-start) | collective-permute-done | bytes 262176 | tf_op jit(solution)/shard_map/ppermute | solution.py:16
  23.4 1.9 %collective-permute-start.1 = (bf16[2,256,256]{2,0,1:T(2,128)(2,1)S(1)}, bf16[2,256,256]{2,0,1:T(2,128)(2,1)}, u32[]{:S(2)}, u32[]{:S(2)}) collective-permute-start(bf16[2,256,256]{2,0,1:T(2,128)(2,1)S(1)} %collective-permute-done), channel_id=1, source_target_pairs={{0,8},{8,16},{16,24},{1,9},{9,17},{17,25},{2,10},{10,18},{18,26},{... | collective-permute-start | bytes 786440 | tf_op jit(solution)/shard_map/ppermute | solution.py:16
  25.3 0.7 %fusion.35 = s32[]{:T(128)} fusion(s32[4]{0:T(128)S(1)} %copy-done.3, s32[]{:T(128)S(6)} %axis_index.28), kind=kLoop, calls=%fused_computation.89 | loop fusion | flops 11 | bytes 24 | tf_op jit(solution)/shard_map/reduce_sum | solution.py:102
  26.0 0.7 %fusion.39 = (pred[]{:T(512)}, pred[256]{0:T(512)(128)(4,1)S(1)}) fusion(s32[256]{0:T(256)S(1)} %get-tuple-element.169, s32[]{:T(128)S(6)} %axis_index.28, s32[]{:T(128)S(6)} %mul.137), kind=kLoop, calls=%fused_computation.95 | loop fusion | flops 6143 | bytes 1289 | tf_op jit(solution)/shard_map/reduce_or | solution.py:69
  26.7 4.5 %collective-permute-done.1 = bf16[2,256,256]{2,0,1:T(2,128)(2,1)} collective-permute-done((bf16[2,256,256]{2,0,1:T(2,128)(2,1)S(1)}, bf16[2,256,256]{2,0,1:T(2,128)(2,1)}, u32[]{:S(2)}, u32[]{:S(2)}) %collective-permute-start.1) | collective-permute-done | bytes 262176 | tf_op jit(solution)/shard_map/ppermute | solution.py:16
  31.2 1.9 %collective-permute-start.2 = (bf16[2,256,256]{2,0,1:T(2,128)(2,1)}, bf16[2,256,256]{2,0,1:T(2,128)(2,1)S(1)}, u32[]{:S(2)}, u32[]{:S(2)}) collective-permute-start(bf16[2,256,256]{2,0,1:T(2,128)(2,1)} %collective-permute-done.1), channel_id=1, source_target_pairs={{0,8},{8,16},{16,24},{1,9},{9,17},{17,25},{2,10},{10,18},{18,26},{... | collective-permute-start | bytes 786440 | tf_op jit(solution)/shard_map/ppermute | solution.py:16
  33.1 0.6 %add_compare_fusion = pred[64]{0:T(512)(128)(4,1)S(1)} fusion(s32[]{:T(128)} %fusion.35, s32[]{:T(128)S(6)} %mul.130), kind=kLoop, calls=%fused_computation.93 | loop fusion | flops 128 | bytes 72 | tf_op jit(solution)/shard_map/lt | solution.py:103
  36.5 0.4 copy-done.2
  37.0 3.9 %conditional.4 = (f32[64,2,6]{0,2,1:T(8,128)}, f32[64,2,6]{0,2,1:T(8,128)S(1)}, f32[64,2,6,128]{3,0,2,1:T(8,128)S(1)}) conditional(s32[]{:T(128)} %convert_element_type.41, () %tuple.32, (pred[256]{0:T(512)(128)(4,1)S(1)}, bf16[2,256,256]{2,0,1:T(2,128)(2,1)S(1)}, bf16[64,2,6,128]{3,2,1,0:T(8,128)(2,1)S(1)}) %tuple.86), branch_computations={%region_9.10_spmd, %region_10.13_spmd} | conditional | flops 102138624 | bytes 4287768 | solution.py:69
  37.2 0.9 %fusion.44 = (f32[64,2,6]{0,2,1:T(8,128)}, f32[64,2,6,256]{3,0,2,1:T(8,128)S(1)}) fusion(bf16[256,2,128,1]{0,2,3,1:T(8,128)(2,1)S(1)} %bitcast.83, bf16[64,2,6,128]{3,2,1,0:T(8,128)(2,1)S(1)} %get-tuple-element.150, pred[256]{0:T(512)(128)(4,1)S(1)} %get-tuple-element.63), kind=kOutput, calls=%fused_computation.100 | convolution fusion | flops 50920704 | bytes 1117440 | tf_op jit(solution)/shard_map/cond/branch_1_fun/tgrd,kgd->tgrk/dot_general | solution.py:48
  38.1 1.0 %fusion.4 = f32[64,2,6]{0,2,1:T(8,128)S(1)} fusion(f32[64,2,6,256]{3,0,2,1:T(8,128)S(1)} %get-tuple-element.194, f32[64,2,6]{0,2,1:T(8,128)} %get-tuple-element.214), kind=kLoop, calls=%fused_computation.7 | loop fusion | flops 392448 | bytes 792576 | tf_op jit(solution)/shard_map/cond/branch_1_fun/reduce_sum | solution.py:57
  39.1 0.7 %exponential_multiply_fusion = (f32[64,2,6]{0,2,1:T(8,128)S(1)}, f32[64,2,6]{0,2,1:T(8,128)S(1)}) fusion(f32[64,2,6]{0,2,1:T(8,128)} %get-tuple-element.214, f32[64,2,6]{0,2,1:T(8,128)S(1)} %fusion.4), kind=kLoop, calls=%fused_computation.10 | loop fusion | flops 2304 | bytes 12288 | tf_op jit(solution)/shard_map/cond/branch_1_fun/mul;broadcast_in_dim | solution.py:57
  39.8 1.0 %fusion.2 = f32[64,2,6,128]{3,0,2,1:T(8,128)S(1)} fusion(bf16[256,2,128,1]{0,2,3,1:T(8,128)(2,1)S(1)} %bitcast.82, f32[64,2,6,256]{3,0,2,1:T(8,128)S(1)} %get-tuple-element.194, f32[64,2,6]{0,2,1:T(8,128)} %get-tuple-element.214, f32[64,2,6]{0,2,1:T(8,128)S(1)} %get-tuple-element.191), kind=kOutput, calls=%fused_computation.4 | convolution fusion | flops 50823168 | bytes 1316864 | tf_op jit(solution)/shard_map/cond/branch_1_fun/tgrk,kgd->tgrd/dot_general | solution.py:58
  40.9 3.3 %conditional.5 = ((f32[64,2,6]{0,2,1:T(8,128)}, f32[64,2,6]{0,2,1:T(8,128)S(1)}, f32[64,2,6,128]{3,0,2,1:T(8,128)S(1)})) conditional(s32[]{:T(128)} %convert_element_type.40, (f32[64,2,6]{0,2,1:T(8,128)}, f32[64,2,6]{0,2,1:T(8,128)S(1)}, f32[64,2,6,128]{3,0,2,1:T(8,128)S(1)}) %conditional.4, (pred[256]{0:T(512)(128)(4,1)S(1)}, ...), branch_computations={%region_13.14_spmd, %region_14.17_spmd} | conditional | flops 102237696 | bytes 4702496 | solution.py:69
  41.5 0.7 %max.6 = f32[64,2,6]{0,2,1:T(8,128)S(1)} maximum(f32[64,2,6]{0,2,1:T(8,128)} %get-tuple-element.66, f32[64,2,6]{0,2,1:T(8,128)S(1)} %get-tuple-element.197) | non-fusion elementwise | flops 768 | bytes 9216 | tf_op jit(solution)/shard_map/cond/branch_1_fun/max | solution.py:54
  42.5 0.7 %multiply_add_fusion = (f32[64,2,6]{0,2,1:T(8,128)S(1)}, f32[64,2,6]{0,2,1:T(8,128)S(1)}) fusion(f32[64,2,6]{0,2,1:T(8,128)S(1)} %fusion.13, f32[64,2,6]{0,2,1:T(8,128)S(1)} %get-tuple-element.70, f32[64,2,6]{0,2,1:T(8,128)} %get-tuple-element.66, f32[64,2,6]{0,2,1:T(8,128)S(1)} %max.6), kind=kLoop, calls=%fused_computation.22 | loop fusion | flops 2304 | bytes 18432 | tf_op jit(solution)/shard_map/cond/branch_1_fun/add | solution.py:57
  43.2 0.6 %copy.108 = f32[64,2,6]{0,2,1:T(8,128)} copy(f32[64,2,6]{0,2,1:T(8,128)S(1)} %max.6) | data formatting | bytes 6144 | tf_op jit(solution)/shard_map/cond
  44.2 4.2 %conditional.6 = ((f32[64,2,6]{0,2,1:T(8,128)}, f32[64,2,6]{0,2,1:T(8,128)S(1)}, f32[64,2,6,128]{3,0,2,1:T(8,128)S(1)})) conditional(s32[]{:T(128)} %convert_element_type.39, (f32[64,2,6]{0,2,1:T(8,128)}, f32[64,2,6]{0,2,1:T(8,128)S(1)}, f32[64,2,6,128]{3,0,2,1:T(8,128)S(1)}) %get-tuple-element.233, (pred[256]{0:T(512)(128)(4,1)S(1)}, ...), branch_computations={%region_17.18_spmd, %region_18.21_spmd} | conditional | flops 102237696 | bytes 4702496 | solution.py:69
  44.2 1.1 %copy.54 = bf16[2,256,256]{1,2,0:T(8,128)(2,1)S(1)} copy(bf16[2,256,256]{2,0,1:T(2,128)(2,1)} %get-tuple-element.158) | data formatting | bytes 524288 | tf_op jit(solution)/shard_map
  45.7 0.7 %max.7 = f32[64,2,6]{0,2,1:T(8,128)S(1)} maximum(f32[64,2,6]{0,2,1:T(8,128)} %get-tuple-element.72, f32[64,2,6]{0,2,1:T(8,128)S(1)} %get-tuple-element.201) | non-fusion elementwise | flops 768 | bytes 9216 | tf_op jit(solution)/shard_map/cond/branch_1_fun/max | solution.py:54
  46.7 0.7 %multiply_add_fusion.1 = (f32[64,2,6]{0,2,1:T(8,128)S(1)}, f32[64,2,6]{0,2,1:T(8,128)S(1)}) fusion(f32[64,2,6]{0,2,1:T(8,128)S(1)} %fusion.21, f32[64,2,6]{0,2,1:T(8,128)S(1)} %get-tuple-element.76, f32[64,2,6]{0,2,1:T(8,128)} %get-tuple-element.72, f32[64,2,6]{0,2,1:T(8,128)S(1)} %max.7), kind=kLoop, calls=%fused_computation.34 | loop fusion | flops 2304 | bytes 18432 | tf_op jit(solution)/shard_map/cond/branch_1_fun/add | solution.py:57
  47.4 0.6 %copy.114 = f32[64,2,6]{0,2,1:T(8,128)} copy(f32[64,2,6]{0,2,1:T(8,128)S(1)} %max.7) | data formatting | bytes 6144 | tf_op jit(solution)/shard_map/cond
  49.1 4.9 %psum.7 = f32[64]{0:T(128)S(1)} all-reduce(f32[64]{0:T(128)S(1)} %get-tuple-element.179), channel_id=1, replica_groups=mesh['span'=4,'seq'=4,'mp'=2] {'mp'}, use_global_device_ids=true, to_apply=%region_26.27 | all-reduce | flops 64 | bytes 512 | tf_op jit(solution)/shard_map/psum | solution.py:98
  54.1 0.8 %select_convert_fusion = bf16[1,64,1536]{2,1,0:T(8,128)(2,1)} fusion(f32[1,64,1536]{2,1,0:T(8,128)S(1)} %reshape.204, f32[1536]{0:T(1024)S(1)} %broadcast_add_fusion, f32[1536]{0:T(1024)S(1)} %convert_element_type.42, f32[64]{0:T(128)S(1)} %add_rsqrt_fusion, pred[64]{0:T(512)(128)(4,1)S(1)} %add_compare_fusion), kind=kLoop, calls=%fused_computation.49 | loop fusion | flops 491520 | bytes 602432 | tf_op jit(solution)/shard_map/convert_element_type | solution.py:110
  (32 shorter events, 3.5 us)
Async XLA Ops:
  0.0 19.8 %copy-start = (bf16[64,1536]{1,0:T(8,128)(2,1)S(1)}, bf16[64,1536]{1,0:T(8,128)(2,1)}, u32[]{:S(2)}) copy-start(bf16[64,1536]{1,0:T(8,128)(2,1)} %param.18) | copy-start | bytes 589828
  1.0 16.7 %copy-start.3 = (s32[4]{0:T(128)S(1)}, s32[4]{0:T(128)}, u32[]{:S(2)}) copy-start(s32[4]{0:T(128)} %param.16) | copy-start | bytes 52
  1.0 18.1 %copy-start.4 = (s32[4]{0:T(128)S(1)}, s32[4]{0:T(128)}, u32[]{:S(2)}) copy-start(s32[4]{0:T(128)} %param.17) | copy-start | bytes 52
  15.6 20.7 %copy-start.1 = (bf16[1,64,1536]{2,1,0:T(8,128)(2,1)S(1)}, bf16[1,64,1536]{2,1,0:T(8,128)(2,1)}, u32[]{:S(2)}) copy-start(bf16[1,64,1536]{2,1,0:T(8,128)(2,1)} %param.14) | copy-start | bytes 589828
  15.6 7.8 %collective-permute-start = (bf16[2,256,256]{2,0,1:T(2,128)(2,1)S(1)}, bf16[2,256,256]{2,0,1:T(2,128)(2,1)S(1)}, u32[]{:S(2)}, u32[]{:S(2)}) collective-permute-start(bf16[2,256,256]{2,0,1:T(2,128)(2,1)S(1)} %bitcast.77), channel_id=1, source_target_pairs={{0,8},{8,16},{16,24},{1,9},{9,17},{17,25},{2,10},{10,18},{18,26},{... | collective-permute-start | bytes 786440 | tf_op jit(solution)/shard_map/ppermute | solution.py:16
  23.4 7.8 %collective-permute-start.1 = (bf16[2,256,256]{2,0,1:T(2,128)(2,1)S(1)}, bf16[2,256,256]{2,0,1:T(2,128)(2,1)}, u32[]{:S(2)}, u32[]{:S(2)}) collective-permute-start(bf16[2,256,256]{2,0,1:T(2,128)(2,1)S(1)} %collective-permute-done), channel_id=1, source_target_pairs={{0,8},{8,16},{16,24},{1,9},{9,17},{17,25},{2,10},{10,18},{18,26},{... | collective-permute-start | bytes 786440 | tf_op jit(solution)/shard_map/ppermute | solution.py:16
  31.2 17.3 %collective-permute-start.2 = (bf16[2,256,256]{2,0,1:T(2,128)(2,1)}, bf16[2,256,256]{2,0,1:T(2,128)(2,1)S(1)}, u32[]{:S(2)}, u32[]{:S(2)}) collective-permute-start(bf16[2,256,256]{2,0,1:T(2,128)(2,1)} %collective-permute-done.1), channel_id=1, source_target_pairs={{0,8},{8,16},{16,24},{1,9},{9,17},{17,25},{2,10},{10,18},{18,26},{... | collective-permute-start | bytes 786440 | tf_op jit(solution)/shard_map/ppermute | solution.py:16
  36.3 0.7 %copy-start.2 = (bf16[1536]{0:T(1024)(128)(2,1)S(1)}, bf16[1536]{0:T(1024)(128)(2,1)}, u32[]{:S(2)}) copy-start(bf16[1536]{0:T(1024)(128)(2,1)} %param.19) | copy-start | bytes 9220
where the time goes:
time: 55.6 us; the launch traced here: 54.9 us
  blocking collectives  19.6 us (35%)
  other arithmetic  11.1 us (20%)
  waiting for transfers between devices  6.59 us (12%)
  starting transfers between devices  5.86 us (11%)
  local copies, waits for them, and re-layouts  4.69 us (8%)
  matrix products  4.23 us (8%)
  between operations  2.69 us (5%)
    all_gather x1, blocking collectives, per_device(): clip_kv = lax.all_gather(local_kv, 'seq', axis=1, tiled=True)  14.6 us
    ppermute x3, waiting for transfers between devices, passed_along(): return lax.ppermute(shard, axis, pairs)  6.59 us
    ppermute x3, starting transfers between devices, passed_along(): return lax.ppermute(shard, axis, pairs)  5.86 us
    psum x1, blocking collectives, per_device(): mean_square = lax.psum(squares, 'mp') / (HEADS * HD)  4.95 us
    reduce_or x4, other arithmetic, block_step(): return lax.cond(jnp.any(usable), update, unchanged, running)  2.65 us
    dot_general x3, matrix products, update(): jnp.einsum('tgrk,kgd->tgrd', weights.astype(jnp.bfloat16), value_rows, pr...  1.8 us
    reduce_sum x3, other arithmetic, update(): weight_sum = weight_sum * shrink + jnp.sum(weights, axis=-1)  1.7 us
    dot_general x3, matrix products, update(): jnp.einsum('tgrd,kgd->tgrk', query_heads, key_rows, preferred_element_typ...  1.6 us
  transfers between devices with their start and end apart: 3, of which 2 were waited for; matrix products, arithmetic and copies ran while one was open for 31% of the time, Pallas kernels for 0%

commit v1 on v0

--- a/solution.py
+++ b/solution.py
@@ -1,13 +1,135 @@
+import functools
 import math
 
 import jax
 import jax.numpy as jnp
 from jax import lax
+from jax.experimental import pallas as pl
+from jax.experimental.pallas import tpu as pltpu
 from jax.sharding import PartitionSpec as P
 
-HEADS = 24
-KVH = 4
 HD = 128
+MASKED = -1e30
+
+
+def exchanged(shard, axis, by):
+    peers = lax.axis_size(axis)
+    return lax.ppermute(shard, axis, [(i, i ^ by) for i in range(peers)])
+
+
+def in_vmem(count):
+    return [pl.BlockSpec(memory_space=pltpu.VMEM)] * count
+
+
+def gate_factor(level, gate_ref, gain_ref):
+    levels = gate_ref.shape[0]
+    one_hot = (lax.broadcasted_iota(jnp.int32, (16, levels), 1) == level).astype(jnp.bfloat16)
+    row = jnp.dot(one_hot, gate_ref[...], preferred_element_type=jnp.float32)[:8]
+    return gain_ref[...].astype(jnp.float32) * (1.0 + row)
+
+
+def attend_kernel(group_size, offsets, tokens_ref, level_ref, q_ref, gate_ref, gain_ref, *refs):
+    kv_refs = refs[: len(offsets)]
+    attended_ref, squares_ref, factor_ref = refs[len(offsets) :]
+    own_clip = lax.axis_index("span")
+    own_seq = lax.axis_index("seq")
+    rows = q_ref.shape[0]
+    piece_keys = kv_refs[0].shape[1]
+    kv_heads = kv_refs[0].shape[2] // HD
+    to_exponent = math.log2(math.e) / math.sqrt(HD)
+    factor_ref[...] = gate_factor(level_ref[own_clip], gate_ref, gain_ref)
+    lane = lax.broadcasted_iota(jnp.int32, (1, piece_keys), 1)
+    biases = []
+    for clip_by, seq_by in offsets:
+        clip = own_clip ^ clip_by
+        live = tokens_ref[clip] - (own_seq ^ seq_by) * piece_keys
+        biases.append(jnp.where(lane < jnp.where(clip <= own_clip, live, 0), 0.0, MASKED))
+    bias = jnp.concatenate(biases, axis=1)
+    squares = jnp.zeros((rows, HD), jnp.float32)
+    for g in range(kv_heads):
+        first = g * group_size
+        heads = [q_ref[:, (first + r) * HD : (first + r + 1) * HD] for r in range(group_size)]
+        query_rows = jnp.concatenate(heads, axis=0)
+        lanes = slice(g * HD, (g + 1) * HD)
+        key_rows = jnp.concatenate([ref[0, :, lanes] for ref in kv_refs], axis=0)
+        value_rows = jnp.concatenate([ref[1, :, lanes] for ref in kv_refs], axis=0)
+        scores = lax.dot_general(
+            query_rows, key_rows, (((1,), (1,)), ((), ())), preferred_element_type=jnp.float32
+        )
+        scores = scores + bias
+        row_max = jnp.max(scores, axis=1, keepdims=True)
+        weights = jnp.exp2((scores - row_max) * to_exponent)
+        weight_sum = jnp.sum(weights, axis=1, keepdims=True)
+        mixed = jnp.dot(
+            weights.astype(jnp.bfloat16), value_rows, preferred_element_type=jnp.float32
+        )
+        mixed = mixed / weight_sum
+        for r in range(group_size):
+            block = mixed[r * rows : (r + 1) * rows]
+            attended_ref[:, (first + r) * HD : (first + r + 1) * HD] = block
+            squares = squares + block * block
+    squares_ref[...] = jnp.sum(squares.T, axis=0, keepdims=True)
+
+
+def finish_kernel(features, tokens_ref, attended_ref, own_ref, other_ref, factor_ref, out_ref):
+    own_clip = lax.axis_index("span")
+    own_seq = lax.axis_index("seq")
+    rows = attended_ref.shape[0]
+    mean_square = (own_ref[...] + other_ref[...]) / features
+    scale = jnp.broadcast_to(lax.rsqrt(mean_square + 1e-06), (HD, rows)).T
+    slot = own_seq * rows + lax.broadcasted_iota(jnp.int32, (rows, HD), 0)
+    live = slot < tokens_ref[own_clip]
+    for h in range(attended_ref.shape[1] // HD):
+        lanes = slice(h * HD, (h + 1) * HD)
+        block = attended_ref[:, lanes] * scale * factor_ref[0:1, lanes]
+        out_ref[0, :, lanes] = jnp.where(live, block, 0.0).astype(out_ref.dtype)
+
+
+def by_exchange(queries, keys_values, clip_tokens, noise_level, level_gate, out_gain):
+    tokens_here, width = queries.shape[1:]
+    kv_heads_here = keys_values.shape[-1] // HD
+    group_size = width // HD // kv_heads_here
+    own = keys_values[:, 0]
+    pieces = {(0, 0): own}
+    for seq_by in range(1, lax.axis_size("seq")):
+        pieces[0, seq_by] = exchanged(own, "seq", seq_by)
+    clip_by = 1
+    steps = []
+    while clip_by < lax.axis_size("span"):
+        steps.append(clip_by)
+        clip_by *= 2
+    for by in reversed(steps):
+        for at in list(pieces):
+            pieces[at[0] ^ by, at[1]] = exchanged(pieces[at], "span", by)
+    offsets = list(pieces)
+    smem = pl.BlockSpec(memory_space=pltpu.SMEM)
+    attended, squares, factor = pl.pallas_call(
+        functools.partial(attend_kernel, group_size, offsets),
+        out_shape=(
+            jax.ShapeDtypeStruct((tokens_here, width), jnp.float32),
+            jax.ShapeDtypeStruct((1, tokens_here), jnp.float32),
+            jax.ShapeDtypeStruct((8, width), jnp.float32),
+        ),
+        in_specs=[smem, smem] + in_vmem(3 + len(offsets)),
+        out_specs=tuple(in_vmem(3)),
+        compiler_params=pltpu.CompilerParams(vmem_limit_bytes=40 * 1024 * 1024),
+        name="attend",
+    )(
+        clip_tokens,
+        noise_level,
+        queries[0],
+        level_gate,
+        out_gain.reshape(1, width),
+        *pieces.values(),
+    )
+    others = [exchanged(squares, "mp", by) for by in range(1, lax.axis_size("mp"))]
+    return pl.pallas_call(
+        functools.partial(finish_kernel, width * lax.axis_size("mp")),
+        out_shape=jax.ShapeDtypeStruct(queries.shape, queries.dtype),
+        in_specs=[smem] + in_vmem(4),
+        out_specs=pl.BlockSpec(memory_space=pltpu.VMEM),
+        name="finish",
+    )(clip_tokens, attended, squares, sum(others), factor)
 
 
 def passed_along(shard, axis, by):
@@ -16,12 +138,13 @@
     return lax.ppermute(shard, axis, pairs)
 
 
-def per_device(queries, keys_values, clip_tokens, noise_level, level_gate, out_gain):
+def by_blocks(queries, keys_values, clip_tokens, noise_level, level_gate, out_gain):
     tokens_here = queries.shape[1]
     slot_count = tokens_here * lax.axis_size("seq")
     clip_count = clip_tokens.shape[0]
     kv_heads_here = keys_values.shape[-1] // HD
-    group_size = HEADS // KVH
+    heads_here = queries.shape[-1] // HD
+    group_size = heads_here // kv_heads_here
     own_clip = lax.axis_index("span")
     own_seq = lax.axis_index("seq")
     query_heads = queries[0].reshape(tokens_here, kv_heads_here, group_size, HD)
@@ -95,7 +218,7 @@
         tokens_here, kv_heads_here * group_size * HD
     )
     squares = jnp.sum(attended * attended, axis=1)
-    mean_square = lax.psum(squares, "mp") / (HEADS * HD)
+    mean_square = lax.psum(squares, "mp") / (heads_here * HD * lax.axis_size("mp"))
     own_level = jnp.sum(jnp.where(clip_ids == own_clip, noise_level, 0))
     one_hot = (jnp.arange(level_gate.shape[0], dtype=jnp.int32) == own_level).astype(jnp.bfloat16)
     gate_row = jnp.dot(one_hot, level_gate, preferred_element_type=jnp.float32)
@@ -110,6 +233,11 @@
     return jnp.where(usable_rows[:, None], normed, 0.0).astype(jnp.bfloat16)[None]
 
 
+def per_device(*arrays):
+    few = all(lax.axis_size(axis) in (2, 4) for axis in ("span", "seq")) and lax.axis_size("mp") == 2
+    return (by_exchange if few else by_blocks)(*arrays)
+
+
 def solution(mesh):
     placed = (
         P("span", "seq", "mp"),

time: 55.6 us -> 32.5 us (0.58)
  the two profiles are of different devices: /device:TPU:14 before, /device:TPU:0 now
where the time goes in v1:
time: 32.5 us; the launch traced here: 32.2 us
  starting transfers between devices  12 us (37%)
  waiting for transfers between devices  10.1 us (31%)
  local copies, waits for them, and re-layouts  5.91 us (18%)
  Pallas kernels  4.12 us (13%)
    ppermute x16, starting transfers between devices, exchanged(): return lax.ppermute(shard, axis, [(i, i ^ by) for i in range(peers)])  12 us
    ppermute x16, waiting for transfers between devices, exchanged(): return lax.ppermute(shard, axis, [(i, i ^ by) for i in range(peers)])  10.1 us
    unnamed x18, local copies, waits for them, and re-layouts  5.22 us
    pallas_call x1, Pallas kernels, by_exchange(): pl.pallas_call(functools.partial(attend_kernel, group_size, offsets), out...  2.29 us
    pallas_call x1, Pallas kernels, by_exchange(): pl.pallas_call(functools.partial(finish_kernel, width * lax.axis_size('mp...  1.82 us
    reshape x1, local copies, waits for them, and re-layouts, by_exchange(): out_gain.reshape(1, width)  0.69 us
  transfers between devices with their start and end apart: 16, of which 6 were waited for; matrix products, arithmetic and copies ran while one was open for 2% of the time, Pallas kernels for 0%

profile of v1, /device:TPU:0, one launch (start us, length us, event | category | flops | bytes accessed | tf_op | source)
XLA Modules:
  0.0 32.2 jit_solution(11204879059637044740)
XLA Ops:
  0.0 2.9 %collective-permute-start.3 = (bf16[2,64,256]{2,1,0:T(8,128)(2,1)}, bf16[2,64,256]{2,1,0:T(8,128)(2,1)S(1)}, u32[]{:S(2)}, u32[]{:S(2)}) collective-permute-start(bf16[2,64,256]{2,1,0:T(8,128)(2,1)} %bitcast.3), channel_id=1, source_target_pairs={{0,16},{8,24},{16,0},{24,8},{1,17},{9,25},{17,1},{25,9},{2,18},{10... | collective-permute-start | bytes 196616 | tf_op jit(solution)/shard_map/ppermute | solution.py:17
  2.9 3.6 %collective-permute-start.2 = (bf16[2,64,256]{2,1,0:T(8,128)(2,1)}, bf16[2,64,256]{2,1,0:T(8,128)(2,1)S(1)}, u32[]{:S(2)}, u32[]{:S(2)}) collective-permute-start(bf16[2,64,256]{2,1,0:T(8,128)(2,1)} %bitcast.4), channel_id=1, source_target_pairs={{0,6},{2,4},{4,2},{6,0},{1,7},{3,5},{5,3},{7,1},{8,14},{10,12},{12... | collective-permute-start | bytes 196616 | tf_op jit(solution)/shard_map/ppermute | solution.py:17
  6.5 0.0 collective-permute-start.7
  6.5 0.0 collective-permute-start.1
  6.5 0.8 %collective-permute-start = (bf16[2,64,256]{2,1,0:T(8,128)(2,1)}, bf16[2,64,256]{2,1,0:T(8,128)(2,1)S(1)}, u32[]{:S(2)}, u32[]{:S(2)}) collective-permute-start(bf16[2,64,256]{2,1,0:T(8,128)(2,1)} %bitcast.7), channel_id=1, source_target_pairs={{0,2},{2,0},{4,6},{6,4},{1,3},{3,1},{5,7},{7,5},{8,10},{10,8},{12,... | collective-permute-start | bytes 196616 | tf_op jit(solution)/shard_map/ppermute | solution.py:17
  7.3 2.0 %collective-permute-done.2.refs_3_ = bf16[2,64,256]{2,1,0:T(8,128)(2,1)S(1)} collective-permute-done((bf16[2,64,256]{2,1,0:T(8,128)(2,1)}, bf16[2,64,256]{2,1,0:T(8,128)(2,1)S(1)}, u32[]{:S(2)}, u32[]{:S(2)}) %collective-permute-start.2) | collective-permute-done | bytes 65568 | tf_op jit(solution)/shard_map/ppermute | solution.py:17
  9.3 0.5 %collective-permute-start.6 = (bf16[2,64,256]{2,1,0:T(8,128)(2,1)S(1)}, bf16[2,64,256]{2,1,0:T(8,128)(2,1)S(1)}, u32[]{:S(2)}, u32[]{:S(2)}) collective-permute-start(bf16[2,64,256]{2,1,0:T(8,128)(2,1)S(1)} %collective-permute-done.2.refs_3_), channel_id=1, source_target_pairs={{0,16},{8,24},{16,0},{24,8},{1,17},{9,25},{17,1},{25,9},{2,18},{10... | collective-permute-start | bytes 196616 | tf_op jit(solution)/shard_map/ppermute | solution.py:17
  9.9 2.8 %collective-permute-done.1.refs_2_ = bf16[2,64,256]{2,1,0:T(8,128)(2,1)S(1)} collective-permute-done((bf16[2,64,256]{2,1,0:T(8,128)(2,1)}, bf16[2,64,256]{2,1,0:T(8,128)(2,1)S(1)}, u32[]{:S(2)}, u32[]{:S(2)}) %collective-permute-start.1) | collective-permute-done | bytes 65568 | tf_op jit(solution)/shard_map/ppermute | solution.py:17
  12.7 0.5 %collective-permute-start.5 = (bf16[2,64,256]{2,1,0:T(8,128)(2,1)S(1)}, bf16[2,64,256]{2,1,0:T(8,128)(2,1)S(1)}, u32[]{:S(2)}, u32[]{:S(2)}) collective-permute-start(bf16[2,64,256]{2,1,0:T(8,128)(2,1)S(1)} %collective-permute-done.1.refs_2_), channel_id=1, source_target_pairs={{0,16},{8,24},{16,0},{24,8},{1,17},{9,25},{17,1},{25,9},{2,18},{10... | collective-permute-start | bytes 196616 | tf_op jit(solution)/shard_map/ppermute | solution.py:17
  13.2 1.5 %collective-permute-start.4 = (bf16[2,64,256]{2,1,0:T(8,128)(2,1)S(1)}, bf16[2,64,256]{2,1,0:T(8,128)(2,1)S(1)}, u32[]{:S(2)}, u32[]{:S(2)}) collective-permute-start(bf16[2,64,256]{2,1,0:T(8,128)(2,1)S(1)} %collective-permute-done.refs_1_), channel_id=1, source_target_pairs={{0,16},{8,24},{16,0},{24,8},{1,17},{9,25},{17,1},{25,9},{2,18},{10... | collective-permute-start | bytes 196616 | tf_op jit(solution)/shard_map/ppermute | solution.py:17
  14.7 0.0 collective-permute-done.10.refs_11_
  14.7 0.5 %collective-permute-start.8 = (bf16[2,64,256]{2,1,0:T(8,128)(2,1)S(1)}, bf16[2,64,256]{2,1,0:T(8,128)(2,1)S(1)}, u32[]{:S(2)}, u32[]{:S(2)}) collective-permute-start(bf16[2,64,256]{2,1,0:T(8,128)(2,1)S(1)} %collective-permute-done.refs_1_), channel_id=1, source_target_pairs={{0,8},{8,0},{16,24},{24,16},{1,9},{9,1},{17,25},{25,17},{2,10},{10... | collective-permute-start | bytes 196616 | tf_op jit(solution)/shard_map/ppermute | solution.py:17
  15.2 0.1 collective-permute-start.14
  15.3 2.1 %collective-permute-done.5.refs_6_ = bf16[2,64,256]{2,1,0:T(8,128)(2,1)S(1)} collective-permute-done((bf16[2,64,256]{2,1,0:T(8,128)(2,1)S(1)}, bf16[2,64,256]{2,1,0:T(8,128)(2,1)S(1)}, u32[]{:S(2)}, u32[]{:S(2)}) %collective-permute-start.5) | collective-permute-done | bytes 65568 | tf_op jit(solution)/shard_map/ppermute | solution.py:17
  17.3 0.7 %collective-permute-done.4.refs_5_ = bf16[2,64,256]{2,1,0:T(8,128)(2,1)S(1)} collective-permute-done((bf16[2,64,256]{2,1,0:T(8,128)(2,1)S(1)}, bf16[2,64,256]{2,1,0:T(8,128)(2,1)S(1)}, u32[]{:S(2)}, u32[]{:S(2)}) %collective-permute-start.4) | collective-permute-done | bytes 65568 | tf_op jit(solution)/shard_map/ppermute | solution.py:17
  18.0 0.7 %reshape.3.gain_ref = bf16[1,1536]{1,0:T(2,128)(2,1)S(1)} reshape(bf16[1536]{0:T(1024)(128)(2,1)} %param.11) | data formatting | bytes 6144 | tf_op jit(solution)/shard_map/reshape | solution.py:122
  18.8 0.0 collective-permute-done.8.refs_9_
  18.8 0.0 collective-permute-done.14.refs_15_
  18.8 0.5 %collective-permute-done.12.refs_13_ = bf16[2,64,256]{2,1,0:T(8,128)(2,1)S(1)} collective-permute-done((bf16[2,64,256]{2,1,0:T(8,128)(2,1)S(1)}, bf16[2,64,256]{2,1,0:T(8,128)(2,1)S(1)}, u32[]{:S(2)}, u32[]{:S(2)}) %collective-permute-start.12) | collective-permute-done | bytes 65568 | tf_op jit(solution)/shard_map/ppermute | solution.py:17
  19.3 0.1 copy-done.5
  19.4 0.0 copy-done.6
  19.4 0.9 %copy-done.1 = bf16[1,64,1536]{2,1,0:T(8,128)(2,1)S(1)} copy-done((bf16[1,64,1536]{2,1,0:T(8,128)(2,1)S(1)}, bf16[1,64,1536]{2,1,0:T(8,128)(2,1)}, u32[]{:S(2)}) %copy-start.1) | copy-done | bytes 196632
  20.3 0.9 %copy-done.2 = bf16[64,1536]{1,0:T(8,128)(2,1)S(1)} copy-done((bf16[64,1536]{1,0:T(8,128)(2,1)S(1)}, bf16[64,1536]{1,0:T(8,128)(2,1)}, u32[]{:S(2)}) %copy-start.2) | copy-done | bytes 196632
  21.3 0.8 %copy-done.3 = bf16[2,1,64,256]{3,2,1,0:T(8,128)(2,1)S(1)} copy-done((bf16[2,1,64,256]{3,2,1,0:T(8,128)(2,1)S(1)}, bf16[2,1,64,256]{3,2,1,0:T(8,128)(2,1)}, u32[]{:S(2)}) %copy-start.3) | copy-done | bytes 65560
  22.1 2.3 %attend.1 = (f32[64,1536]{1,0:T(8,128)S(1)}, f32[1,64]{1,0:T(1,128)S(1)}, f32[8,1536]{1,0:T(8,128)S(1)}) custom-call(s32[4]{0:T(128)S(1)} %copy-done.5, s32[4]{0:T(128)S(1)} %copy-done.6, bf16[64,1536]{1,0:T(8,128)(2,1)S(1)} %bitcast.2, bf16[64,1536]{1,0:T(8,128)(2,1)S(1)} %copy-done.2, bf16[1,1536]{1,0:T(2,128)(2,1)S(1)} %reshape.3.gain_ref, ...), custom_call_target="tpu_custom_call" | custom-call | tf_op jit(solution)/shard_map/attend/pallas_call | solution.py:106
  24.4 0.7 %copy-done = f32[64,1536]{1,0:T(8,128)} copy-done((f32[64,1536]{1,0:T(8,128)}, f32[64,1536]{1,0:T(8,128)S(1)}, u32[]{:S(2)}) %copy-start) | copy-done | bytes 393240
  25.1 0.6 %copy-done.4 = f32[8,1536]{1,0:T(8,128)} copy-done((f32[8,1536]{1,0:T(8,128)}, f32[8,1536]{1,0:T(8,128)S(1)}, u32[]{:S(2)}) %copy-start.4) | copy-done | bytes 49176
  25.8 0.6 %copy-done.7 = f32[1,64]{1,0:T(1,128)} copy-done((f32[1,64]{1,0:T(1,128)}, f32[1,64]{1,0:T(1,128)S(1)}, u32[]{:S(2)}) %copy-start.7) | copy-done | bytes 280
  26.3 1.5 %collective-permute-start.15 = (f32[1,64]{1,0:T(1,128)S(1)}, f32[1,64]{1,0:T(1,128)S(1)}, u32[]{:S(2)}, u32[]{:S(2)}) collective-permute-start(f32[1,64]{1,0:T(1,128)S(1)} %get-tuple-element.9.own_ref), channel_id=1, source_target_pairs={{0,1},{1,0},{2,3},{3,2},{4,5},{5,4},{6,7},{7,6},{8,9},{9,8},{10,11... | collective-permute-start | bytes 776 | tf_op jit(solution)/shard_map/ppermute | solution.py:17
  27.8 2.0 %collective-permute-done.15.other_ref = f32[1,64]{1,0:T(1,128)S(1)} collective-permute-done((f32[1,64]{1,0:T(1,128)S(1)}, f32[1,64]{1,0:T(1,128)S(1)}, u32[]{:S(2)}, u32[]{:S(2)}) %collective-permute-start.15) | collective-permute-done | bytes 288 | tf_op jit(solution)/shard_map/ppermute | solution.py:17
  29.9 0.5 %copy-done.8 = f32[1,64]{1,0:T(1,128)} copy-done((f32[1,64]{1,0:T(1,128)}, f32[1,64]{1,0:T(1,128)S(1)}, u32[]{:S(2)}) %copy-start.8) | copy-done | bytes 280
  30.4 1.8 %finish.1 = bf16[1,64,1536]{2,1,0:T(8,128)(2,1)} custom-call(s32[4]{0:T(128)} %tokens_ref.3, f32[64,1536]{1,0:T(8,128)} %copy-done, f32[1,64]{1,0:T(1,128)} %copy-done.7, f32[1,64]{1,0:T(1,128)} %copy-done.8, f32[8,1536]{1,0:T(8,128)} %copy-done.4), custom_call_target="tpu_custom_call" | custom-call | tf_op jit(solution)/shard_map/finish/pallas_call | solution.py:126
  (21 shorter events, 0.0 us)
Async XLA Ops:
  0.0 7.3 %collective-permute-start.3 = (bf16[2,64,256]{2,1,0:T(8,128)(2,1)}, bf16[2,64,256]{2,1,0:T(8,128)(2,1)S(1)}, u32[]{:S(2)}, u32[]{:S(2)}) collective-permute-start(bf16[2,64,256]{2,1,0:T(8,128)(2,1)} %bitcast.3), channel_id=1, source_target_pairs={{0,16},{8,24},{16,0},{24,8},{1,17},{9,25},{17,1},{25,9},{2,18},{10... | collective-permute-start | bytes 196616 | tf_op jit(solution)/shard_map/ppermute | solution.py:17
  2.9 6.4 %collective-permute-start.2 = (bf16[2,64,256]{2,1,0:T(8,128)(2,1)}, bf16[2,64,256]{2,1,0:T(8,128)(2,1)S(1)}, u32[]{:S(2)}, u32[]{:S(2)}) collective-permute-start(bf16[2,64,256]{2,1,0:T(8,128)(2,1)} %bitcast.4), channel_id=1, source_target_pairs={{0,6},{2,4},{4,2},{6,0},{1,7},{3,5},{5,3},{7,1},{8,14},{10,12},{12... | collective-permute-start | bytes 196616 | tf_op jit(solution)/shard_map/ppermute | solution.py:17
  6.5 2.8 %collective-permute-start.7 = (bf16[2,64,256]{2,1,0:T(8,128)(2,1)}, bf16[2,64,256]{2,1,0:T(8,128)(2,1)S(1)}, u32[]{:S(2)}, u32[]{:S(2)}) collective-permute-start(bf16[2,64,256]{2,1,0:T(8,128)(2,1)} %bitcast.5), channel_id=1, source_target_pairs={{0,8},{8,0},{16,24},{24,16},{1,9},{9,1},{17,25},{25,17},{2,10},{10... | collective-permute-start | bytes 196616 | tf_op jit(solution)/shard_map/ppermute | solution.py:17
  6.5 6.1 %collective-permute-start.1 = (bf16[2,64,256]{2,1,0:T(8,128)(2,1)}, bf16[2,64,256]{2,1,0:T(8,128)(2,1)S(1)}, u32[]{:S(2)}, u32[]{:S(2)}) collective-permute-start(bf16[2,64,256]{2,1,0:T(8,128)(2,1)} %bitcast.6), channel_id=1, source_target_pairs={{0,4},{2,6},{4,0},{6,2},{1,5},{3,7},{5,1},{7,3},{8,12},{10,14},{12... | collective-permute-start | bytes 196616 | tf_op jit(solution)/shard_map/ppermute | solution.py:17
  6.5 6.6 %collective-permute-start = (bf16[2,64,256]{2,1,0:T(8,128)(2,1)}, bf16[2,64,256]{2,1,0:T(8,128)(2,1)S(1)}, u32[]{:S(2)}, u32[]{:S(2)}) collective-permute-start(bf16[2,64,256]{2,1,0:T(8,128)(2,1)} %bitcast.7), channel_id=1, source_target_pairs={{0,2},{2,0},{4,6},{6,4},{1,3},{3,1},{5,7},{7,5},{8,10},{10,8},{12,... | collective-permute-start | bytes 196616 | tf_op jit(solution)/shard_map/ppermute | solution.py:17
  7.3 7.4 %collective-permute-start.11 = (bf16[2,64,256]{2,1,0:T(8,128)(2,1)S(1)}, bf16[2,64,256]{2,1,0:T(8,128)(2,1)S(1)}, u32[]{:S(2)}, u32[]{:S(2)}) collective-permute-start(bf16[2,64,256]{2,1,0:T(8,128)(2,1)S(1)} %collective-permute-done.3.refs_4_), channel_id=1, source_target_pairs={{0,8},{8,0},{16,24},{24,16},{1,9},{9,1},{17,25},{25,17},{2,10},{10... | collective-permute-start | bytes 196616 | tf_op jit(solution)/shard_map/ppermute | solution.py:17
  9.3 5.4 %collective-permute-start.10 = (bf16[2,64,256]{2,1,0:T(8,128)(2,1)S(1)}, bf16[2,64,256]{2,1,0:T(8,128)(2,1)S(1)}, u32[]{:S(2)}, u32[]{:S(2)}) collective-permute-start(bf16[2,64,256]{2,1,0:T(8,128)(2,1)S(1)} %collective-permute-done.2.refs_3_), channel_id=1, source_target_pairs={{0,8},{8,0},{16,24},{24,16},{1,9},{9,1},{17,25},{25,17},{2,10},{10... | collective-permute-start | bytes 196616 | tf_op jit(solution)/shard_map/ppermute | solution.py:17
  9.3 5.9 %collective-permute-start.6 = (bf16[2,64,256]{2,1,0:T(8,128)(2,1)S(1)}, bf16[2,64,256]{2,1,0:T(8,128)(2,1)S(1)}, u32[]{:S(2)}, u32[]{:S(2)}) collective-permute-start(bf16[2,64,256]{2,1,0:T(8,128)(2,1)S(1)} %collective-permute-done.2.refs_3_), channel_id=1, source_target_pairs={{0,16},{8,24},{16,0},{24,8},{1,17},{9,25},{17,1},{25,9},{2,18},{10... | collective-permute-start | bytes 196616 | tf_op jit(solution)/shard_map/ppermute | solution.py:17
  12.7 4.7 %collective-permute-start.5 = (bf16[2,64,256]{2,1,0:T(8,128)(2,1)S(1)}, bf16[2,64,256]{2,1,0:T(8,128)(2,1)S(1)}, u32[]{:S(2)}, u32[]{:S(2)}) collective-permute-start(bf16[2,64,256]{2,1,0:T(8,128)(2,1)S(1)} %collective-permute-done.1.refs_2_), channel_id=1, source_target_pairs={{0,16},{8,24},{16,0},{24,8},{1,17},{9,25},{17,1},{25,9},{2,18},{10... | collective-permute-start | bytes 196616 | tf_op jit(solution)/shard_map/ppermute | solution.py:17
  13.2 4.8 %collective-permute-start.4 = (bf16[2,64,256]{2,1,0:T(8,128)(2,1)S(1)}, bf16[2,64,256]{2,1,0:T(8,128)(2,1)S(1)}, u32[]{:S(2)}, u32[]{:S(2)}) collective-permute-start(bf16[2,64,256]{2,1,0:T(8,128)(2,1)S(1)} %collective-permute-done.refs_1_), channel_id=1, source_target_pairs={{0,16},{8,24},{16,0},{24,8},{1,17},{9,25},{17,1},{25,9},{2,18},{10... | collective-permute-start | bytes 196616 | tf_op jit(solution)/shard_map/ppermute | solution.py:17
  14.7 4.1 %collective-permute-start.9 = (bf16[2,64,256]{2,1,0:T(8,128)(2,1)S(1)}, bf16[2,64,256]{2,1,0:T(8,128)(2,1)S(1)}, u32[]{:S(2)}, u32[]{:S(2)}) collective-permute-start(bf16[2,64,256]{2,1,0:T(8,128)(2,1)S(1)} %collective-permute-done.1.refs_2_), channel_id=1, source_target_pairs={{0,8},{8,0},{16,24},{24,16},{1,9},{9,1},{17,25},{25,17},{2,10},{10... | collective-permute-start | bytes 196616 | tf_op jit(solution)/shard_map/ppermute | solution.py:17
  14.7 4.1 %collective-permute-start.8 = (bf16[2,64,256]{2,1,0:T(8,128)(2,1)S(1)}, bf16[2,64,256]{2,1,0:T(8,128)(2,1)S(1)}, u32[]{:S(2)}, u32[]{:S(2)}) collective-permute-start(bf16[2,64,256]{2,1,0:T(8,128)(2,1)S(1)} %collective-permute-done.refs_1_), channel_id=1, source_target_pairs={{0,8},{8,0},{16,24},{24,16},{1,9},{9,1},{17,25},{25,17},{2,10},{10... | collective-permute-start | bytes 196616 | tf_op jit(solution)/shard_map/ppermute | solution.py:17
  15.2 3.6 %collective-permute-start.14 = (bf16[2,64,256]{2,1,0:T(8,128)(2,1)S(1)}, bf16[2,64,256]{2,1,0:T(8,128)(2,1)S(1)}, u32[]{:S(2)}, u32[]{:S(2)}) collective-permute-start(bf16[2,64,256]{2,1,0:T(8,128)(2,1)S(1)} %collective-permute-done.6.refs_7_), channel_id=1, source_target_pairs={{0,8},{8,0},{16,24},{24,16},{1,9},{9,1},{17,25},{25,17},{2,10},{10... | collective-permute-start | bytes 196616 | tf_op jit(solution)/shard_map/ppermute | solution.py:17
  17.3 1.4 %collective-permute-start.13 = (bf16[2,64,256]{2,1,0:T(8,128)(2,1)S(1)}, bf16[2,64,256]{2,1,0:T(8,128)(2,1)S(1)}, u32[]{:S(2)}, u32[]{:S(2)}) collective-permute-start(bf16[2,64,256]{2,1,0:T(8,128)(2,1)S(1)} %collective-permute-done.5.refs_6_), channel_id=1, source_target_pairs={{0,8},{8,0},{16,24},{24,16},{1,9},{9,1},{17,25},{25,17},{2,10},{10... | collective-permute-start | bytes 196616 | tf_op jit(solution)/shard_map/ppermute | solution.py:17
  18.0 1.3 %collective-permute-start.12 = (bf16[2,64,256]{2,1,0:T(8,128)(2,1)S(1)}, bf16[2,64,256]{2,1,0:T(8,128)(2,1)S(1)}, u32[]{:S(2)}, u32[]{:S(2)}) collective-permute-start(bf16[2,64,256]{2,1,0:T(8,128)(2,1)S(1)} %collective-permute-done.4.refs_5_), channel_id=1, source_target_pairs={{0,8},{8,0},{16,24},{24,16},{1,9},{9,1},{17,25},{25,17},{2,10},{10... | collective-permute-start | bytes 196616 | tf_op jit(solution)/shard_map/ppermute | solution.py:17
  18.7 0.7 %copy-start.5 = (s32[4]{0:T(128)S(1)}, s32[4]{0:T(128)}, u32[]{:S(2)}) copy-start(s32[4]{0:T(128)} %tokens_ref.3) | copy-start | bytes 52
  18.7 0.7 %copy-start.6 = (s32[4]{0:T(128)S(1)}, s32[4]{0:T(128)}, u32[]{:S(2)}) copy-start(s32[4]{0:T(128)} %level_ref.1) | copy-start | bytes 52
  19.4 0.9 %copy-start.1 = (bf16[1,64,1536]{2,1,0:T(8,128)(2,1)S(1)}, bf16[1,64,1536]{2,1,0:T(8,128)(2,1)}, u32[]{:S(2)}) copy-start(bf16[1,64,1536]{2,1,0:T(8,128)(2,1)} %param.6) | copy-start | bytes 589828
  20.3 0.9 %copy-start.2 = (bf16[64,1536]{1,0:T(8,128)(2,1)S(1)}, bf16[64,1536]{1,0:T(8,128)(2,1)}, u32[]{:S(2)}) copy-start(bf16[64,1536]{1,0:T(8,128)(2,1)} %gate_ref.1) | copy-start | bytes 589828
  21.3 0.8 %copy-start.3 = (bf16[2,1,64,256]{3,2,1,0:T(8,128)(2,1)S(1)}, bf16[2,1,64,256]{3,2,1,0:T(8,128)(2,1)}, u32[]{:S(2)}) copy-start(bf16[2,1,64,256]{3,2,1,0:T(8,128)(2,1)} %param.7) | copy-start | bytes 196612
  24.4 0.7 %copy-start = (f32[64,1536]{1,0:T(8,128)}, f32[64,1536]{1,0:T(8,128)S(1)}, u32[]{:S(2)}) copy-start(f32[64,1536]{1,0:T(8,128)S(1)} %get-tuple-element.8.attended_ref) | copy-start | bytes 1179652
  25.1 0.6 %copy-start.4 = (f32[8,1536]{1,0:T(8,128)}, f32[8,1536]{1,0:T(8,128)S(1)}, u32[]{:S(2)}) copy-start(f32[8,1536]{1,0:T(8,128)S(1)} %get-tuple-element.10.factor_ref) | copy-start | bytes 147460
  25.8 0.6 %copy-start.7 = (f32[1,64]{1,0:T(1,128)}, f32[1,64]{1,0:T(1,128)S(1)}, u32[]{:S(2)}) copy-start(f32[1,64]{1,0:T(1,128)S(1)} %get-tuple-element.9.own_ref) | copy-start | bytes 772
  26.3 3.5 %collective-permute-start.15 = (f32[1,64]{1,0:T(1,128)S(1)}, f32[1,64]{1,0:T(1,128)S(1)}, u32[]{:S(2)}, u32[]{:S(2)}) collective-permute-start(f32[1,64]{1,0:T(1,128)S(1)} %get-tuple-element.9.own_ref), channel_id=1, source_target_pairs={{0,1},{1,0},{2,3},{3,2},{4,5},{5,4},{6,7},{7,6},{8,9},{9,8},{10,11... | collective-permute-start | bytes 776 | tf_op jit(solution)/shard_map/ppermute | solution.py:17
  29.9 0.5 %copy-start.8 = (f32[1,64]{1,0:T(1,128)}, f32[1,64]{1,0:T(1,128)S(1)}, u32[]{:S(2)}) copy-start(f32[1,64]{1,0:T(1,128)S(1)} %collective-permute-done.15.other_ref) | copy-start | bytes 772

commit v2 on v0

--- a/solution.py
+++ b/solution.py
@@ -1,13 +1,223 @@
+import functools
 import math
 
 import jax
 import jax.numpy as jnp
 from jax import lax
+from jax.experimental import pallas as pl
+from jax.experimental.pallas import tpu as pltpu
 from jax.sharding import PartitionSpec as P
 
-HEADS = 24
-KVH = 4
 HD = 128
+MASKED = -1e30
+
+
+def exchanged(shard, axis, by):
+    peers = lax.axis_size(axis)
+    return lax.ppermute(shard, axis, [(i, i ^ by) for i in range(peers)])
+
+
+def in_vmem(count):
+    return [pl.BlockSpec(memory_space=pltpu.VMEM)] * count
+
+
+def in_hbm(array):
+    return pltpu.with_memory_space_constraint(array, pltpu.HBM)
+
+
+def gate_factor(level, gate_ref, gain_ref):
+    levels = gate_ref.shape[0]
+    one_hot = (lax.broadcasted_iota(jnp.int32, (16, levels), 1) == level).astype(jnp.bfloat16)
+    row = jnp.dot(one_hot, gate_ref[...], preferred_element_type=jnp.float32)[:8]
+    gain = gain_ref[...].astype(jnp.float32)
+    return jnp.broadcast_to(gain[None, :], row.shape) * (1.0 + row)
+
+
+def prepare_kernel(offsets, count, *refs):
+    sources, outs, (arrived,) = refs[:6], refs[6 : 6 + count], refs[-1:]
+    rows_ref, own_ref, factor_ref, bias_ref, live_ref = outs
+    scratch = refs[6 + count : -1]
+    q_ref, gate_ref, gain_ref, tokens_ref, level_ref = scratch
+    places = (q_ref, gate_ref, gain_ref, tokens_ref, level_ref, own_ref)
+    copies = [
+        pltpu.make_async_copy(src, dst, arrived.at[i])
+        for i, (src, dst) in enumerate(zip(sources, places))
+    ]
+    for copy in copies:
+        copy.start()
+    copies[0].wait()
+    kv_heads, stacked = rows_ref.shape[:2]
+    rows = q_ref.shape[0]
+    group_size = stacked // rows
+    for g in range(kv_heads):
+        for r in range(group_size):
+            h = g * group_size + r
+            rows_ref[g, r * rows : (r + 1) * rows] = q_ref[:, h * HD : (h + 1) * HD]
+    for copy in copies[1:]:
+        copy.wait()
+    own_clip = lax.axis_index("span")
+    own_seq = lax.axis_index("seq")
+    factor_ref[...] = gate_factor(level_ref[own_clip], gate_ref, gain_ref)
+    lane = lax.broadcasted_iota(jnp.int32, (8, rows), 1)
+    biases = []
+    for clip_by, seq_by in offsets:
+        clip = own_clip ^ clip_by
+        live = tokens_ref[clip] - (own_seq ^ seq_by) * rows
+        biases.append(jnp.where(lane < jnp.where(clip <= own_clip, live, 0), 0.0, MASKED))
+    bias_ref[...] = jnp.concatenate(biases, axis=1)
+    slot = own_seq * rows + lax.broadcasted_iota(jnp.int32, live_ref.shape, 0)
+    live_ref[...] = (slot < tokens_ref[own_clip]).astype(jnp.float32)
+
+
+def fold(query_rows, kv_refs, bias, lanes, state):
+    to_exponent = math.log2(math.e) / math.sqrt(HD)
+    key_rows = jnp.concatenate([ref[0, :, lanes] for ref in kv_refs], axis=0)
+    value_rows = jnp.concatenate([ref[1, :, lanes] for ref in kv_refs], axis=0)
+    scores = lax.dot_general(
+        query_rows, key_rows, (((1,), (1,)), ((), ())), preferred_element_type=jnp.float32
+    )
+    scores = scores + bias
+    tiles = [slice(i, i + HD) for i in range(0, scores.shape[1], HD)]
+    highest = functools.reduce(jnp.maximum, [scores[:, tile] for tile in tiles])
+    if state is not None:
+        highest = jnp.maximum(highest, state[0])
+    new_max = jnp.max(highest, axis=1, keepdims=True)
+    weights = jnp.exp2((scores - new_max) * to_exponent)
+    weight_sums = functools.reduce(jnp.add, [weights[:, tile] for tile in tiles])
+    mixed = jnp.dot(weights.astype(jnp.bfloat16), value_rows, preferred_element_type=jnp.float32)
+    if state is not None:
+        shrink = jnp.exp2((state[0] - new_max) * to_exponent)
+        weight_sums = weight_sums + state[1] * shrink
+        mixed = mixed + state[2] * shrink
+    return new_max, weight_sums, mixed
+
+
+def early_kernel(rows_ref, bias_ref, *refs):
+    kv_refs, (max_ref, sums_ref, mixed_ref) = refs[:-3], refs[-3:]
+    keys = kv_refs[0].shape[1] * len(kv_refs)
+    for g in range(rows_ref.shape[0]):
+        lanes = slice(g * HD, (g + 1) * HD)
+        state = fold(rows_ref[g], kv_refs, bias_ref[0:1, :keys], lanes, None)
+        max_ref[g] = jnp.broadcast_to(state[0], max_ref.shape[1:])
+        sums_ref[g] = state[1]
+        mixed_ref[g] = state[2]
+
+
+def late_kernel(group_size, rows_ref, bias_ref, *refs):
+    states, kv_refs, (attended_ref, squares_ref) = refs[:3], refs[3:-2], refs[-2:]
+    rows = rows_ref.shape[1] // group_size
+    first = bias_ref.shape[1] - kv_refs[0].shape[1] * len(kv_refs)
+    squares = jnp.zeros((rows, HD), jnp.float32)
+    for g in range(rows_ref.shape[0]):
+        lanes = slice(g * HD, (g + 1) * HD)
+        state = [ref[g] for ref in states]
+        _, weight_sums, mixed = fold(rows_ref[g], kv_refs, bias_ref[0:1, first:], lanes, state)
+        mixed = mixed / jnp.sum(weight_sums, axis=1, keepdims=True)
+        for r in range(group_size):
+            block = mixed[r * rows : (r + 1) * rows]
+            h = g * group_size + r
+            attended_ref[:, h * HD : (h + 1) * HD] = block
+            squares = squares + block * block
+    squares_ref[...] = jnp.sum(squares.T, axis=0, keepdims=True)
+
+
+def finish_kernel(features, attended_ref, own_ref, other_ref, factor_ref, live_ref, out_ref):
+    rows = attended_ref.shape[0]
+    mean_square = (own_ref[...] + other_ref[...]) / features
+    scale = jnp.broadcast_to(lax.rsqrt(mean_square + 1e-06), (HD, rows)).T
+    live = live_ref[...] > 0.0
+    for h in range(attended_ref.shape[1] // HD):
+        lanes = slice(h * HD, (h + 1) * HD)
+        block = attended_ref[:, lanes] * scale * factor_ref[0:1, lanes]
+        out_ref[0, :, lanes] = jnp.where(live, block, 0.0).astype(out_ref.dtype)
+
+
+def kernel(body, outs, count, megabytes, name):
+    several = isinstance(outs, tuple)
+    return pl.pallas_call(
+        body,
+        out_shape=outs,
+        in_specs=in_vmem(count),
+        out_specs=tuple(in_vmem(len(outs))) if several else in_vmem(1)[0],
+        compiler_params=pltpu.CompilerParams(vmem_limit_bytes=megabytes * 1024 * 1024),
+        name=name,
+    )
+
+
+def after(array, *others):
+    return lax.optimization_barrier((array, *others))[0]
+
+
+def arrival_order():
+    clips, parts = lax.axis_size("span"), lax.axis_size("seq")
+    across = clips // 2
+    late = [(by, at) for at in range(1, max(parts // 2, 1) + 1) for by in range(across, clips)]
+    early = [(by, at) for by in range(clips) for at in range(parts)]
+    return [at for at in early if at not in late], late
+
+
+def travel(own, prepared):
+    pieces = {(0, 0): own}
+    far_first = range(lax.axis_size("seq") - 1, 0, -1)
+    for seq_by in far_first:
+        pieces[0, seq_by] = exchanged(own, "seq", seq_by)
+    across = lax.axis_size("span") // 2
+    for seq_by in (0, *far_first):
+        piece = pieces[0, seq_by]
+        if seq_by == far_first[1 if len(far_first) > 1 else 0]:
+            piece = after(piece, prepared)
+        pieces[across, seq_by] = exchanged(piece, "span", across)
+        if across > 1:
+            pieces[1, seq_by] = exchanged(pieces[0, seq_by], "span", 1)
+    if across > 1:
+        for seq_by in (0, *far_first):
+            pieces[across + 1, seq_by] = exchanged(pieces[across, seq_by], "span", 1)
+    return pieces
+
+
+def by_exchange(queries, keys_values, clip_tokens, noise_level, level_gate, out_gain):
+    tokens_here, width = queries.shape[1:]
+    kv_heads_here = keys_values.shape[-1] // HD
+    group_size = width // HD // kv_heads_here
+    own = keys_values[:, 0]
+    f32 = functools.partial(jax.ShapeDtypeStruct, dtype=jnp.float32)
+    stacked = (kv_heads_here, group_size * tokens_here, HD)
+    early, late = arrival_order()
+    outs = (
+        jax.ShapeDtypeStruct(stacked, queries.dtype),
+        jax.ShapeDtypeStruct(own.shape, own.dtype),
+        f32((8, width)),
+        f32((8, tokens_here * len(early + late))),
+        f32((tokens_here, HD)),
+    )
+    sources = (queries[0], level_gate, out_gain, clip_tokens, noise_level, own)
+    spaces = (pltpu.VMEM, pltpu.VMEM, pltpu.VMEM, pltpu.SMEM, pltpu.SMEM)
+    rows, own_kept, factor, bias, live = pl.pallas_call(
+        functools.partial(prepare_kernel, early + late, len(outs)),
+        out_shape=outs,
+        in_specs=[pl.BlockSpec(memory_space=pltpu.HBM)] * len(sources),
+        out_specs=tuple(in_vmem(len(outs))),
+        scratch_shapes=[space(x.shape, x.dtype) for space, x in zip(spaces, sources)]
+        + [pltpu.SemaphoreType.DMA((len(sources),))],
+        compiler_params=pltpu.CompilerParams(vmem_limit_bytes=8 * 1024 * 1024),
+        name="prepare",
+    )(*(in_hbm(x) for x in sources))
+    pieces = travel(own, rows)
+    pieces[0, 0] = own_kept
+    state = kernel(early_kernel, (f32(stacked),) * 3, 2 + len(early), 16, "attend_early")(
+        rows, bias, *[pieces[at] for at in early]
+    )
+    attended, squares = kernel(
+        functools.partial(late_kernel, group_size),
+        (f32((tokens_here, width)), f32((1, tokens_here))),
+        5 + len(late), 16, "attend_late",
+    )(rows, bias, *state, *[pieces[at] for at in late])
+    others = [exchanged(squares, "mp", by) for by in range(1, lax.axis_size("mp"))]
+    return kernel(
+        functools.partial(finish_kernel, width * lax.axis_size("mp")),
+        jax.ShapeDtypeStruct(queries.shape, queries.dtype),
+        5, 4, "finish",
+    )(attended, squares, sum(others), factor, live)
 
 
 def passed_along(shard, axis, by):
@@ -16,12 +226,13 @@
     return lax.ppermute(shard, axis, pairs)
 
 
-def per_device(queries, keys_values, clip_tokens, noise_level, level_gate, out_gain):
+def by_blocks(queries, keys_values, clip_tokens, noise_level, level_gate, out_gain):
     tokens_here = queries.shape[1]
     slot_count = tokens_here * lax.axis_size("seq")
     clip_count = clip_tokens.shape[0]
     kv_heads_here = keys_values.shape[-1] // HD
-    group_size = HEADS // KVH
+    heads_here = queries.shape[-1] // HD
+    group_size = heads_here // kv_heads_here
     own_clip = lax.axis_index("span")
     own_seq = lax.axis_index("seq")
     query_heads = queries[0].reshape(tokens_here, kv_heads_here, group_size, HD)
@@ -95,7 +306,7 @@
         tokens_here, kv_heads_here * group_size * HD
     )
     squares = jnp.sum(attended * attended, axis=1)
-    mean_square = lax.psum(squares, "mp") / (HEADS * HD)
+    mean_square = lax.psum(squares, "mp") / (heads_here * HD * lax.axis_size("mp"))
     own_level = jnp.sum(jnp.where(clip_ids == own_clip, noise_level, 0))
     one_hot = (jnp.arange(level_gate.shape[0], dtype=jnp.int32) == own_level).astype(jnp.bfloat16)
     gate_row = jnp.dot(one_hot, level_gate, preferred_element_type=jnp.float32)
@@ -110,6 +321,11 @@
     return jnp.where(usable_rows[:, None], normed, 0.0).astype(jnp.bfloat16)[None]
 
 
+def per_device(*arrays):
+    few = all(lax.axis_size(axis) in (2, 4) for axis in ("span", "seq")) and lax.axis_size("mp") == 2
+    return (by_exchange if few else by_blocks)(*arrays)
+
+
 def solution(mesh):
     placed = (
         P("span", "seq", "mp"),

time: 55.6 us -> 23.3 us (0.42)
  the two profiles are of different devices: /device:TPU:14 before, /device:TPU:0 now
where the time goes in v2:
time: 23.3 us; the launch traced here: 23.2 us
  starting transfers between devices  12.6 us (54%)
  waiting for transfers between devices  6.57 us (28%)
  Pallas kernels  3.93 us (17%)
    ppermute x16, starting transfers between devices, exchanged(): return lax.ppermute(shard, axis, [(i, i ^ by) for i in range(peers)])  12.6 us
    ppermute x16, waiting for transfers between devices, exchanged(): return lax.ppermute(shard, axis, [(i, i ^ by) for i in range(peers)])  6.57 us
    pallas_call x1, Pallas kernels, by_exchange(): pl.pallas_call(functools.partial(prepare_kernel, early + late, len(outs))...  1.25 us
    pallas_call x1, Pallas kernels, by_exchange(): kernel(early_kernel, (f32(stacked),) * 3, 2 + len(early), 16, 'attend_ear...  1.21 us
    pallas_call x1, Pallas kernels, by_exchange(): kernel(functools.partial(finish_kernel, width * lax.axis_size('mp')), jax...  0.81 us
    pallas_call x1, Pallas kernels, by_exchange(): kernel(functools.partial(late_kernel, group_size), (f32((tokens_here, wid...  0.66 us
  transfers between devices with their start and end apart: 16, of which 6 were waited for; matrix products, arithmetic and copies ran while one was open for 0% of the time, Pallas kernels for 11%

profile of v2, /device:TPU:0, one launch (start us, length us, event | category | flops | bytes accessed | tf_op | source)
XLA Modules:
  0.0 23.2 jit_solution(7350138651965895476)
XLA Ops:
  0.0 5.0 %collective-permute-start.2 = (bf16[2,64,256]{2,1,0:T(8,128)(2,1)}, bf16[2,64,256]{2,1,0:T(8,128)(2,1)S(1)}, u32[]{:S(2)}, u32[]{:S(2)}) collective-permute-start(bf16[2,64,256]{2,1,0:T(8,128)(2,1)} %bitcast.3), channel_id=1, source_target_pairs={{0,6},{2,4},{4,2},{6,0},{1,7},{3,5},{5,3},{7,1},{8,14},{10,12},{12... | collective-permute-start | bytes 196616 | tf_op jit(solution)/shard_map/ppermute | solution.py:17
  5.0 0.0 collective-permute-start
  5.1 0.6 %collective-permute-start.1 = (bf16[2,64,256]{2,1,0:T(8,128)(2,1)}, bf16[2,64,256]{2,1,0:T(8,128)(2,1)S(1)}, u32[]{:S(2)}, u32[]{:S(2)}) collective-permute-start(bf16[2,64,256]{2,1,0:T(8,128)(2,1)} %bitcast.5), channel_id=1, source_target_pairs={{0,4},{2,6},{4,0},{6,2},{1,5},{3,7},{5,1},{7,3},{8,12},{10,14},{12... | collective-permute-start | bytes 196616 | tf_op jit(solution)/shard_map/ppermute | solution.py:17
  5.6 1.7 %collective-permute-start.7 = (bf16[2,64,256]{2,1,0:T(8,128)(2,1)}, bf16[2,64,256]{2,1,0:T(8,128)(2,1)S(1)}, u32[]{:S(2)}, u32[]{:S(2)}) collective-permute-start(bf16[2,64,256]{2,1,0:T(8,128)(2,1)} %bitcast.6), channel_id=1, source_target_pairs={{0,16},{8,24},{16,0},{24,8},{1,17},{9,25},{17,1},{25,9},{2,18},{10... | collective-permute-start | bytes 196616 | tf_op jit(solution)/shard_map/ppermute | solution.py:17
  7.3 0.0 collective-permute-start.3
  7.3 1.2 %prepare.1 = (bf16[2,384,128]{2,1,0:T(8,128)(2,1)S(1)}, bf16[2,64,256]{2,1,0:T(8,128)(2,1)S(1)}, f32[8,1536]{1,0:T(8,128)S(1)}, f32[8,1024]{1,0:T(8,128)S(1)}, f32[64,128]{1,0:T(8,128)S(1)}) custom-call(bf16[64,1536]{1,0:T(8,128)(2,1)} %bitcast.2, bf16[64,1536]{1,0:T(8,128)(2,1)} %refs_1_.1, bf16[1536]{0:T(1024)(128)(2,1)} %refs_2_.1, s32[4]{0:T(128)} %refs_3_.1, ...), custom_call_target="tpu_custom_call" | custom-call | tf_op jit(solution)/shard_map/prepare/pallas_call | solution.py:195
  8.6 1.1 %collective-permute-start.8 = (bf16[2,64,256]{2,1,0:T(8,128)(2,1)S(1)}, bf16[2,64,256]{2,1,0:T(8,128)(2,1)S(1)}, u32[]{:S(2)}, u32[]{:S(2)}) collective-permute-start(bf16[2,64,256]{2,1,0:T(8,128)(2,1)S(1)} %collective-permute-done.2.refs_3_), channel_id=1, source_target_pairs={{0,16},{8,24},{16,0},{24,8},{1,17},{9,25},{17,1},{25,9},{2,18},{10... | collective-permute-start | bytes 196616 | tf_op jit(solution)/shard_map/ppermute | solution.py:17
  9.7 0.3 %collective-permute-done.refs_1_ = bf16[2,64,256]{2,1,0:T(8,128)(2,1)S(1)} collective-permute-done((bf16[2,64,256]{2,1,0:T(8,128)(2,1)}, bf16[2,64,256]{2,1,0:T(8,128)(2,1)S(1)}, u32[]{:S(2)}, u32[]{:S(2)}) %collective-permute-start) | collective-permute-done | bytes 65568 | tf_op jit(solution)/shard_map/ppermute | solution.py:17
  9.9 0.0 collective-permute-start.4
  9.9 1.0 %collective-permute-done.1.refs_2_ = bf16[2,64,256]{2,1,0:T(8,128)(2,1)S(1)} collective-permute-done((bf16[2,64,256]{2,1,0:T(8,128)(2,1)}, bf16[2,64,256]{2,1,0:T(8,128)(2,1)S(1)}, u32[]{:S(2)}, u32[]{:S(2)}) %collective-permute-start.1) | collective-permute-done | bytes 65568 | tf_op jit(solution)/shard_map/ppermute | solution.py:17
  10.9 0.0 collective-permute-start.5
  10.9 0.0 collective-permute-done.7.refs_8_
  10.9 1.5 %collective-permute-start.13 = (bf16[2,64,256]{2,1,0:T(8,128)(2,1)S(1)}, bf16[2,64,256]{2,1,0:T(8,128)(2,1)S(1)}, u32[]{:S(2)}, u32[]{:S(2)}) collective-permute-start(bf16[2,64,256]{2,1,0:T(8,128)(2,1)S(1)} %collective-permute-done.1.refs_2_), channel_id=1, source_target_pairs={{0,16},{8,24},{16,0},{24,8},{1,17},{9,25},{17,1},{25,9},{2,18},{10... | collective-permute-start | bytes 196616 | tf_op jit(solution)/shard_map/ppermute | solution.py:17
  12.4 0.5 %collective-permute-start.11 = (bf16[2,64,256]{2,1,0:T(8,128)(2,1)S(1)}, bf16[2,64,256]{2,1,0:T(8,128)(2,1)S(1)}, u32[]{:S(2)}, u32[]{:S(2)}) collective-permute-start(bf16[2,64,256]{2,1,0:T(8,128)(2,1)S(1)} %collective-permute-done.refs_1_), channel_id=1, source_target_pairs={{0,16},{8,24},{16,0},{24,8},{1,17},{9,25},{17,1},{25,9},{2,18},{10... | collective-permute-start | bytes 196616 | tf_op jit(solution)/shard_map/ppermute | solution.py:17
  12.9 0.2 %collective-permute-done.8.refs_9_ = bf16[2,64,256]{2,1,0:T(8,128)(2,1)S(1)} collective-permute-done((bf16[2,64,256]{2,1,0:T(8,128)(2,1)S(1)}, bf16[2,64,256]{2,1,0:T(8,128)(2,1)S(1)}, u32[]{:S(2)}, u32[]{:S(2)}) %collective-permute-start.8) | collective-permute-done | bytes 65568 | tf_op jit(solution)/shard_map/ppermute | solution.py:17
  13.2 0.0 collective-permute-start.6
  13.2 0.0 collective-permute-done.4.refs_5_
  13.2 0.5 %collective-permute-start.9 = (bf16[2,64,256]{2,1,0:T(8,128)(2,1)S(1)}, bf16[2,64,256]{2,1,0:T(8,128)(2,1)S(1)}, u32[]{:S(2)}, u32[]{:S(2)}) collective-permute-start(bf16[2,64,256]{2,1,0:T(8,128)(2,1)S(1)} %collective-permute-done.7.refs_8_), channel_id=1, source_target_pairs={{0,8},{8,0},{16,24},{24,16},{1,9},{9,1},{17,25},{25,17},{2,10},{10... | collective-permute-start | bytes 196616 | tf_op jit(solution)/shard_map/ppermute | solution.py:17
  13.7 0.0 collective-permute-done.5.refs_6_
  13.7 0.1 collective-permute-start.10
  13.8 1.9 %collective-permute-done.13.refs_5_ = bf16[2,64,256]{2,1,0:T(8,128)(2,1)S(1)} collective-permute-done((bf16[2,64,256]{2,1,0:T(8,128)(2,1)S(1)}, bf16[2,64,256]{2,1,0:T(8,128)(2,1)S(1)}, u32[]{:S(2)}, u32[]{:S(2)}) %collective-permute-start.13) | collective-permute-done | bytes 65568 | tf_op jit(solution)/shard_map/ppermute | solution.py:17
  15.6 1.2 %collective-permute-done.11.refs_3_ = bf16[2,64,256]{2,1,0:T(8,128)(2,1)S(1)} collective-permute-done((bf16[2,64,256]{2,1,0:T(8,128)(2,1)S(1)}, bf16[2,64,256]{2,1,0:T(8,128)(2,1)S(1)}, u32[]{:S(2)}, u32[]{:S(2)}) %collective-permute-start.11) | collective-permute-done | bytes 65568 | tf_op jit(solution)/shard_map/ppermute | solution.py:17
  16.8 0.0 collective-permute-start.12
  16.8 0.0 collective-permute-done.6.refs_7_
  16.8 0.0 collective-permute-done.9.refs_10_
  16.8 1.2 %attend_early.1 = (f32[2,384,128]{2,1,0:T(8,128)S(1)}, f32[2,384,128]{2,1,0:T(8,128)S(1)}, f32[2,384,128]{2,1,0:T(8,128)S(1)}) custom-call(bf16[2,384,128]{2,1,0:T(8,128)(2,1)S(1)} %get-tuple-element.16.rows_ref, f32[8,1024]{1,0:T(8,128)S(1)} %get-tuple-element.17.bias_ref, bf16[2,64,256]{2,1,0:T(8,128)(2,1)S(1)} %get-tuple-element.18.refs_0_, ...), custom_call_target="tpu_custom_call" | custom-call | tf_op jit(solution)/shard_map/attend_early/pallas_call | solution.py:207
  18.1 0.0 collective-permute-done.14.refs_6_
  18.1 0.0 collective-permute-done.12.refs_4_
  18.1 0.7 %attend_late.1 = (f32[64,1536]{1,0:T(8,128)S(1)}, f32[1,64]{1,0:T(1,128)S(1)}) custom-call(bf16[2,384,128]{2,1,0:T(8,128)(2,1)S(1)} %get-tuple-element.16.rows_ref, f32[8,1024]{1,0:T(8,128)S(1)} %get-tuple-element.17.bias_ref, f32[2,384,128]{2,1,0:T(8,128)S(1)} %get-tuple-element.19.refs_0_, f32[2,384,128]{2,1,0:T(8,128)S(1)} %get-tuple-element.20.refs_1_, ...), custom_call_target="tpu_custom_call" | custom-call | tf_op jit(solution)/shard_map/attend_late/pallas_call | solution.py:210
  18.7 1.6 %collective-permute-start.15 = (f32[1,64]{1,0:T(1,128)S(1)}, f32[1,64]{1,0:T(1,128)S(1)}, u32[]{:S(2)}, u32[]{:S(2)}) collective-permute-start(f32[1,64]{1,0:T(1,128)S(1)} %get-tuple-element.24.own_ref), channel_id=1, source_target_pairs={{0,1},{1,0},{2,3},{3,2},{4,5},{5,4},{6,7},{7,6},{8,9},{9,8},{10,11... | collective-permute-start | bytes 776 | tf_op jit(solution)/shard_map/ppermute | solution.py:17
  20.3 2.0 %collective-permute-done.15.other_ref = f32[1,64]{1,0:T(1,128)S(1)} collective-permute-done((f32[1,64]{1,0:T(1,128)S(1)}, f32[1,64]{1,0:T(1,128)S(1)}, u32[]{:S(2)}, u32[]{:S(2)}) %collective-permute-start.15) | collective-permute-done | bytes 288 | tf_op jit(solution)/shard_map/ppermute | solution.py:17
  22.3 0.8 %finish.1 = bf16[1,64,1536]{2,1,0:T(8,128)(2,1)} custom-call(f32[64,1536]{1,0:T(8,128)S(1)} %get-tuple-element.23.attended_ref, f32[1,64]{1,0:T(1,128)S(1)} %get-tuple-element.24.own_ref, f32[1,64]{1,0:T(1,128)S(1)} %collective-permute-done.15.other_ref, f32[8,1536]{1,0:T(8,128)S(1)} %get-tuple-element.25.factor_ref, f32[64,128]{1,0:T(8,128)S(1)} %get-tuple-element.26.live_ref), custom_call_target="tpu_custom_call" | custom-call | tf_op jit(solution)/shard_map/finish/pallas_call | solution.py:216
  (4 shorter events, 0.0 us)
Async XLA Ops:
  0.0 8.6 %collective-permute-start.2 = (bf16[2,64,256]{2,1,0:T(8,128)(2,1)}, bf16[2,64,256]{2,1,0:T(8,128)(2,1)S(1)}, u32[]{:S(2)}, u32[]{:S(2)}) collective-permute-start(bf16[2,64,256]{2,1,0:T(8,128)(2,1)} %bitcast.3), channel_id=1, source_target_pairs={{0,6},{2,4},{4,2},{6,0},{1,7},{3,5},{5,3},{7,1},{8,14},{10,12},{12... | collective-permute-start | bytes 196616 | tf_op jit(solution)/shard_map/ppermute | solution.py:17
  5.0 4.9 %collective-permute-start = (bf16[2,64,256]{2,1,0:T(8,128)(2,1)}, bf16[2,64,256]{2,1,0:T(8,128)(2,1)S(1)}, u32[]{:S(2)}, u32[]{:S(2)}) collective-permute-start(bf16[2,64,256]{2,1,0:T(8,128)(2,1)} %bitcast.4), channel_id=1, source_target_pairs={{0,2},{2,0},{4,6},{6,4},{1,3},{3,1},{5,7},{7,5},{8,10},{10,8},{12,... | collective-permute-start | bytes 196616 | tf_op jit(solution)/shard_map/ppermute | solution.py:17
  5.1 5.8 %collective-permute-start.1 = (bf16[2,64,256]{2,1,0:T(8,128)(2,1)}, bf16[2,64,256]{2,1,0:T(8,128)(2,1)S(1)}, u32[]{:S(2)}, u32[]{:S(2)}) collective-permute-start(bf16[2,64,256]{2,1,0:T(8,128)(2,1)} %bitcast.5), channel_id=1, source_target_pairs={{0,4},{2,6},{4,0},{6,2},{1,5},{3,7},{5,1},{7,3},{8,12},{10,14},{12... | collective-permute-start | bytes 196616 | tf_op jit(solution)/shard_map/ppermute | solution.py:17
  5.6 5.3 %collective-permute-start.7 = (bf16[2,64,256]{2,1,0:T(8,128)(2,1)}, bf16[2,64,256]{2,1,0:T(8,128)(2,1)S(1)}, u32[]{:S(2)}, u32[]{:S(2)}) collective-permute-start(bf16[2,64,256]{2,1,0:T(8,128)(2,1)} %bitcast.6), channel_id=1, source_target_pairs={{0,16},{8,24},{16,0},{24,8},{1,17},{9,25},{17,1},{25,9},{2,18},{10... | collective-permute-start | bytes 196616 | tf_op jit(solution)/shard_map/ppermute | solution.py:17
  7.3 5.1 %collective-permute-start.3 = (bf16[2,64,256]{2,1,0:T(8,128)(2,1)}, bf16[2,64,256]{2,1,0:T(8,128)(2,1)S(1)}, u32[]{:S(2)}, u32[]{:S(2)}) collective-permute-start(bf16[2,64,256]{2,1,0:T(8,128)(2,1)} %bitcast.7), channel_id=1, source_target_pairs={{0,8},{8,0},{16,24},{24,16},{1,9},{9,1},{17,25},{25,17},{2,10},{10... | collective-permute-start | bytes 196616 | tf_op jit(solution)/shard_map/ppermute | solution.py:17
  8.6 4.6 %collective-permute-start.8 = (bf16[2,64,256]{2,1,0:T(8,128)(2,1)S(1)}, bf16[2,64,256]{2,1,0:T(8,128)(2,1)S(1)}, u32[]{:S(2)}, u32[]{:S(2)}) collective-permute-start(bf16[2,64,256]{2,1,0:T(8,128)(2,1)S(1)} %collective-permute-done.2.refs_3_), channel_id=1, source_target_pairs={{0,16},{8,24},{16,0},{24,8},{1,17},{9,25},{17,1},{25,9},{2,18},{10... | collective-permute-start | bytes 196616 | tf_op jit(solution)/shard_map/ppermute | solution.py:17
  9.9 3.3 %collective-permute-start.4 = (bf16[2,64,256]{2,1,0:T(8,128)(2,1)S(1)}, bf16[2,64,256]{2,1,0:T(8,128)(2,1)S(1)}, u32[]{:S(2)}, u32[]{:S(2)}) collective-permute-start(bf16[2,64,256]{2,1,0:T(8,128)(2,1)S(1)} %collective-permute-done.refs_1_), channel_id=1, source_target_pairs={{0,8},{8,0},{16,24},{24,16},{1,9},{9,1},{17,25},{25,17},{2,10},{10... | collective-permute-start | bytes 196616 | tf_op jit(solution)/shard_map/ppermute | solution.py:17
  10.9 2.8 %collective-permute-start.5 = (bf16[2,64,256]{2,1,0:T(8,128)(2,1)S(1)}, bf16[2,64,256]{2,1,0:T(8,128)(2,1)S(1)}, u32[]{:S(2)}, u32[]{:S(2)}) collective-permute-start(bf16[2,64,256]{2,1,0:T(8,128)(2,1)S(1)} %collective-permute-done.1.refs_2_), channel_id=1, source_target_pairs={{0,8},{8,0},{16,24},{24,16},{1,9},{9,1},{17,25},{25,17},{2,10},{10... | collective-permute-start | bytes 196616 | tf_op jit(solution)/shard_map/ppermute | solution.py:17
  10.9 4.7 %collective-permute-start.13 = (bf16[2,64,256]{2,1,0:T(8,128)(2,1)S(1)}, bf16[2,64,256]{2,1,0:T(8,128)(2,1)S(1)}, u32[]{:S(2)}, u32[]{:S(2)}) collective-permute-start(bf16[2,64,256]{2,1,0:T(8,128)(2,1)S(1)} %collective-permute-done.1.refs_2_), channel_id=1, source_target_pairs={{0,16},{8,24},{16,0},{24,8},{1,17},{9,25},{17,1},{25,9},{2,18},{10... | collective-permute-start | bytes 196616 | tf_op jit(solution)/shard_map/ppermute | solution.py:17
  12.4 4.4 %collective-permute-start.11 = (bf16[2,64,256]{2,1,0:T(8,128)(2,1)S(1)}, bf16[2,64,256]{2,1,0:T(8,128)(2,1)S(1)}, u32[]{:S(2)}, u32[]{:S(2)}) collective-permute-start(bf16[2,64,256]{2,1,0:T(8,128)(2,1)S(1)} %collective-permute-done.refs_1_), channel_id=1, source_target_pairs={{0,16},{8,24},{16,0},{24,8},{1,17},{9,25},{17,1},{25,9},{2,18},{10... | collective-permute-start | bytes 196616 | tf_op jit(solution)/shard_map/ppermute | solution.py:17
  13.2 3.6 %collective-permute-start.6 = (bf16[2,64,256]{2,1,0:T(8,128)(2,1)S(1)}, bf16[2,64,256]{2,1,0:T(8,128)(2,1)S(1)}, u32[]{:S(2)}, u32[]{:S(2)}) collective-permute-start(bf16[2,64,256]{2,1,0:T(8,128)(2,1)S(1)} %collective-permute-done.2.refs_3_), channel_id=1, source_target_pairs={{0,8},{8,0},{16,24},{24,16},{1,9},{9,1},{17,25},{25,17},{2,10},{10... | collective-permute-start | bytes 196616 | tf_op jit(solution)/shard_map/ppermute | solution.py:17
  13.2 3.6 %collective-permute-start.9 = (bf16[2,64,256]{2,1,0:T(8,128)(2,1)S(1)}, bf16[2,64,256]{2,1,0:T(8,128)(2,1)S(1)}, u32[]{:S(2)}, u32[]{:S(2)}) collective-permute-start(bf16[2,64,256]{2,1,0:T(8,128)(2,1)S(1)} %collective-permute-done.7.refs_8_), channel_id=1, source_target_pairs={{0,8},{8,0},{16,24},{24,16},{1,9},{9,1},{17,25},{25,17},{2,10},{10... | collective-permute-start | bytes 196616 | tf_op jit(solution)/shard_map/ppermute | solution.py:17
  13.7 3.1 %collective-permute-start.10 = (bf16[2,64,256]{2,1,0:T(8,128)(2,1)S(1)}, bf16[2,64,256]{2,1,0:T(8,128)(2,1)S(1)}, u32[]{:S(2)}, u32[]{:S(2)}) collective-permute-start(bf16[2,64,256]{2,1,0:T(8,128)(2,1)S(1)} %collective-permute-done.8.refs_9_), channel_id=1, source_target_pairs={{0,8},{8,0},{16,24},{24,16},{1,9},{9,1},{17,25},{25,17},{2,10},{10... | collective-permute-start | bytes 196616 | tf_op jit(solution)/shard_map/ppermute | solution.py:17
  15.6 2.4 %collective-permute-start.14 = (bf16[2,64,256]{2,1,0:T(8,128)(2,1)S(1)}, bf16[2,64,256]{2,1,0:T(8,128)(2,1)S(1)}, u32[]{:S(2)}, u32[]{:S(2)}) collective-permute-start(bf16[2,64,256]{2,1,0:T(8,128)(2,1)S(1)} %collective-permute-done.13.refs_5_), channel_id=1, source_target_pairs={{0,8},{8,0},{16,24},{24,16},{1,9},{9,1},{17,25},{25,17},{2,10},{10... | collective-permute-start | bytes 196616 | tf_op jit(solution)/shard_map/ppermute | solution.py:17
  16.8 1.3 %collective-permute-start.12 = (bf16[2,64,256]{2,1,0:T(8,128)(2,1)S(1)}, bf16[2,64,256]{2,1,0:T(8,128)(2,1)S(1)}, u32[]{:S(2)}, u32[]{:S(2)}) collective-permute-start(bf16[2,64,256]{2,1,0:T(8,128)(2,1)S(1)} %collective-permute-done.11.refs_3_), channel_id=1, source_target_pairs={{0,8},{8,0},{16,24},{24,16},{1,9},{9,1},{17,25},{25,17},{2,10},{10... | collective-permute-start | bytes 196616 | tf_op jit(solution)/shard_map/ppermute | solution.py:17
  18.7 3.6 %collective-permute-start.15 = (f32[1,64]{1,0:T(1,128)S(1)}, f32[1,64]{1,0:T(1,128)S(1)}, u32[]{:S(2)}, u32[]{:S(2)}) collective-permute-start(f32[1,64]{1,0:T(1,128)S(1)} %get-tuple-element.24.own_ref), channel_id=1, source_target_pairs={{0,1},{1,0},{2,3},{3,2},{4,5},{5,4},{6,7},{7,6},{8,9},{9,8},{10,11... | collective-permute-start | bytes 776 | tf_op jit(solution)/shard_map/ppermute | solution.py:17

commit v3 on v2

--- a/solution.py
+++ b/solution.py
@@ -1,4 +1,5 @@
 import functools
+import itertools
 import math
 
 import jax
@@ -10,11 +11,25 @@
 
 HD = 128
 MASKED = -1e30
-
-
-def exchanged(shard, axis, by):
-    peers = lax.axis_size(axis)
-    return lax.ppermute(shard, axis, [(i, i ^ by) for i in range(peers)])
+PREPARED = "prepared"
+
+
+def plan_of():
+    steps = [("p3", (0, 3), "own", None), ("p2", (0, 2), "own", None), ("p1", (0, 1), "own", None)]
+    for part in "0321":
+        source = "own" if part == "0" else "p" + part
+        steps.append(("x" + part, (2, 0), source, PREPARED if part == "2" else None))
+        steps.append(("c" + part, (1, 0), source, None))
+    steps += [("d" + part, (1, 0), "x" + part, None) for part in "0321"]
+    early = ["kept", "p1", "p2", "p3", "c0", "c1", "c2", "c3", "x0", "x3", "d0", "d3"]
+    return steps, early, ["x1", "d1", "x2", "d2"]
+
+
+def exchanged(shard, axes, by):
+    sizes = [lax.axis_size(axis) for axis in axes]
+    places = list(itertools.product(*(range(size) for size in sizes)))
+    to = [tuple(i ^ k for i, k in zip(place, by)) for place in places]
+    return lax.ppermute(shard, axes, [(i, places.index(there)) for i, there in enumerate(to)])
 
 
 def in_vmem(count):
@@ -71,8 +86,9 @@
 
 def fold(query_rows, kv_refs, bias, lanes, state):
     to_exponent = math.log2(math.e) / math.sqrt(HD)
-    key_rows = jnp.concatenate([ref[0, :, lanes] for ref in kv_refs], axis=0)
-    value_rows = jnp.concatenate([ref[1, :, lanes] for ref in kv_refs], axis=0)
+    pieces = [(ref, i) for ref in kv_refs for i in range(ref.shape[0])]
+    key_rows = jnp.concatenate([ref[i, 0, :, lanes] for ref, i in pieces], axis=0)
+    value_rows = jnp.concatenate([ref[i, 1, :, lanes] for ref, i in pieces], axis=0)
     scores = lax.dot_general(
         query_rows, key_rows, (((1,), (1,)), ((), ())), preferred_element_type=jnp.float32
     )
@@ -92,33 +108,52 @@
     return new_max, weight_sums, mixed
 
 
-def early_kernel(rows_ref, bias_ref, *refs):
+def keys_in(kv_refs):
+    return sum(ref.shape[0] * ref.shape[2] for ref in kv_refs)
+
+
+def upper_clips():
+    return lax.axis_index("span") >= lax.axis_size("span") // 2
+
+
+def early_kernel(lower_count, rows_ref, bias_ref, *refs):
     kv_refs, (max_ref, sums_ref, mixed_ref) = refs[:-3], refs[-3:]
-    keys = kv_refs[0].shape[1] * len(kv_refs)
-    for g in range(rows_ref.shape[0]):
-        lanes = slice(g * HD, (g + 1) * HD)
-        state = fold(rows_ref[g], kv_refs, bias_ref[0:1, :keys], lanes, None)
-        max_ref[g] = jnp.broadcast_to(state[0], max_ref.shape[1:])
-        sums_ref[g] = state[1]
-        mixed_ref[g] = state[2]
+
+    def fold_in(kv_refs):
+        keys = keys_in(kv_refs)
+        for g in range(rows_ref.shape[0]):
+            lanes = slice(g * HD, (g + 1) * HD)
+            state = fold(rows_ref[g], kv_refs, bias_ref[0:1, :keys], lanes, None)
+            max_ref[g] = jnp.broadcast_to(state[0], max_ref.shape[1:])
+            sums_ref[g] = state[1]
+            mixed_ref[g] = state[2]
+
+    pl.when(upper_clips())(lambda: fold_in(kv_refs))
+    pl.when(jnp.logical_not(upper_clips()))(lambda: fold_in(kv_refs[:lower_count]))
 
 
 def late_kernel(group_size, rows_ref, bias_ref, *refs):
     states, kv_refs, (attended_ref, squares_ref) = refs[:3], refs[3:-2], refs[-2:]
     rows = rows_ref.shape[1] // group_size
-    first = bias_ref.shape[1] - kv_refs[0].shape[1] * len(kv_refs)
-    squares = jnp.zeros((rows, HD), jnp.float32)
-    for g in range(rows_ref.shape[0]):
-        lanes = slice(g * HD, (g + 1) * HD)
-        state = [ref[g] for ref in states]
-        _, weight_sums, mixed = fold(rows_ref[g], kv_refs, bias_ref[0:1, first:], lanes, state)
-        mixed = mixed / jnp.sum(weight_sums, axis=1, keepdims=True)
-        for r in range(group_size):
-            block = mixed[r * rows : (r + 1) * rows]
-            h = g * group_size + r
-            attended_ref[:, h * HD : (h + 1) * HD] = block
-            squares = squares + block * block
-    squares_ref[...] = jnp.sum(squares.T, axis=0, keepdims=True)
+    first = bias_ref.shape[1] - keys_in(kv_refs)
+
+    def end(folds):
+        squares = jnp.zeros((rows, HD), jnp.float32)
+        for g in range(rows_ref.shape[0]):
+            lanes = slice(g * HD, (g + 1) * HD)
+            state = [ref[g] for ref in states]
+            if folds:
+                state = fold(rows_ref[g], kv_refs, bias_ref[0:1, first:], lanes, state)
+            mixed = state[2] / jnp.sum(state[1], axis=1, keepdims=True)
+            for r in range(group_size):
+                block = mixed[r * rows : (r + 1) * rows]
+                h = g * group_size + r
+                attended_ref[:, h * HD : (h + 1) * HD] = block
+                squares = squares + block * block
+        squares_ref[...] = jnp.sum(squares.T, axis=0, keepdims=True)
+
+    pl.when(upper_clips())(lambda: end(True))
+    pl.when(jnp.logical_not(upper_clips()))(lambda: end(False))
 
 
 def finish_kernel(features, attended_ref, own_ref, other_ref, factor_ref, live_ref, out_ref):
@@ -148,52 +183,65 @@
     return lax.optimization_barrier((array, *others))[0]
 
 
-def arrival_order():
-    clips, parts = lax.axis_size("span"), lax.axis_size("seq")
-    across = clips // 2
-    late = [(by, at) for at in range(1, max(parts // 2, 1) + 1) for by in range(across, clips)]
-    early = [(by, at) for by in range(clips) for at in range(parts)]
-    return [at for at in early if at not in late], late
-
-
-def travel(own, prepared):
-    pieces = {(0, 0): own}
-    far_first = range(lax.axis_size("seq") - 1, 0, -1)
-    for seq_by in far_first:
-        pieces[0, seq_by] = exchanged(own, "seq", seq_by)
-    across = lax.axis_size("span") // 2
-    for seq_by in (0, *far_first):
-        piece = pieces[0, seq_by]
-        if seq_by == far_first[1 if len(far_first) > 1 else 0]:
-            piece = after(piece, prepared)
-        pieces[across, seq_by] = exchanged(piece, "span", across)
-        if across > 1:
-            pieces[1, seq_by] = exchanged(pieces[0, seq_by], "span", 1)
-    if across > 1:
-        for seq_by in (0, *far_first):
-            pieces[across + 1, seq_by] = exchanged(pieces[across, seq_by], "span", 1)
-    return pieces
+def offsets_of(steps):
+    at = {"own": [(0, 0)], "kept": [(0, 0)]}
+    for name, hop, source, _ in steps:
+        if hop is None:
+            at[name] = [offset for part in source for offset in at[part]]
+        else:
+            at[name] = [(clip ^ hop[0], part ^ hop[1]) for clip, part in at[source]]
+    return at
+
+
+def pack_kernel(*refs):
+    at = 0
+    for ref in refs[:-1]:
+        refs[-1][at : at + ref.shape[0]] = ref[...]
+        at += ref.shape[0]
+
+
+def pack(arrays):
+    shape = (sum(array.shape[0] for array in arrays), *arrays[0].shape[1:])
+    out = jax.ShapeDtypeStruct(shape, arrays[0].dtype)
+    return kernel(pack_kernel, out, len(arrays), 4, "pack")(*arrays)
+
+
+def travel(steps, own, kept, prepared):
+    have = {"own": own, "kept": kept, PREPARED: prepared}
+    for name, hop, source, wait_for in steps:
+        if hop is None:
+            have[name] = pack([have[part] for part in source])
+        else:
+            shard = have[source]
+            if wait_for is not None:
+                shard = after(shard, *[have[n] for n in wait_for.split()])
+            have[name] = exchanged(shard, ("span", "seq"), hop)
+    return have
 
 
 def by_exchange(queries, keys_values, clip_tokens, noise_level, level_gate, out_gain):
     tokens_here, width = queries.shape[1:]
     kv_heads_here = keys_values.shape[-1] // HD
     group_size = width // HD // kv_heads_here
-    own = keys_values[:, 0]
+    own = keys_values[None, :, 0]
     f32 = functools.partial(jax.ShapeDtypeStruct, dtype=jnp.float32)
     stacked = (kv_heads_here, group_size * tokens_here, HD)
-    early, late = arrival_order()
+    steps, early, late = plan_of()
+    offsets = offsets_of(steps)
+    across = lax.axis_size("span") // 2
+    lower_count = sum(all(by < across for by, _ in offsets[name]) for name in early)
+    offsets = [at for name in early + late for at in offsets[name]]
     outs = (
         jax.ShapeDtypeStruct(stacked, queries.dtype),
         jax.ShapeDtypeStruct(own.shape, own.dtype),
         f32((8, width)),
-        f32((8, tokens_here * len(early + late))),
+        f32((8, tokens_here * len(offsets))),
         f32((tokens_here, HD)),
     )
     sources = (queries[0], level_gate, out_gain, clip_tokens, noise_level, own)
     spaces = (pltpu.VMEM, pltpu.VMEM, pltpu.VMEM, pltpu.SMEM, pltpu.SMEM)
     rows, own_kept, factor, bias, live = pl.pallas_call(
-        functools.partial(prepare_kernel, early + late, len(outs)),
+        functools.partial(prepare_kernel, offsets, len(outs)),
         out_shape=outs,
         in_specs=[pl.BlockSpec(memory_space=pltpu.HBM)] * len(sources),
         out_specs=tuple(in_vmem(len(outs))),
@@ -202,17 +250,18 @@
         compiler_params=pltpu.CompilerParams(vmem_limit_bytes=8 * 1024 * 1024),
         name="prepare",
     )(*(in_hbm(x) for x in sources))
-    pieces = travel(own, rows)
-    pieces[0, 0] = own_kept
-    state = kernel(early_kernel, (f32(stacked),) * 3, 2 + len(early), 16, "attend_early")(
-        rows, bias, *[pieces[at] for at in early]
+    have = travel(steps, own, own_kept, rows)
+    state = kernel(
+        functools.partial(early_kernel, lower_count), (f32(stacked),) * 3, 2 + len(early), 16, "attend_early"
+    )(
+        rows, bias, *[have[name] for name in early]
     )
     attended, squares = kernel(
         functools.partial(late_kernel, group_size),
         (f32((tokens_here, width)), f32((1, tokens_here))),
         5 + len(late), 16, "attend_late",
-    )(rows, bias, *state, *[pieces[at] for at in late])
-    others = [exchanged(squares, "mp", by) for by in range(1, lax.axis_size("mp"))]
+    )(rows, bias, *state, *[have[name] for name in late])
+    others = [exchanged(squares, ("mp",), (by,)) for by in range(1, lax.axis_size("mp"))]
     return kernel(
         functools.partial(finish_kernel, width * lax.axis_size("mp")),
         jax.ShapeDtypeStruct(queries.shape, queries.dtype),
@@ -322,7 +371,8 @@
 
 
 def per_device(*arrays):
-    few = all(lax.axis_size(axis) in (2, 4) for axis in ("span", "seq")) and lax.axis_size("mp") == 2
+    sizes = tuple(lax.axis_size(axis) for axis in ("span", "seq", "mp"))
+    few = sizes == (4, 4, 2)
     return (by_exchange if few else by_blocks)(*arrays)
 
 

time: 23.3 us -> 22.9 us (0.983)
  Pallas kernels: 3.93 us -> 3.23 us
  waiting for transfers between devices: 6.57 us -> 6.88 us
    pallas_call x1, Pallas kernels: 0.66 us -> 0.27 us  [by_exchange(): kernel(functools.partial(late_kernel, group_size), (f32((tokens_here, wid...]
    pallas_call x2, Pallas kernels: 2.46 us -> 2.15 us  [the longest x1 1.25 us: by_exchange(): pl.pallas_call(functools.partial(prepare_kernel, offsets, len(outs)), out...]
    ppermute x16, waiting for transfers between devices: 6.57 us -> 6.88 us  [exchanged(): lax.ppermute(shard, axes, [(i, places.index(there)) for i, there in enume...]
  transfers between devices with their start and end apart: 16 -> 16, of which waited for: 6 -> 7; matrix products, arithmetic and copies ran while one was open for 0% -> 0% of each run, Pallas kernels for 11% -> 9%
where the time goes in v3:
time: 22.9 us; the launch traced here: 22.8 us
  starting transfers between devices  12.6 us (55%)
  waiting for transfers between devices  6.88 us (30%)
  Pallas kernels  3.23 us (14%)
    ppermute x16, starting transfers between devices, exchanged(): lax.ppermute(shard, axes, [(i, places.index(there)) for i, there in enume...  12.6 us
    ppermute x16, waiting for transfers between devices, exchanged(): lax.ppermute(shard, axes, [(i, places.index(there)) for i, there in enume...  6.88 us
    pallas_call x1, Pallas kernels, by_exchange(): pl.pallas_call(functools.partial(prepare_kernel, offsets, len(outs)), out...  1.25 us
    pallas_call x1, Pallas kernels, by_exchange(): kernel(functools.partial(early_kernel, lower_count), (f32(stacked),) * 3,...  0.9 us
    pallas_call x1, Pallas kernels, by_exchange(): kernel(functools.partial(finish_kernel, width * lax.axis_size('mp')), jax...  0.81 us
  transfers between devices with their start and end apart: 16, of which 7 were waited for; matrix products, arithmetic and copies ran while one was open for 0% of the time, Pallas kernels for 9%

profile of v3, /device:TPU:0, one launch (start us, length us, event | category | flops | bytes accessed | tf_op | source)
XLA Modules:
  0.0 22.8 jit_solution(7245305341134814219)
XLA Ops:
  0.0 5.0 %collective-permute-start.2 = (bf16[1,2,64,256]{3,2,1,0:T(8,128)(2,1)}, bf16[1,2,64,256]{3,2,1,0:T(8,128)(2,1)S(1)}, u32[]{:S(2)}, u32[]{:S(2)}) collective-permute-start(bf16[1,2,64,256]{3,2,1,0:T(8,128)(2,1)} %bitcast.3), channel_id=1, source_target_pairs={{0,6},{2,4},{4,2},{6,0},{8,14},{10,12},{12,10},{14,8},{16,22},{18,... | collective-permute-start | bytes 196616 | tf_op jit(solution)/shard_map/ppermute | solution.py:32
  5.0 0.0 collective-permute-start
  5.1 0.6 %collective-permute-start.1 = (bf16[1,2,64,256]{3,2,1,0:T(8,128)(2,1)}, bf16[1,2,64,256]{3,2,1,0:T(8,128)(2,1)S(1)}, u32[]{:S(2)}, u32[]{:S(2)}) collective-permute-start(bf16[1,2,64,256]{3,2,1,0:T(8,128)(2,1)} %bitcast.5), channel_id=1, source_target_pairs={{0,4},{2,6},{4,0},{6,2},{8,12},{10,14},{12,8},{14,10},{16,20},{18,... | collective-permute-start | bytes 196616 | tf_op jit(solution)/shard_map/ppermute | solution.py:32
  5.6 1.7 %collective-permute-start.7 = (bf16[1,2,64,256]{3,2,1,0:T(8,128)(2,1)}, bf16[1,2,64,256]{3,2,1,0:T(8,128)(2,1)S(1)}, u32[]{:S(2)}, u32[]{:S(2)}) collective-permute-start(bf16[1,2,64,256]{3,2,1,0:T(8,128)(2,1)} %bitcast.6), channel_id=1, source_target_pairs={{0,16},{2,18},{4,20},{6,22},{8,24},{10,26},{12,28},{14,30},{16,0},... | collective-permute-start | bytes 196616 | tf_op jit(solution)/shard_map/ppermute | solution.py:32
  7.3 0.0 collective-permute-start.3
  7.3 1.2 %prepare.1 = (bf16[2,384,128]{2,1,0:T(8,128)(2,1)S(1)}, bf16[1,2,64,256]{3,2,1,0:T(8,128)(2,1)S(1)}, f32[8,1536]{1,0:T(8,128)S(1)}, f32[8,1024]{1,0:T(8,128)S(1)}, f32[64,128]{1,0:T(8,128)S(1)}) custom-call(bf16[64,1536]{1,0:T(8,128)(2,1)} %bitcast.2, bf16[64,1536]{1,0:T(8,128)(2,1)} %refs_1_.1, bf16[1536]{0:T(1024)(128)(2,1)} %refs_2_.1, s32[4]{0:T(128)} %refs_3_.1, ...), custom_call_target="tpu_custom_call" | custom-call | tf_op jit(solution)/shard_map/prepare/pallas_call | solution.py:243
  8.6 0.0 collective-permute-done.2.refs_3_
  8.6 1.1 %collective-permute-start.8 = (bf16[1,2,64,256]{3,2,1,0:T(8,128)(2,1)S(1)}, bf16[1,2,64,256]{3,2,1,0:T(8,128)(2,1)S(1)}, u32[]{:S(2)}, u32[]{:S(2)}) collective-permute-start(bf16[1,2,64,256]{3,2,1,0:T(8,128)(2,1)S(1)} %collective-permute-done.2.refs_3_), channel_id=1, source_target_pairs={{0,16},{2,18},{4,20},{6,22},{8,24},{10,26},{12,28},{14,30},{16,0},... | collective-permute-start | bytes 196616 | tf_op jit(solution)/shard_map/ppermute | solution.py:32
  9.7 0.3 %collective-permute-done.refs_1_ = bf16[1,2,64,256]{3,2,1,0:T(8,128)(2,1)S(1)} collective-permute-done((bf16[1,2,64,256]{3,2,1,0:T(8,128)(2,1)}, bf16[1,2,64,256]{3,2,1,0:T(8,128)(2,1)S(1)}, u32[]{:S(2)}, u32[]{:S(2)}) %collective-permute-start) | collective-permute-done | bytes 65568 | tf_op jit(solution)/shard_map/ppermute | solution.py:32
  9.9 0.0 collective-permute-start.4
  9.9 1.0 %collective-permute-done.1.refs_2_ = bf16[1,2,64,256]{3,2,1,0:T(8,128)(2,1)S(1)} collective-permute-done((bf16[1,2,64,256]{3,2,1,0:T(8,128)(2,1)}, bf16[1,2,64,256]{3,2,1,0:T(8,128)(2,1)S(1)}, u32[]{:S(2)}, u32[]{:S(2)}) %collective-permute-start.1) | collective-permute-done | bytes 65568 | tf_op jit(solution)/shard_map/ppermute | solution.py:32
  10.9 0.0 collective-permute-start.5
  10.9 0.0 collective-permute-done.7.refs_8_
  10.9 1.5 %collective-permute-start.13 = (bf16[1,2,64,256]{3,2,1,0:T(8,128)(2,1)S(1)}, bf16[1,2,64,256]{3,2,1,0:T(8,128)(2,1)S(1)}, u32[]{:S(2)}, u32[]{:S(2)}) collective-permute-start(bf16[1,2,64,256]{3,2,1,0:T(8,128)(2,1)S(1)} %collective-permute-done.1.refs_2_), channel_id=1, source_target_pairs={{0,16},{2,18},{4,20},{6,22},{8,24},{10,26},{12,28},{14,30},{16,0},... | collective-permute-start | bytes 196616 | tf_op jit(solution)/shard_map/ppermute | solution.py:32
  12.4 0.0 collective-permute-done.3.refs_4_
  12.4 0.5 %collective-permute-start.11 = (bf16[1,2,64,256]{3,2,1,0:T(8,128)(2,1)S(1)}, bf16[1,2,64,256]{3,2,1,0:T(8,128)(2,1)S(1)}, u32[]{:S(2)}, u32[]{:S(2)}) collective-permute-start(bf16[1,2,64,256]{3,2,1,0:T(8,128)(2,1)S(1)} %collective-permute-done.refs_1_), channel_id=1, source_target_pairs={{0,16},{2,18},{4,20},{6,22},{8,24},{10,26},{12,28},{14,30},{16,0},... | collective-permute-start | bytes 196616 | tf_op jit(solution)/shard_map/ppermute | solution.py:32
  12.9 0.2 %collective-permute-done.8.refs_9_ = bf16[1,2,64,256]{3,2,1,0:T(8,128)(2,1)S(1)} collective-permute-done((bf16[1,2,64,256]{3,2,1,0:T(8,128)(2,1)S(1)}, bf16[1,2,64,256]{3,2,1,0:T(8,128)(2,1)S(1)}, u32[]{:S(2)}, u32[]{:S(2)}) %collective-permute-start.8) | collective-permute-done | bytes 65568 | tf_op jit(solution)/shard_map/ppermute | solution.py:32
  13.2 0.0 collective-permute-start.6
  13.2 0.5 %collective-permute-start.9 = (bf16[1,2,64,256]{3,2,1,0:T(8,128)(2,1)S(1)}, bf16[1,2,64,256]{3,2,1,0:T(8,128)(2,1)S(1)}, u32[]{:S(2)}, u32[]{:S(2)}) collective-permute-start(bf16[1,2,64,256]{3,2,1,0:T(8,128)(2,1)S(1)} %collective-permute-done.7.refs_8_), channel_id=1, source_target_pairs={{0,8},{2,10},{4,12},{6,14},{8,0},{10,2},{12,4},{14,6},{16,24},{18,... | collective-permute-start | bytes 196616 | tf_op jit(solution)/shard_map/ppermute | solution.py:32
  13.7 0.1 collective-permute-start.10
  13.8 1.9 %collective-permute-done.13.refs_5_ = bf16[1,2,64,256]{3,2,1,0:T(8,128)(2,1)S(1)} collective-permute-done((bf16[1,2,64,256]{3,2,1,0:T(8,128)(2,1)S(1)}, bf16[1,2,64,256]{3,2,1,0:T(8,128)(2,1)S(1)}, u32[]{:S(2)}, u32[]{:S(2)}) %collective-permute-start.13) | collective-permute-done | bytes 65568 | tf_op jit(solution)/shard_map/ppermute | solution.py:32
  15.6 0.0 collective-permute-start.14
  15.6 1.2 %collective-permute-done.11.refs_3_ = bf16[1,2,64,256]{3,2,1,0:T(8,128)(2,1)S(1)} collective-permute-done((bf16[1,2,64,256]{3,2,1,0:T(8,128)(2,1)S(1)}, bf16[1,2,64,256]{3,2,1,0:T(8,128)(2,1)S(1)}, u32[]{:S(2)}, u32[]{:S(2)}) %collective-permute-start.11) | collective-permute-done | bytes 65568 | tf_op jit(solution)/shard_map/ppermute | solution.py:32
  16.8 0.0 collective-permute-done.9.refs_10_
  16.8 0.0 collective-permute-done.10.refs_11_
  16.8 0.9 %attend_early.1 = (f32[2,384,128]{2,1,0:T(8,128)S(1)}, f32[2,384,128]{2,1,0:T(8,128)S(1)}, f32[2,384,128]{2,1,0:T(8,128)S(1)}) custom-call(bf16[2,384,128]{2,1,0:T(8,128)(2,1)S(1)} %get-tuple-element.16.rows_ref, f32[8,1024]{1,0:T(8,128)S(1)} %get-tuple-element.17.bias_ref, bf16[1,2,64,256]{3,2,1,0:T(8,128)(2,1)S(1)} %get-tuple-element.18.refs_0_, ...), custom_call_target="tpu_custom_call" | custom-call | tf_op jit(solution)/shard_map/attend_early/pallas_call | solution.py:254
  17.7 0.0 collective-permute-done.14.refs_6_
  17.8 0.3 %collective-permute-done.12.refs_4_ = bf16[1,2,64,256]{3,2,1,0:T(8,128)(2,1)S(1)} collective-permute-done((bf16[1,2,64,256]{3,2,1,0:T(8,128)(2,1)S(1)}, bf16[1,2,64,256]{3,2,1,0:T(8,128)(2,1)S(1)}, u32[]{:S(2)}, u32[]{:S(2)}) %collective-permute-start.12) | collective-permute-done | bytes 65568 | tf_op jit(solution)/shard_map/ppermute | solution.py:32
  18.1 0.3 %attend_late.1 = (f32[64,1536]{1,0:T(8,128)S(1)}, f32[1,64]{1,0:T(1,128)S(1)}) custom-call(bf16[2,384,128]{2,1,0:T(8,128)(2,1)S(1)} %get-tuple-element.16.rows_ref, f32[8,1024]{1,0:T(8,128)S(1)} %get-tuple-element.17.bias_ref, f32[2,384,128]{2,1,0:T(8,128)S(1)} %get-tuple-element.19.refs_0_, f32[2,384,128]{2,1,0:T(8,128)S(1)} %get-tuple-element.20.refs_1_, ...), custom_call_target="tpu_custom_call" | custom-call | tf_op jit(solution)/shard_map/attend_late/pallas_call | solution.py:259
  18.3 1.6 %collective-permute-start.15 = (f32[1,64]{1,0:T(1,128)S(1)}, f32[1,64]{1,0:T(1,128)S(1)}, u32[]{:S(2)}, u32[]{:S(2)}) collective-permute-start(f32[1,64]{1,0:T(1,128)S(1)} %get-tuple-element.24.own_ref), channel_id=1, source_target_pairs={{0,1},{1,0},{2,3},{3,2},{4,5},{5,4},{6,7},{7,6},{8,9},{9,8},{10,11... | collective-permute-start | bytes 776 | tf_op jit(solution)/shard_map/ppermute | solution.py:32
  19.9 2.0 %collective-permute-done.15.other_ref = f32[1,64]{1,0:T(1,128)S(1)} collective-permute-done((f32[1,64]{1,0:T(1,128)S(1)}, f32[1,64]{1,0:T(1,128)S(1)}, u32[]{:S(2)}, u32[]{:S(2)}) %collective-permute-start.15) | collective-permute-done | bytes 288 | tf_op jit(solution)/shard_map/ppermute | solution.py:32
  22.0 0.8 %finish.1 = bf16[1,64,1536]{2,1,0:T(8,128)(2,1)} custom-call(f32[64,1536]{1,0:T(8,128)S(1)} %get-tuple-element.23.attended_ref, f32[1,64]{1,0:T(1,128)S(1)} %get-tuple-element.24.own_ref, f32[1,64]{1,0:T(1,128)S(1)} %collective-permute-done.15.other_ref, f32[8,1536]{1,0:T(8,128)S(1)} %get-tuple-element.25.factor_ref, f32[64,128]{1,0:T(8,128)S(1)} %get-tuple-element.26.live_ref), custom_call_target="tpu_custom_call" | custom-call | tf_op jit(solution)/shard_map/finish/pallas_call | solution.py:265
  (4 shorter events, 0.0 us)
Async XLA Ops:
  0.0 8.6 %collective-permute-start.2 = (bf16[1,2,64,256]{3,2,1,0:T(8,128)(2,1)}, bf16[1,2,64,256]{3,2,1,0:T(8,128)(2,1)S(1)}, u32[]{:S(2)}, u32[]{:S(2)}) collective-permute-start(bf16[1,2,64,256]{3,2,1,0:T(8,128)(2,1)} %bitcast.3), channel_id=1, source_target_pairs={{0,6},{2,4},{4,2},{6,0},{8,14},{10,12},{12,10},{14,8},{16,22},{18,... | collective-permute-start | bytes 196616 | tf_op jit(solution)/shard_map/ppermute | solution.py:32
  5.0 4.9 %collective-permute-start = (bf16[1,2,64,256]{3,2,1,0:T(8,128)(2,1)}, bf16[1,2,64,256]{3,2,1,0:T(8,128)(2,1)S(1)}, u32[]{:S(2)}, u32[]{:S(2)}) collective-permute-start(bf16[1,2,64,256]{3,2,1,0:T(8,128)(2,1)} %bitcast.4), channel_id=1, source_target_pairs={{0,2},{2,0},{4,6},{6,4},{8,10},{10,8},{12,14},{14,12},{16,18},{18,... | collective-permute-start | bytes 196616 | tf_op jit(solution)/shard_map/ppermute | solution.py:32
  5.1 5.8 %collective-permute-start.1 = (bf16[1,2,64,256]{3,2,1,0:T(8,128)(2,1)}, bf16[1,2,64,256]{3,2,1,0:T(8,128)(2,1)S(1)}, u32[]{:S(2)}, u32[]{:S(2)}) collective-permute-start(bf16[1,2,64,256]{3,2,1,0:T(8,128)(2,1)} %bitcast.5), channel_id=1, source_target_pairs={{0,4},{2,6},{4,0},{6,2},{8,12},{10,14},{12,8},{14,10},{16,20},{18,... | collective-permute-start | bytes 196616 | tf_op jit(solution)/shard_map/ppermute | solution.py:32
  5.6 5.3 %collective-permute-start.7 = (bf16[1,2,64,256]{3,2,1,0:T(8,128)(2,1)}, bf16[1,2,64,256]{3,2,1,0:T(8,128)(2,1)S(1)}, u32[]{:S(2)}, u32[]{:S(2)}) collective-permute-start(bf16[1,2,64,256]{3,2,1,0:T(8,128)(2,1)} %bitcast.6), channel_id=1, source_target_pairs={{0,16},{2,18},{4,20},{6,22},{8,24},{10,26},{12,28},{14,30},{16,0},... | collective-permute-start | bytes 196616 | tf_op jit(solution)/shard_map/ppermute | solution.py:32
  7.3 5.1 %collective-permute-start.3 = (bf16[1,2,64,256]{3,2,1,0:T(8,128)(2,1)}, bf16[1,2,64,256]{3,2,1,0:T(8,128)(2,1)S(1)}, u32[]{:S(2)}, u32[]{:S(2)}) collective-permute-start(bf16[1,2,64,256]{3,2,1,0:T(8,128)(2,1)} %bitcast.7), channel_id=1, source_target_pairs={{0,8},{2,10},{4,12},{6,14},{8,0},{10,2},{12,4},{14,6},{16,24},{18,... | collective-permute-start | bytes 196616 | tf_op jit(solution)/shard_map/ppermute | solution.py:32
  8.6 4.6 %collective-permute-start.8 = (bf16[1,2,64,256]{3,2,1,0:T(8,128)(2,1)S(1)}, bf16[1,2,64,256]{3,2,1,0:T(8,128)(2,1)S(1)}, u32[]{:S(2)}, u32[]{:S(2)}) collective-permute-start(bf16[1,2,64,256]{3,2,1,0:T(8,128)(2,1)S(1)} %collective-permute-done.2.refs_3_), channel_id=1, source_target_pairs={{0,16},{2,18},{4,20},{6,22},{8,24},{10,26},{12,28},{14,30},{16,0},... | collective-permute-start | bytes 196616 | tf_op jit(solution)/shard_map/ppermute | solution.py:32
  9.9 3.3 %collective-permute-start.4 = (bf16[1,2,64,256]{3,2,1,0:T(8,128)(2,1)S(1)}, bf16[1,2,64,256]{3,2,1,0:T(8,128)(2,1)S(1)}, u32[]{:S(2)}, u32[]{:S(2)}) collective-permute-start(bf16[1,2,64,256]{3,2,1,0:T(8,128)(2,1)S(1)} %collective-permute-done.refs_1_), channel_id=1, source_target_pairs={{0,8},{2,10},{4,12},{6,14},{8,0},{10,2},{12,4},{14,6},{16,24},{18,... | collective-permute-start | bytes 196616 | tf_op jit(solution)/shard_map/ppermute | solution.py:32
  10.9 2.8 %collective-permute-start.5 = (bf16[1,2,64,256]{3,2,1,0:T(8,128)(2,1)S(1)}, bf16[1,2,64,256]{3,2,1,0:T(8,128)(2,1)S(1)}, u32[]{:S(2)}, u32[]{:S(2)}) collective-permute-start(bf16[1,2,64,256]{3,2,1,0:T(8,128)(2,1)S(1)} %collective-permute-done.1.refs_2_), channel_id=1, source_target_pairs={{0,8},{2,10},{4,12},{6,14},{8,0},{10,2},{12,4},{14,6},{16,24},{18,... | collective-permute-start | bytes 196616 | tf_op jit(solution)/shard_map/ppermute | solution.py:32
  10.9 4.7 %collective-permute-start.13 = (bf16[1,2,64,256]{3,2,1,0:T(8,128)(2,1)S(1)}, bf16[1,2,64,256]{3,2,1,0:T(8,128)(2,1)S(1)}, u32[]{:S(2)}, u32[]{:S(2)}) collective-permute-start(bf16[1,2,64,256]{3,2,1,0:T(8,128)(2,1)S(1)} %collective-permute-done.1.refs_2_), channel_id=1, source_target_pairs={{0,16},{2,18},{4,20},{6,22},{8,24},{10,26},{12,28},{14,30},{16,0},... | collective-permute-start | bytes 196616 | tf_op jit(solution)/shard_map/ppermute | solution.py:32
  12.4 4.4 %collective-permute-start.11 = (bf16[1,2,64,256]{3,2,1,0:T(8,128)(2,1)S(1)}, bf16[1,2,64,256]{3,2,1,0:T(8,128)(2,1)S(1)}, u32[]{:S(2)}, u32[]{:S(2)}) collective-permute-start(bf16[1,2,64,256]{3,2,1,0:T(8,128)(2,1)S(1)} %collective-permute-done.refs_1_), channel_id=1, source_target_pairs={{0,16},{2,18},{4,20},{6,22},{8,24},{10,26},{12,28},{14,30},{16,0},... | collective-permute-start | bytes 196616 | tf_op jit(solution)/shard_map/ppermute | solution.py:32
  13.2 3.6 %collective-permute-start.6 = (bf16[1,2,64,256]{3,2,1,0:T(8,128)(2,1)S(1)}, bf16[1,2,64,256]{3,2,1,0:T(8,128)(2,1)S(1)}, u32[]{:S(2)}, u32[]{:S(2)}) collective-permute-start(bf16[1,2,64,256]{3,2,1,0:T(8,128)(2,1)S(1)} %collective-permute-done.2.refs_3_), channel_id=1, source_target_pairs={{0,8},{2,10},{4,12},{6,14},{8,0},{10,2},{12,4},{14,6},{16,24},{18,... | collective-permute-start | bytes 196616 | tf_op jit(solution)/shard_map/ppermute | solution.py:32
  13.2 3.6 %collective-permute-start.9 = (bf16[1,2,64,256]{3,2,1,0:T(8,128)(2,1)S(1)}, bf16[1,2,64,256]{3,2,1,0:T(8,128)(2,1)S(1)}, u32[]{:S(2)}, u32[]{:S(2)}) collective-permute-start(bf16[1,2,64,256]{3,2,1,0:T(8,128)(2,1)S(1)} %collective-permute-done.7.refs_8_), channel_id=1, source_target_pairs={{0,8},{2,10},{4,12},{6,14},{8,0},{10,2},{12,4},{14,6},{16,24},{18,... | collective-permute-start | bytes 196616 | tf_op jit(solution)/shard_map/ppermute | solution.py:32
  13.7 3.1 %collective-permute-start.10 = (bf16[1,2,64,256]{3,2,1,0:T(8,128)(2,1)S(1)}, bf16[1,2,64,256]{3,2,1,0:T(8,128)(2,1)S(1)}, u32[]{:S(2)}, u32[]{:S(2)}) collective-permute-start(bf16[1,2,64,256]{3,2,1,0:T(8,128)(2,1)S(1)} %collective-permute-done.8.refs_9_), channel_id=1, source_target_pairs={{0,8},{2,10},{4,12},{6,14},{8,0},{10,2},{12,4},{14,6},{16,24},{18,... | collective-permute-start | bytes 196616 | tf_op jit(solution)/shard_map/ppermute | solution.py:32
  15.6 2.1 %collective-permute-start.14 = (bf16[1,2,64,256]{3,2,1,0:T(8,128)(2,1)S(1)}, bf16[1,2,64,256]{3,2,1,0:T(8,128)(2,1)S(1)}, u32[]{:S(2)}, u32[]{:S(2)}) collective-permute-start(bf16[1,2,64,256]{3,2,1,0:T(8,128)(2,1)S(1)} %collective-permute-done.13.refs_5_), channel_id=1, source_target_pairs={{0,8},{2,10},{4,12},{6,14},{8,0},{10,2},{12,4},{14,6},{16,24},{18,... | collective-permute-start | bytes 196616 | tf_op jit(solution)/shard_map/ppermute | solution.py:32
  16.8 1.3 %collective-permute-start.12 = (bf16[1,2,64,256]{3,2,1,0:T(8,128)(2,1)S(1)}, bf16[1,2,64,256]{3,2,1,0:T(8,128)(2,1)S(1)}, u32[]{:S(2)}, u32[]{:S(2)}) collective-permute-start(bf16[1,2,64,256]{3,2,1,0:T(8,128)(2,1)S(1)} %collective-permute-done.11.refs_3_), channel_id=1, source_target_pairs={{0,8},{2,10},{4,12},{6,14},{8,0},{10,2},{12,4},{14,6},{16,24},{18,... | collective-permute-start | bytes 196616 | tf_op jit(solution)/shard_map/ppermute | solution.py:32
  18.3 3.6 %collective-permute-start.15 = (f32[1,64]{1,0:T(1,128)S(1)}, f32[1,64]{1,0:T(1,128)S(1)}, u32[]{:S(2)}, u32[]{:S(2)}) collective-permute-start(f32[1,64]{1,0:T(1,128)S(1)} %get-tuple-element.24.own_ref), channel_id=1, source_target_pairs={{0,1},{1,0},{2,3},{3,2},{4,5},{5,4},{6,7},{7,6},{8,9},{9,8},{10,11... | collective-permute-start | bytes 776 | tf_op jit(solution)/shard_map/ppermute | solution.py:32

commit v4 on v3

--- a/solution.py
+++ b/solution.py
@@ -16,13 +16,13 @@
 
 def plan_of():
     steps = [("p3", (0, 3), "own", None), ("p2", (0, 2), "own", None), ("p1", (0, 1), "own", None)]
-    for part in "0321":
-        source = "own" if part == "0" else "p" + part
-        steps.append(("x" + part, (2, 0), source, PREPARED if part == "2" else None))
-        steps.append(("c" + part, (1, 0), source, None))
+    steps += [("x0", (2, 0), "own", None), ("c0", (1, 0), "own", PREPARED)]
+    steps += [("x3", (2, 0), "p3", None), ("x2", (2, 0), "p2", None)]
+    steps += [("c3", (1, 0), "p3", None), ("c2", (1, 0), "p2", None)]
+    steps += [("x1", (2, 0), "p1", None), ("c1", (1, 0), "p1", None)]
     steps += [("d" + part, (1, 0), "x" + part, None) for part in "0321"]
-    early = ["kept", "p1", "p2", "p3", "c0", "c1", "c2", "c3", "x0", "x3", "d0", "d3"]
-    return steps, early, ["x1", "d1", "x2", "d2"]
+    early = ["kept", "p3", "p2", "c2", "c0", "c1", "p1", "c3", "x1", "x3", "d3", "d0"]
+    return steps, early, ["d2", "d1", "x2", "x0"]
 
 
 def exchanged(shard, axes, by):
@@ -112,38 +112,57 @@
     return sum(ref.shape[0] * ref.shape[2] for ref in kv_refs)
 
 
-def upper_clips():
-    return lax.axis_index("span") >= lax.axis_size("span") // 2
-
-
-def early_kernel(lower_count, rows_ref, bias_ref, *refs):
+def on_half(offsets, counts, call):
+    across = lax.axis_size("span") // 2
+    upper = lax.axis_index("span") >= across
+    useful, at = [], 0
+    for i, count in enumerate(counts):
+        if any(by < across for by, _ in offsets[at : at + count]):
+            useful.append(i)
+        at += count
+    while sum(counts[i] for i in useful) % 2:
+        useful.append(min(i for i in range(len(counts)) if i not in useful))
+    pl.when(upper)(lambda: call(list(range(len(counts)))))
+    pl.when(jnp.logical_not(upper))(lambda: call(useful))
+
+
+def bias_of(bias_ref, first, kv_refs, chosen):
+    parts, at = [], first
+    for i, ref in enumerate(kv_refs):
+        if i in chosen:
+            parts.append(bias_ref[0:1, at : at + keys_in([ref])])
+        at += keys_in([ref])
+    return jnp.concatenate(parts, axis=1)
+
+
+def early_kernel(offsets, rows_ref, bias_ref, *refs):
     kv_refs, (max_ref, sums_ref, mixed_ref) = refs[:-3], refs[-3:]
 
-    def fold_in(kv_refs):
-        keys = keys_in(kv_refs)
+    def fold_in(chosen):
+        bias = bias_of(bias_ref, 0, kv_refs, chosen)
         for g in range(rows_ref.shape[0]):
             lanes = slice(g * HD, (g + 1) * HD)
-            state = fold(rows_ref[g], kv_refs, bias_ref[0:1, :keys], lanes, None)
+            state = fold(rows_ref[g], [kv_refs[i] for i in sorted(chosen)], bias, lanes, None)
             max_ref[g] = jnp.broadcast_to(state[0], max_ref.shape[1:])
             sums_ref[g] = state[1]
             mixed_ref[g] = state[2]
 
-    pl.when(upper_clips())(lambda: fold_in(kv_refs))
-    pl.when(jnp.logical_not(upper_clips()))(lambda: fold_in(kv_refs[:lower_count]))
-
-
-def late_kernel(group_size, rows_ref, bias_ref, *refs):
+    on_half(offsets, [ref.shape[0] for ref in kv_refs], fold_in)
+
+
+def late_kernel(group_size, offsets, rows_ref, bias_ref, *refs):
     states, kv_refs, (attended_ref, squares_ref) = refs[:3], refs[3:-2], refs[-2:]
     rows = rows_ref.shape[1] // group_size
     first = bias_ref.shape[1] - keys_in(kv_refs)
 
-    def end(folds):
+    def end(chosen):
         squares = jnp.zeros((rows, HD), jnp.float32)
         for g in range(rows_ref.shape[0]):
             lanes = slice(g * HD, (g + 1) * HD)
             state = [ref[g] for ref in states]
-            if folds:
-                state = fold(rows_ref[g], kv_refs, bias_ref[0:1, first:], lanes, state)
+            if chosen:
+                bias = bias_of(bias_ref, first, kv_refs, chosen)
+                state = fold(rows_ref[g], [kv_refs[i] for i in sorted(chosen)], bias, lanes, state)
             mixed = state[2] / jnp.sum(state[1], axis=1, keepdims=True)
             for r in range(group_size):
                 block = mixed[r * rows : (r + 1) * rows]
@@ -152,8 +171,7 @@
                 squares = squares + block * block
         squares_ref[...] = jnp.sum(squares.T, axis=0, keepdims=True)
 
-    pl.when(upper_clips())(lambda: end(True))
-    pl.when(jnp.logical_not(upper_clips()))(lambda: end(False))
+    on_half(offsets, [ref.shape[0] for ref in kv_refs], end)
 
 
 def finish_kernel(features, attended_ref, own_ref, other_ref, factor_ref, live_ref, out_ref):
@@ -186,36 +204,17 @@
 def offsets_of(steps):
     at = {"own": [(0, 0)], "kept": [(0, 0)]}
     for name, hop, source, _ in steps:
-        if hop is None:
-            at[name] = [offset for part in source for offset in at[part]]
-        else:
-            at[name] = [(clip ^ hop[0], part ^ hop[1]) for clip, part in at[source]]
+        at[name] = [(clip ^ hop[0], part ^ hop[1]) for clip, part in at[source]]
     return at
-
-
-def pack_kernel(*refs):
-    at = 0
-    for ref in refs[:-1]:
-        refs[-1][at : at + ref.shape[0]] = ref[...]
-        at += ref.shape[0]
-
-
-def pack(arrays):
-    shape = (sum(array.shape[0] for array in arrays), *arrays[0].shape[1:])
-    out = jax.ShapeDtypeStruct(shape, arrays[0].dtype)
-    return kernel(pack_kernel, out, len(arrays), 4, "pack")(*arrays)
 
 
 def travel(steps, own, kept, prepared):
     have = {"own": own, "kept": kept, PREPARED: prepared}
     for name, hop, source, wait_for in steps:
-        if hop is None:
-            have[name] = pack([have[part] for part in source])
-        else:
-            shard = have[source]
-            if wait_for is not None:
-                shard = after(shard, *[have[n] for n in wait_for.split()])
-            have[name] = exchanged(shard, ("span", "seq"), hop)
+        shard = have[source]
+        if wait_for is not None:
+            shard = after(shard, have[wait_for])
+        have[name] = exchanged(shard, ("span", "seq"), hop)
     return have
 
 
@@ -228,9 +227,9 @@
     stacked = (kv_heads_here, group_size * tokens_here, HD)
     steps, early, late = plan_of()
     offsets = offsets_of(steps)
-    across = lax.axis_size("span") // 2
-    lower_count = sum(all(by < across for by, _ in offsets[name]) for name in early)
-    offsets = [at for name in early + late for at in offsets[name]]
+    early_at = [at for name in early for at in offsets[name]]
+    late_at = [at for name in late for at in offsets[name]]
+    offsets = early_at + late_at
     outs = (
         jax.ShapeDtypeStruct(stacked, queries.dtype),
         jax.ShapeDtypeStruct(own.shape, own.dtype),
@@ -252,12 +251,12 @@
     )(*(in_hbm(x) for x in sources))
     have = travel(steps, own, own_kept, rows)
     state = kernel(
-        functools.partial(early_kernel, lower_count), (f32(stacked),) * 3, 2 + len(early), 16, "attend_early"
+        functools.partial(early_kernel, early_at), (f32(stacked),) * 3, 2 + len(early), 16, "attend_early"
     )(
         rows, bias, *[have[name] for name in early]
     )
     attended, squares = kernel(
-        functools.partial(late_kernel, group_size),
+        functools.partial(late_kernel, group_size, late_at),
         (f32((tokens_here, width)), f32((1, tokens_here))),
         5 + len(late), 16, "attend_late",
     )(rows, bias, *state, *[have[name] for name in late])

time: 22.9 us -> 22.4 us (0.978)
  waiting for transfers between devices: 6.88 us -> 5.23 us
  starting transfers between devices: 12.6 us -> 13.6 us
    ppermute x16, waiting for transfers between devices: 6.88 us -> 5.23 us  [exchanged(): lax.ppermute(shard, axes, [(i, places.index(there)) for i, there in enume...]
    ppermute x16, starting transfers between devices: 12.6 us -> 13.6 us  [exchanged(): lax.ppermute(shard, axes, [(i, places.index(there)) for i, there in enume...]
  transfers between devices with their start and end apart: 16 -> 16, of which waited for: 7 -> 5; matrix products, arithmetic and copies ran while one was open for 0% -> 0% of each run, Pallas kernels for 9% -> 10%
where the time goes in v4:
time: 22.4 us; the launch traced here: 22.2 us
  starting transfers between devices  13.6 us (61%)
  waiting for transfers between devices  5.23 us (23%)
  Pallas kernels  3.28 us (15%)
    ppermute x16, starting transfers between devices, exchanged(): lax.ppermute(shard, axes, [(i, places.index(there)) for i, there in enume...  13.6 us
    ppermute x16, waiting for transfers between devices, exchanged(): lax.ppermute(shard, axes, [(i, places.index(there)) for i, there in enume...  5.23 us
    pallas_call x1, Pallas kernels, by_exchange(): pl.pallas_call(functools.partial(prepare_kernel, offsets, len(outs)), out...  1.28 us
    pallas_call x1, Pallas kernels, by_exchange(): kernel(functools.partial(early_kernel, early_at), (f32(stacked),) * 3, 2...  0.9 us
    pallas_call x1, Pallas kernels, by_exchange(): kernel(functools.partial(finish_kernel, width * lax.axis_size('mp')), jax...  0.81 us
  transfers between devices with their start and end apart: 16, of which 5 were waited for; matrix products, arithmetic and copies ran while one was open for 0% of the time, Pallas kernels for 10%

profile of v4, /device:TPU:0, one launch (start us, length us, event | category | flops | bytes accessed | tf_op | source)
XLA Modules:
  0.0 22.2 jit_solution(5848570320987380171)
XLA Ops:
  0.0 5.0 %collective-permute-start = (bf16[1,2,64,256]{3,2,1,0:T(8,128)(2,1)}, bf16[1,2,64,256]{3,2,1,0:T(8,128)(2,1)S(1)}, u32[]{:S(2)}, u32[]{:S(2)}) collective-permute-start(bf16[1,2,64,256]{3,2,1,0:T(8,128)(2,1)} %bitcast.3), channel_id=1, source_target_pairs={{0,6},{2,4},{4,2},{6,0},{8,14},{10,12},{12,10},{14,8},{16,22},{18,... | collective-permute-start | bytes 196616 | tf_op jit(solution)/shard_map/ppermute | solution.py:32
  5.0 0.0 collective-permute-start.4
  5.1 0.6 %collective-permute-start.1 = (bf16[1,2,64,256]{3,2,1,0:T(8,128)(2,1)}, bf16[1,2,64,256]{3,2,1,0:T(8,128)(2,1)S(1)}, u32[]{:S(2)}, u32[]{:S(2)}) collective-permute-start(bf16[1,2,64,256]{3,2,1,0:T(8,128)(2,1)} %bitcast.5), channel_id=1, source_target_pairs={{0,4},{2,6},{4,0},{6,2},{8,12},{10,14},{12,8},{14,10},{16,20},{18,... | collective-permute-start | bytes 196616 | tf_op jit(solution)/shard_map/ppermute | solution.py:32
  5.6 1.3 %prepare.1 = (bf16[2,384,128]{2,1,0:T(8,128)(2,1)S(1)}, bf16[1,2,64,256]{3,2,1,0:T(8,128)(2,1)S(1)}, f32[8,1536]{1,0:T(8,128)S(1)}, f32[8,1024]{1,0:T(8,128)S(1)}, f32[64,128]{1,0:T(8,128)S(1)}) custom-call(bf16[64,1536]{1,0:T(8,128)(2,1)} %bitcast.2, bf16[64,1536]{1,0:T(8,128)(2,1)} %refs_1_.1, bf16[1536]{0:T(1024)(128)(2,1)} %refs_2_.1, s32[4]{0:T(128)} %refs_3_.1, ...), custom_call_target="tpu_custom_call" | custom-call | tf_op jit(solution)/shard_map/prepare/pallas_call | solution.py:242
  6.9 0.1 collective-permute-start.3
  7.0 1.8 %collective-permute-start.10 = (bf16[1,2,64,256]{3,2,1,0:T(8,128)(2,1)S(1)}, bf16[1,2,64,256]{3,2,1,0:T(8,128)(2,1)S(1)}, u32[]{:S(2)}, u32[]{:S(2)}) collective-permute-start(bf16[1,2,64,256]{3,2,1,0:T(8,128)(2,1)S(1)} %bitcast.8), channel_id=1, source_target_pairs={{0,16},{2,18},{4,20},{6,22},{8,24},{10,26},{12,28},{14,30},{16,0},... | collective-permute-start | bytes 196616 | tf_op jit(solution)/shard_map/ppermute | solution.py:32
  8.8 0.0 collective-permute-done.refs_1_
  8.8 0.9 %collective-permute-start.8 = (bf16[1,2,64,256]{3,2,1,0:T(8,128)(2,1)S(1)}, bf16[1,2,64,256]{3,2,1,0:T(8,128)(2,1)S(1)}, u32[]{:S(2)}, u32[]{:S(2)}) collective-permute-start(bf16[1,2,64,256]{3,2,1,0:T(8,128)(2,1)S(1)} %collective-permute-done.refs_1_), channel_id=1, source_target_pairs={{0,16},{2,18},{4,20},{6,22},{8,24},{10,26},{12,28},{14,30},{16,0},... | collective-permute-start | bytes 196616 | tf_op jit(solution)/shard_map/ppermute | solution.py:32
  9.7 0.3 %collective-permute-done.4.refs_6_ = bf16[1,2,64,256]{3,2,1,0:T(8,128)(2,1)S(1)} collective-permute-done((bf16[1,2,64,256]{3,2,1,0:T(8,128)(2,1)}, bf16[1,2,64,256]{3,2,1,0:T(8,128)(2,1)S(1)}, u32[]{:S(2)}, u32[]{:S(2)}) %collective-permute-start.4) | collective-permute-done | bytes 65568 | tf_op jit(solution)/shard_map/ppermute | solution.py:32
  9.9 1.6 %collective-permute-start.7 = (bf16[1,2,64,256]{3,2,1,0:T(8,128)(2,1)S(1)}, bf16[1,2,64,256]{3,2,1,0:T(8,128)(2,1)S(1)}, u32[]{:S(2)}, u32[]{:S(2)}) collective-permute-start(bf16[1,2,64,256]{3,2,1,0:T(8,128)(2,1)S(1)} %collective-permute-done.4.refs_6_), channel_id=1, source_target_pairs={{0,16},{2,18},{4,20},{6,22},{8,24},{10,26},{12,28},{14,30},{16,0},... | collective-permute-start | bytes 196616 | tf_op jit(solution)/shard_map/ppermute | solution.py:32
  11.5 0.0 collective-permute-done.1.refs_2_
  11.5 0.0 collective-permute-start.2
  11.6 0.0 collective-permute-done.3.refs_4_
  11.6 0.8 %collective-permute-start.12 = (bf16[1,2,64,256]{3,2,1,0:T(8,128)(2,1)S(1)}, bf16[1,2,64,256]{3,2,1,0:T(8,128)(2,1)S(1)}, u32[]{:S(2)}, u32[]{:S(2)}) collective-permute-start(bf16[1,2,64,256]{3,2,1,0:T(8,128)(2,1)S(1)} %collective-permute-done.1.refs_2_), channel_id=1, source_target_pairs={{0,16},{2,18},{4,20},{6,22},{8,24},{10,26},{12,28},{14,30},{16,0},... | collective-permute-start | bytes 196616 | tf_op jit(solution)/shard_map/ppermute | solution.py:32
  12.4 0.0 collective-permute-done.10.refs_6_
  12.4 0.2 %collective-permute-start.5 = (bf16[1,2,64,256]{3,2,1,0:T(8,128)(2,1)S(1)}, bf16[1,2,64,256]{3,2,1,0:T(8,128)(2,1)S(1)}, u32[]{:S(2)}, u32[]{:S(2)}) collective-permute-start(bf16[1,2,64,256]{3,2,1,0:T(8,128)(2,1)S(1)} %collective-permute-done.4.refs_6_), channel_id=1, source_target_pairs={{0,8},{2,10},{4,12},{6,14},{8,0},{10,2},{12,4},{14,6},{16,24},{18,... | collective-permute-start | bytes 196616 | tf_op jit(solution)/shard_map/ppermute | solution.py:32
  12.6 1.0 %collective-permute-done.8.refs_9_ = bf16[1,2,64,256]{3,2,1,0:T(8,128)(2,1)S(1)} collective-permute-done((bf16[1,2,64,256]{3,2,1,0:T(8,128)(2,1)S(1)}, bf16[1,2,64,256]{3,2,1,0:T(8,128)(2,1)S(1)}, u32[]{:S(2)}, u32[]{:S(2)}) %collective-permute-start.8) | collective-permute-done | bytes 65568 | tf_op jit(solution)/shard_map/ppermute | solution.py:32
  13.6 0.0 collective-permute-start.6
  13.6 0.7 %collective-permute-done.7.refs_8_ = bf16[1,2,64,256]{3,2,1,0:T(8,128)(2,1)S(1)} collective-permute-done((bf16[1,2,64,256]{3,2,1,0:T(8,128)(2,1)S(1)}, bf16[1,2,64,256]{3,2,1,0:T(8,128)(2,1)S(1)}, u32[]{:S(2)}, u32[]{:S(2)}) %collective-permute-start.7) | collective-permute-done | bytes 65568 | tf_op jit(solution)/shard_map/ppermute | solution.py:32
  14.3 0.0 collective-permute-start.11
  14.3 0.0 collective-permute-done.2.refs_3_
  14.4 0.5 %collective-permute-start.9 = (bf16[1,2,64,256]{3,2,1,0:T(8,128)(2,1)S(1)}, bf16[1,2,64,256]{3,2,1,0:T(8,128)(2,1)S(1)}, u32[]{:S(2)}, u32[]{:S(2)}) collective-permute-start(bf16[1,2,64,256]{3,2,1,0:T(8,128)(2,1)S(1)} %collective-permute-done.8.refs_9_), channel_id=1, source_target_pairs={{0,8},{2,10},{4,12},{6,14},{8,0},{10,2},{12,4},{14,6},{16,24},{18,... | collective-permute-start | bytes 196616 | tf_op jit(solution)/shard_map/ppermute | solution.py:32
  14.9 1.2 %collective-permute-done.12.refs_5_ = bf16[1,2,64,256]{3,2,1,0:T(8,128)(2,1)S(1)} collective-permute-done((bf16[1,2,64,256]{3,2,1,0:T(8,128)(2,1)S(1)}, bf16[1,2,64,256]{3,2,1,0:T(8,128)(2,1)S(1)}, u32[]{:S(2)}, u32[]{:S(2)}) %collective-permute-start.12) | collective-permute-done | bytes 65568 | tf_op jit(solution)/shard_map/ppermute | solution.py:32
  16.1 0.0 collective-permute-start.13
  16.1 0.5 %collective-permute-start.14 = (bf16[1,2,64,256]{3,2,1,0:T(8,128)(2,1)S(1)}, bf16[1,2,64,256]{3,2,1,0:T(8,128)(2,1)S(1)}, u32[]{:S(2)}, u32[]{:S(2)}) collective-permute-start(bf16[1,2,64,256]{3,2,1,0:T(8,128)(2,1)S(1)} %collective-permute-done.7.refs_8_), channel_id=1, source_target_pairs={{0,8},{2,10},{4,12},{6,14},{8,0},{10,2},{12,4},{14,6},{16,24},{18,... | collective-permute-start | bytes 196616 | tf_op jit(solution)/shard_map/ppermute | solution.py:32
  16.6 0.0 collective-permute-done.9.refs_10_
  16.6 0.9 %attend_early.1 = (f32[2,384,128]{2,1,0:T(8,128)S(1)}, f32[2,384,128]{2,1,0:T(8,128)S(1)}, f32[2,384,128]{2,1,0:T(8,128)S(1)}) custom-call(bf16[2,384,128]{2,1,0:T(8,128)(2,1)S(1)} %get-tuple-element.16.rows_ref, f32[8,1024]{1,0:T(8,128)S(1)} %get-tuple-element.17.bias_ref, bf16[1,2,64,256]{3,2,1,0:T(8,128)(2,1)S(1)} %get-tuple-element.18.refs_0_, ...), custom_call_target="tpu_custom_call" | custom-call | tf_op jit(solution)/shard_map/attend_early/pallas_call | solution.py:253
  17.5 0.0 collective-permute-done.13.refs_3_
  17.5 0.3 %attend_late.1 = (f32[64,1536]{1,0:T(8,128)S(1)}, f32[1,64]{1,0:T(1,128)S(1)}) custom-call(bf16[2,384,128]{2,1,0:T(8,128)(2,1)S(1)} %get-tuple-element.16.rows_ref, f32[8,1024]{1,0:T(8,128)S(1)} %get-tuple-element.17.bias_ref, f32[2,384,128]{2,1,0:T(8,128)S(1)} %get-tuple-element.20.refs_0_, f32[2,384,128]{2,1,0:T(8,128)S(1)} %get-tuple-element.21.refs_1_, ...), custom_call_target="tpu_custom_call" | custom-call | tf_op jit(solution)/shard_map/attend_late/pallas_call | solution.py:258
  17.8 1.6 %collective-permute-start.15 = (f32[1,64]{1,0:T(1,128)S(1)}, f32[1,64]{1,0:T(1,128)S(1)}, u32[]{:S(2)}, u32[]{:S(2)}) collective-permute-start(f32[1,64]{1,0:T(1,128)S(1)} %get-tuple-element.24.own_ref), channel_id=1, source_target_pairs={{0,1},{1,0},{2,3},{3,2},{4,5},{5,4},{6,7},{7,6},{8,9},{9,8},{10,11... | collective-permute-start | bytes 776 | tf_op jit(solution)/shard_map/ppermute | solution.py:32
  19.4 2.0 %collective-permute-done.15.other_ref = f32[1,64]{1,0:T(1,128)S(1)} collective-permute-done((f32[1,64]{1,0:T(1,128)S(1)}, f32[1,64]{1,0:T(1,128)S(1)}, u32[]{:S(2)}, u32[]{:S(2)}) %collective-permute-start.15) | collective-permute-done | bytes 288 | tf_op jit(solution)/shard_map/ppermute | solution.py:32
  21.4 0.8 %finish.1 = bf16[1,64,1536]{2,1,0:T(8,128)(2,1)} custom-call(f32[64,1536]{1,0:T(8,128)S(1)} %get-tuple-element.23.attended_ref, f32[1,64]{1,0:T(1,128)S(1)} %get-tuple-element.24.own_ref, f32[1,64]{1,0:T(1,128)S(1)} %collective-permute-done.15.other_ref, f32[8,1536]{1,0:T(8,128)S(1)} %get-tuple-element.25.factor_ref, f32[64,128]{1,0:T(8,128)S(1)} %get-tuple-element.26.live_ref), custom_call_target="tpu_custom_call" | custom-call | tf_op jit(solution)/shard_map/finish/pallas_call | solution.py:264
  (6 shorter events, 0.0 us)
Async XLA Ops:
  0.0 8.8 %collective-permute-start = (bf16[1,2,64,256]{3,2,1,0:T(8,128)(2,1)}, bf16[1,2,64,256]{3,2,1,0:T(8,128)(2,1)S(1)}, u32[]{:S(2)}, u32[]{:S(2)}) collective-permute-start(bf16[1,2,64,256]{3,2,1,0:T(8,128)(2,1)} %bitcast.3), channel_id=1, source_target_pairs={{0,6},{2,4},{4,2},{6,0},{8,14},{10,12},{12,10},{14,8},{16,22},{18,... | collective-permute-start | bytes 196616 | tf_op jit(solution)/shard_map/ppermute | solution.py:32
  5.0 4.9 %collective-permute-start.4 = (bf16[1,2,64,256]{3,2,1,0:T(8,128)(2,1)}, bf16[1,2,64,256]{3,2,1,0:T(8,128)(2,1)S(1)}, u32[]{:S(2)}, u32[]{:S(2)}) collective-permute-start(bf16[1,2,64,256]{3,2,1,0:T(8,128)(2,1)} %bitcast.4), channel_id=1, source_target_pairs={{0,2},{2,0},{4,6},{6,4},{8,10},{10,8},{12,14},{14,12},{16,18},{18,... | collective-permute-start | bytes 196616 | tf_op jit(solution)/shard_map/ppermute | solution.py:32
  5.1 6.5 %collective-permute-start.1 = (bf16[1,2,64,256]{3,2,1,0:T(8,128)(2,1)}, bf16[1,2,64,256]{3,2,1,0:T(8,128)(2,1)S(1)}, u32[]{:S(2)}, u32[]{:S(2)}) collective-permute-start(bf16[1,2,64,256]{3,2,1,0:T(8,128)(2,1)} %bitcast.5), channel_id=1, source_target_pairs={{0,4},{2,6},{4,0},{6,2},{8,12},{10,14},{12,8},{14,10},{16,20},{18,... | collective-permute-start | bytes 196616 | tf_op jit(solution)/shard_map/ppermute | solution.py:32
  5.6 1.3 %copy-start = (bf16[2,1,64,256]{3,2,1,0:T(8,128)(2,1)S(1)}, bf16[2,1,64,256]{3,2,1,0:T(8,128)(2,1)}, u32[]{:S(2)}) copy-start(bf16[2,1,64,256]{3,2,1,0:T(8,128)(2,1)} %param.7) | copy-start | bytes 196612
  6.9 4.6 %collective-permute-start.3 = (bf16[1,2,64,256]{3,2,1,0:T(8,128)(2,1)S(1)}, bf16[1,2,64,256]{3,2,1,0:T(8,128)(2,1)S(1)}, u32[]{:S(2)}, u32[]{:S(2)}) collective-permute-start(bf16[1,2,64,256]{3,2,1,0:T(8,128)(2,1)S(1)} %bitcast.7), channel_id=1, source_target_pairs={{0,8},{2,10},{4,12},{6,14},{8,0},{10,2},{12,4},{14,6},{16,24},{18,... | collective-permute-start | bytes 196616 | tf_op jit(solution)/shard_map/ppermute | solution.py:32
  7.0 5.4 %collective-permute-start.10 = (bf16[1,2,64,256]{3,2,1,0:T(8,128)(2,1)S(1)}, bf16[1,2,64,256]{3,2,1,0:T(8,128)(2,1)S(1)}, u32[]{:S(2)}, u32[]{:S(2)}) collective-permute-start(bf16[1,2,64,256]{3,2,1,0:T(8,128)(2,1)S(1)} %bitcast.8), channel_id=1, source_target_pairs={{0,16},{2,18},{4,20},{6,22},{8,24},{10,26},{12,28},{14,30},{16,0},... | collective-permute-start | bytes 196616 | tf_op jit(solution)/shard_map/ppermute | solution.py:32
  8.8 4.9 %collective-permute-start.8 = (bf16[1,2,64,256]{3,2,1,0:T(8,128)(2,1)S(1)}, bf16[1,2,64,256]{3,2,1,0:T(8,128)(2,1)S(1)}, u32[]{:S(2)}, u32[]{:S(2)}) collective-permute-start(bf16[1,2,64,256]{3,2,1,0:T(8,128)(2,1)S(1)} %collective-permute-done.refs_1_), channel_id=1, source_target_pairs={{0,16},{2,18},{4,20},{6,22},{8,24},{10,26},{12,28},{14,30},{16,0},... | collective-permute-start | bytes 196616 | tf_op jit(solution)/shard_map/ppermute | solution.py:32
  9.9 4.4 %collective-permute-start.7 = (bf16[1,2,64,256]{3,2,1,0:T(8,128)(2,1)S(1)}, bf16[1,2,64,256]{3,2,1,0:T(8,128)(2,1)S(1)}, u32[]{:S(2)}, u32[]{:S(2)}) collective-permute-start(bf16[1,2,64,256]{3,2,1,0:T(8,128)(2,1)S(1)} %collective-permute-done.4.refs_6_), channel_id=1, source_target_pairs={{0,16},{2,18},{4,20},{6,22},{8,24},{10,26},{12,28},{14,30},{16,0},... | collective-permute-start | bytes 196616 | tf_op jit(solution)/shard_map/ppermute | solution.py:32
  11.5 2.8 %collective-permute-start.2 = (bf16[1,2,64,256]{3,2,1,0:T(8,128)(2,1)S(1)}, bf16[1,2,64,256]{3,2,1,0:T(8,128)(2,1)S(1)}, u32[]{:S(2)}, u32[]{:S(2)}) collective-permute-start(bf16[1,2,64,256]{3,2,1,0:T(8,128)(2,1)S(1)} %collective-permute-done.1.refs_2_), channel_id=1, source_target_pairs={{0,8},{2,10},{4,12},{6,14},{8,0},{10,2},{12,4},{14,6},{16,24},{18,... | collective-permute-start | bytes 196616 | tf_op jit(solution)/shard_map/ppermute | solution.py:32
  11.6 4.5 %collective-permute-start.12 = (bf16[1,2,64,256]{3,2,1,0:T(8,128)(2,1)S(1)}, bf16[1,2,64,256]{3,2,1,0:T(8,128)(2,1)S(1)}, u32[]{:S(2)}, u32[]{:S(2)}) collective-permute-start(bf16[1,2,64,256]{3,2,1,0:T(8,128)(2,1)S(1)} %collective-permute-done.1.refs_2_), channel_id=1, source_target_pairs={{0,16},{2,18},{4,20},{6,22},{8,24},{10,26},{12,28},{14,30},{16,0},... | collective-permute-start | bytes 196616 | tf_op jit(solution)/shard_map/ppermute | solution.py:32
  12.4 3.7 %collective-permute-start.5 = (bf16[1,2,64,256]{3,2,1,0:T(8,128)(2,1)S(1)}, bf16[1,2,64,256]{3,2,1,0:T(8,128)(2,1)S(1)}, u32[]{:S(2)}, u32[]{:S(2)}) collective-permute-start(bf16[1,2,64,256]{3,2,1,0:T(8,128)(2,1)S(1)} %collective-permute-done.4.refs_6_), channel_id=1, source_target_pairs={{0,8},{2,10},{4,12},{6,14},{8,0},{10,2},{12,4},{14,6},{16,24},{18,... | collective-permute-start | bytes 196616 | tf_op jit(solution)/shard_map/ppermute | solution.py:32
  13.6 2.9 %collective-permute-start.6 = (bf16[1,2,64,256]{3,2,1,0:T(8,128)(2,1)S(1)}, bf16[1,2,64,256]{3,2,1,0:T(8,128)(2,1)S(1)}, u32[]{:S(2)}, u32[]{:S(2)}) collective-permute-start(bf16[1,2,64,256]{3,2,1,0:T(8,128)(2,1)S(1)} %collective-permute-done.refs_1_), channel_id=1, source_target_pairs={{0,8},{2,10},{4,12},{6,14},{8,0},{10,2},{12,4},{14,6},{16,24},{18,... | collective-permute-start | bytes 196616 | tf_op jit(solution)/shard_map/ppermute | solution.py:32
  14.3 2.2 %collective-permute-start.11 = (bf16[1,2,64,256]{3,2,1,0:T(8,128)(2,1)S(1)}, bf16[1,2,64,256]{3,2,1,0:T(8,128)(2,1)S(1)}, u32[]{:S(2)}, u32[]{:S(2)}) collective-permute-start(bf16[1,2,64,256]{3,2,1,0:T(8,128)(2,1)S(1)} %collective-permute-done.10.refs_6_), channel_id=1, source_target_pairs={{0,8},{2,10},{4,12},{6,14},{8,0},{10,2},{12,4},{14,6},{16,24},{18,... | collective-permute-start | bytes 196616 | tf_op jit(solution)/shard_map/ppermute | solution.py:32
  14.4 2.2 %collective-permute-start.9 = (bf16[1,2,64,256]{3,2,1,0:T(8,128)(2,1)S(1)}, bf16[1,2,64,256]{3,2,1,0:T(8,128)(2,1)S(1)}, u32[]{:S(2)}, u32[]{:S(2)}) collective-permute-start(bf16[1,2,64,256]{3,2,1,0:T(8,128)(2,1)S(1)} %collective-permute-done.8.refs_9_), channel_id=1, source_target_pairs={{0,8},{2,10},{4,12},{6,14},{8,0},{10,2},{12,4},{14,6},{16,24},{18,... | collective-permute-start | bytes 196616 | tf_op jit(solution)/shard_map/ppermute | solution.py:32
  16.1 1.4 %collective-permute-start.13 = (bf16[1,2,64,256]{3,2,1,0:T(8,128)(2,1)S(1)}, bf16[1,2,64,256]{3,2,1,0:T(8,128)(2,1)S(1)}, u32[]{:S(2)}, u32[]{:S(2)}) collective-permute-start(bf16[1,2,64,256]{3,2,1,0:T(8,128)(2,1)S(1)} %collective-permute-done.12.refs_5_), channel_id=1, source_target_pairs={{0,8},{2,10},{4,12},{6,14},{8,0},{10,2},{12,4},{14,6},{16,24},{18,... | collective-permute-start | bytes 196616 | tf_op jit(solution)/shard_map/ppermute | solution.py:32
  16.1 1.4 %collective-permute-start.14 = (bf16[1,2,64,256]{3,2,1,0:T(8,128)(2,1)S(1)}, bf16[1,2,64,256]{3,2,1,0:T(8,128)(2,1)S(1)}, u32[]{:S(2)}, u32[]{:S(2)}) collective-permute-start(bf16[1,2,64,256]{3,2,1,0:T(8,128)(2,1)S(1)} %collective-permute-done.7.refs_8_), channel_id=1, source_target_pairs={{0,8},{2,10},{4,12},{6,14},{8,0},{10,2},{12,4},{14,6},{16,24},{18,... | collective-permute-start | bytes 196616 | tf_op jit(solution)/shard_map/ppermute | solution.py:32
  17.8 3.6 %collective-permute-start.15 = (f32[1,64]{1,0:T(1,128)S(1)}, f32[1,64]{1,0:T(1,128)S(1)}, u32[]{:S(2)}, u32[]{:S(2)}) collective-permute-start(f32[1,64]{1,0:T(1,128)S(1)} %get-tuple-element.24.own_ref), channel_id=1, source_target_pairs={{0,1},{1,0},{2,3},{3,2},{4,5},{5,4},{6,7},{7,6},{8,9},{9,8},{10,11... | collective-permute-start | bytes 776 | tf_op jit(solution)/shard_map/ppermute | solution.py:32

commit v5 on v4

--- a/solution.py
+++ b/solution.py
@@ -21,8 +21,8 @@
     steps += [("c3", (1, 0), "p3", None), ("c2", (1, 0), "p2", None)]
     steps += [("x1", (2, 0), "p1", None), ("c1", (1, 0), "p1", None)]
     steps += [("d" + part, (1, 0), "x" + part, None) for part in "0321"]
-    early = ["kept", "p3", "p2", "c2", "c0", "c1", "p1", "c3", "x1", "x3", "d3", "d0"]
-    return steps, early, ["d2", "d1", "x2", "x0"]
+    early = ["kept", "p3", "d0", "p1", "c0", "c1", "c2", "c3", "x1", "x3", "p2", "d3"]
+    return steps, early, ["x0", "d1", "x2", "d2"]
 
 
 def exchanged(shard, axes, by):
@@ -108,70 +108,74 @@
     return new_max, weight_sums, mixed
 
 
-def keys_in(kv_refs):
-    return sum(ref.shape[0] * ref.shape[2] for ref in kv_refs)
-
-
-def on_half(offsets, counts, call):
+def on_upper(upper):
     across = lax.axis_size("span") // 2
-    upper = lax.axis_index("span") >= across
-    useful, at = [], 0
-    for i, count in enumerate(counts):
-        if any(by < across for by, _ in offsets[at : at + count]):
-            useful.append(i)
-        at += count
-    while sum(counts[i] for i in useful) % 2:
-        useful.append(min(i for i in range(len(counts)) if i not in useful))
-    pl.when(upper)(lambda: call(list(range(len(counts)))))
-    pl.when(jnp.logical_not(upper))(lambda: call(useful))
-
-
-def bias_of(bias_ref, first, kv_refs, chosen):
-    parts, at = [], first
-    for i, ref in enumerate(kv_refs):
-        if i in chosen:
-            parts.append(bias_ref[0:1, at : at + keys_in([ref])])
-        at += keys_in([ref])
-    return jnp.concatenate(parts, axis=1)
+    return (lax.axis_index("span") >= across) == upper
+
+
+def usable_on_lower(offsets):
+    across = lax.axis_size("span") // 2
+    chosen = [i for i, (by, _) in enumerate(offsets) if by < across]
+    others = [i for i in range(len(offsets)) if i not in chosen]
+    return sorted(chosen + others[: len(chosen) % 2])
+
+
+def bias_of(bias_ref, first, keys, chosen):
+    tiles = [bias_ref[0:1, first + i * keys : first + (i + 1) * keys] for i in chosen]
+    return jnp.concatenate(tiles, axis=1)
+
+
+def put_attended(attended_ref, g, state):
+    rows = attended_ref.shape[0]
+    mixed = state[2] / jnp.sum(state[1], axis=1, keepdims=True)
+    group_size = mixed.shape[0] // rows
+    squares = jnp.zeros((rows, HD), jnp.float32)
+    for r in range(group_size):
+        block = mixed[r * rows : (r + 1) * rows]
+        h = g * group_size + r
+        attended_ref[:, h * HD : (h + 1) * HD] = block
+        squares = squares + block * block
+    return squares
 
 
 def early_kernel(offsets, rows_ref, bias_ref, *refs):
-    kv_refs, (max_ref, sums_ref, mixed_ref) = refs[:-3], refs[-3:]
-
-    def fold_in(chosen):
-        bias = bias_of(bias_ref, 0, kv_refs, chosen)
+    kv_refs, state_refs, (attended_ref, squares_ref) = refs[:-5], refs[-5:-2], refs[-2:]
+    keys = kv_refs[0].shape[2]
+
+    def fold_in(chosen, is_all):
+        squares = []
+        bias = bias_of(bias_ref, 0, keys, chosen)
         for g in range(rows_ref.shape[0]):
             lanes = slice(g * HD, (g + 1) * HD)
-            state = fold(rows_ref[g], [kv_refs[i] for i in sorted(chosen)], bias, lanes, None)
-            max_ref[g] = jnp.broadcast_to(state[0], max_ref.shape[1:])
-            sums_ref[g] = state[1]
-            mixed_ref[g] = state[2]
-
-    on_half(offsets, [ref.shape[0] for ref in kv_refs], fold_in)
-
-
-def late_kernel(group_size, offsets, rows_ref, bias_ref, *refs):
-    states, kv_refs, (attended_ref, squares_ref) = refs[:3], refs[3:-2], refs[-2:]
-    rows = rows_ref.shape[1] // group_size
-    first = bias_ref.shape[1] - keys_in(kv_refs)
-
-    def end(chosen):
-        squares = jnp.zeros((rows, HD), jnp.float32)
+            state = fold(rows_ref[g], [kv_refs[i] for i in chosen], bias, lanes, None)
+            if is_all:
+                squares.append(put_attended(attended_ref, g, state))
+            else:
+                state_refs[0][g] = jnp.broadcast_to(state[0], state_refs[0].shape[1:])
+                state_refs[1][g] = state[1]
+                state_refs[2][g] = state[2]
+        if is_all:
+            squares_ref[...] = jnp.sum(sum(squares).T, axis=0, keepdims=True)
+
+    pl.when(on_upper(True))(lambda: fold_in(range(len(kv_refs)), False))
+    pl.when(on_upper(False))(lambda: fold_in(usable_on_lower(offsets), True))
+
+
+def late_kernel(rows_ref, bias_ref, *refs):
+    states, kv_refs, (attended_ref, squares_ref) = refs[:3], refs[5:-2], refs[-2:]
+    keys = kv_refs[0].shape[2]
+    first = bias_ref.shape[1] - keys * len(kv_refs)
+
+    def end():
+        squares = []
+        bias = bias_of(bias_ref, first, keys, range(len(kv_refs)))
         for g in range(rows_ref.shape[0]):
             lanes = slice(g * HD, (g + 1) * HD)
-            state = [ref[g] for ref in states]
-            if chosen:
-                bias = bias_of(bias_ref, first, kv_refs, chosen)
-                state = fold(rows_ref[g], [kv_refs[i] for i in sorted(chosen)], bias, lanes, state)
-            mixed = state[2] / jnp.sum(state[1], axis=1, keepdims=True)
-            for r in range(group_size):
-                block = mixed[r * rows : (r + 1) * rows]
-                h = g * group_size + r
-                attended_ref[:, h * HD : (h + 1) * HD] = block
-                squares = squares + block * block
-        squares_ref[...] = jnp.sum(squares.T, axis=0, keepdims=True)
-
-    on_half(offsets, [ref.shape[0] for ref in kv_refs], end)
+            state = fold(rows_ref[g], kv_refs, bias, lanes, [ref[g] for ref in states])
+            squares.append(put_attended(attended_ref, g, state))
+        squares_ref[...] = jnp.sum(sum(squares).T, axis=0, keepdims=True)
+
+    pl.when(on_upper(True))(end)
 
 
 def finish_kernel(features, attended_ref, own_ref, other_ref, factor_ref, live_ref, out_ref):
@@ -185,13 +189,14 @@
         out_ref[0, :, lanes] = jnp.where(live, block, 0.0).astype(out_ref.dtype)
 
 
-def kernel(body, outs, count, megabytes, name):
+def kernel(body, outs, count, megabytes, name, in_place={}):
     several = isinstance(outs, tuple)
     return pl.pallas_call(
         body,
         out_shape=outs,
         in_specs=in_vmem(count),
         out_specs=tuple(in_vmem(len(outs))) if several else in_vmem(1)[0],
+        input_output_aliases=in_place,
         compiler_params=pltpu.CompilerParams(vmem_limit_bytes=megabytes * 1024 * 1024),
         name=name,
     )
@@ -250,16 +255,16 @@
         name="prepare",
     )(*(in_hbm(x) for x in sources))
     have = travel(steps, own, own_kept, rows)
-    state = kernel(
-        functools.partial(early_kernel, early_at), (f32(stacked),) * 3, 2 + len(early), 16, "attend_early"
-    )(
-        rows, bias, *[have[name] for name in early]
-    )
+    ends = (f32((tokens_here, width)), f32((1, tokens_here)))
+    *state, attended, squares = kernel(
+        functools.partial(early_kernel, early_at),
+        (f32(stacked),) * 3 + ends,
+        2 + len(early), 16, "attend_early",
+    )(rows, bias, *[have[name] for name in early])
+    assert not usable_on_lower(late_at)
     attended, squares = kernel(
-        functools.partial(late_kernel, group_size, late_at),
-        (f32((tokens_here, width)), f32((1, tokens_here))),
-        5 + len(late), 16, "attend_late",
-    )(rows, bias, *state, *[have[name] for name in late])
+        late_kernel, ends, 7 + len(late), 16, "attend_late", in_place={5: 0, 6: 1}
+    )(rows, bias, *state, attended, squares, *[have[name] for name in late])
     others = [exchanged(squares, ("mp",), (by,)) for by in range(1, lax.axis_size("mp"))]
     return kernel(
         functools.partial(finish_kernel, width * lax.axis_size("mp")),

time: 22.4 us -> 22.1 us (0.987)
  no operation moved by 1% of the time
where the time goes in v5:
time: 22.1 us; the launch traced here: 22 us
  starting transfers between devices  13.7 us (62%)
  waiting for transfers between devices  5.11 us (23%)
  Pallas kernels  3.1 us (14%)
    ppermute x16, starting transfers between devices, exchanged(): lax.ppermute(shard, axes, [(i, places.index(there)) for i, there in enume...  13.7 us
    ppermute x16, waiting for transfers between devices, exchanged(): lax.ppermute(shard, axes, [(i, places.index(there)) for i, there in enume...  5.11 us
    pallas_call x1, Pallas kernels, by_exchange(): pl.pallas_call(functools.partial(prepare_kernel, offsets, len(outs)), out...  1.28 us
    pallas_call x1, Pallas kernels, by_exchange(): kernel(functools.partial(early_kernel, early_at), (f32(stacked),) * 3 + e...  1 us
    pallas_call x1, Pallas kernels, by_exchange(): kernel(functools.partial(finish_kernel, width * lax.axis_size('mp')), jax...  0.81 us
  transfers between devices with their start and end apart: 16, of which 5 were waited for; matrix products, arithmetic and copies ran while one was open for 0% of the time, Pallas kernels for 10%

profile of v5, /device:TPU:0, one launch (start us, length us, event | category | flops | bytes accessed | tf_op | source)
XLA Modules:
  0.0 22.0 jit_solution(10922106355988482148)
XLA Ops:
  0.0 5.0 %collective-permute-start = (bf16[1,2,64,256]{3,2,1,0:T(8,128)(2,1)}, bf16[1,2,64,256]{3,2,1,0:T(8,128)(2,1)S(1)}, u32[]{:S(2)}, u32[]{:S(2)}) collective-permute-start(bf16[1,2,64,256]{3,2,1,0:T(8,128)(2,1)} %bitcast.3), channel_id=1, source_target_pairs={{0,6},{2,4},{4,2},{6,0},{8,14},{10,12},{12,10},{14,8},{16,22},{18,... | collective-permute-start | bytes 196616 | tf_op jit(solution)/shard_map/ppermute | solution.py:32
  5.0 0.0 collective-permute-start.3
  5.1 1.3 %prepare.1 = (bf16[2,384,128]{2,1,0:T(8,128)(2,1)S(1)}, bf16[1,2,64,256]{3,2,1,0:T(8,128)(2,1)S(1)}, f32[8,1536]{1,0:T(8,128)S(1)}, f32[8,1024]{1,0:T(8,128)S(1)}, f32[64,128]{1,0:T(8,128)S(1)}) custom-call(bf16[64,1536]{1,0:T(8,128)(2,1)} %bitcast.2, bf16[64,1536]{1,0:T(8,128)(2,1)} %refs_1_.1, bf16[1536]{0:T(1024)(128)(2,1)} %refs_2_.1, s32[4]{0:T(128)} %refs_3_.1, ...), custom_call_target="tpu_custom_call" | custom-call | tf_op jit(solution)/shard_map/prepare/pallas_call | solution.py:247
  6.4 0.1 collective-permute-start.4
  6.4 0.6 %collective-permute-start.6 = (bf16[1,2,64,256]{3,2,1,0:T(8,128)(2,1)S(1)}, bf16[1,2,64,256]{3,2,1,0:T(8,128)(2,1)S(1)}, u32[]{:S(2)}, u32[]{:S(2)}) collective-permute-start(bf16[1,2,64,256]{3,2,1,0:T(8,128)(2,1)S(1)} %bitcast.7), channel_id=1, source_target_pairs={{0,4},{2,6},{4,0},{6,2},{8,12},{10,14},{12,8},{14,10},{16,20},{18,... | collective-permute-start | bytes 196616 | tf_op jit(solution)/shard_map/ppermute | solution.py:32
  7.1 1.7 %collective-permute-start.1 = (bf16[1,2,64,256]{3,2,1,0:T(8,128)(2,1)S(1)}, bf16[1,2,64,256]{3,2,1,0:T(8,128)(2,1)S(1)}, u32[]{:S(2)}, u32[]{:S(2)}) collective-permute-start(bf16[1,2,64,256]{3,2,1,0:T(8,128)(2,1)S(1)} %bitcast.8), channel_id=1, source_target_pairs={{0,16},{2,18},{4,20},{6,22},{8,24},{10,26},{12,28},{14,30},{16,0},... | collective-permute-start | bytes 196616 | tf_op jit(solution)/shard_map/ppermute | solution.py:32
  8.8 0.0 collective-permute-done.refs_1_
  8.8 0.9 %collective-permute-start.10 = (bf16[1,2,64,256]{3,2,1,0:T(8,128)(2,1)S(1)}, bf16[1,2,64,256]{3,2,1,0:T(8,128)(2,1)S(1)}, u32[]{:S(2)}, u32[]{:S(2)}) collective-permute-start(bf16[1,2,64,256]{3,2,1,0:T(8,128)(2,1)S(1)} %collective-permute-done.refs_1_), channel_id=1, source_target_pairs={{0,16},{2,18},{4,20},{6,22},{8,24},{10,26},{12,28},{14,30},{16,0},... | collective-permute-start | bytes 196616 | tf_op jit(solution)/shard_map/ppermute | solution.py:32
  9.7 0.0 collective-permute-done.3.refs_3_
  9.7 1.4 %collective-permute-start.9 = (bf16[1,2,64,256]{3,2,1,0:T(8,128)(2,1)S(1)}, bf16[1,2,64,256]{3,2,1,0:T(8,128)(2,1)S(1)}, u32[]{:S(2)}, u32[]{:S(2)}) collective-permute-start(bf16[1,2,64,256]{3,2,1,0:T(8,128)(2,1)S(1)} %collective-permute-done.3.refs_3_), channel_id=1, source_target_pairs={{0,16},{2,18},{4,20},{6,22},{8,24},{10,26},{12,28},{14,30},{16,0},... | collective-permute-start | bytes 196616 | tf_op jit(solution)/shard_map/ppermute | solution.py:32
  11.0 0.0 collective-permute-done.4.refs_4_
  11.0 0.0 collective-permute-start.5
  11.0 0.8 %collective-permute-done.6.refs_10_ = bf16[1,2,64,256]{3,2,1,0:T(8,128)(2,1)S(1)} collective-permute-done((bf16[1,2,64,256]{3,2,1,0:T(8,128)(2,1)S(1)}, bf16[1,2,64,256]{3,2,1,0:T(8,128)(2,1)S(1)}, u32[]{:S(2)}, u32[]{:S(2)}) %collective-permute-start.6) | collective-permute-done | bytes 65568 | tf_op jit(solution)/shard_map/ppermute | solution.py:32
  11.8 1.9 %collective-permute-start.13 = (bf16[1,2,64,256]{3,2,1,0:T(8,128)(2,1)S(1)}, bf16[1,2,64,256]{3,2,1,0:T(8,128)(2,1)S(1)}, u32[]{:S(2)}, u32[]{:S(2)}) collective-permute-start(bf16[1,2,64,256]{3,2,1,0:T(8,128)(2,1)S(1)} %collective-permute-done.6.refs_10_), channel_id=1, source_target_pairs={{0,16},{2,18},{4,20},{6,22},{8,24},{10,26},{12,28},{14,30},{16,0},... | collective-permute-start | bytes 196616 | tf_op jit(solution)/shard_map/ppermute | solution.py:32
  13.7 0.0 collective-permute-done.10.refs_9_
  13.7 0.0 collective-permute-start.8
  13.7 0.4 %collective-permute-done.9.refs_8_ = bf16[1,2,64,256]{3,2,1,0:T(8,128)(2,1)S(1)} collective-permute-done((bf16[1,2,64,256]{3,2,1,0:T(8,128)(2,1)S(1)}, bf16[1,2,64,256]{3,2,1,0:T(8,128)(2,1)S(1)}, u32[]{:S(2)}, u32[]{:S(2)}) %collective-permute-start.9) | collective-permute-done | bytes 65568 | tf_op jit(solution)/shard_map/ppermute | solution.py:32
  14.1 0.1 collective-permute-start.2
  14.2 0.0 collective-permute-done.5.refs_5_
  14.2 0.4 %collective-permute-start.11 = (bf16[1,2,64,256]{3,2,1,0:T(8,128)(2,1)S(1)}, bf16[1,2,64,256]{3,2,1,0:T(8,128)(2,1)S(1)}, u32[]{:S(2)}, u32[]{:S(2)}) collective-permute-start(bf16[1,2,64,256]{3,2,1,0:T(8,128)(2,1)S(1)} %collective-permute-done.10.refs_9_), channel_id=1, source_target_pairs={{0,8},{2,10},{4,12},{6,14},{8,0},{10,2},{12,4},{14,6},{16,24},{18,... | collective-permute-start | bytes 196616 | tf_op jit(solution)/shard_map/ppermute | solution.py:32
  14.7 0.0 collective-permute-done.7.refs_6_
  14.7 0.1 collective-permute-start.12
  14.7 1.6 %collective-permute-done.13.refs_7_ = bf16[1,2,64,256]{3,2,1,0:T(8,128)(2,1)S(1)} collective-permute-done((bf16[1,2,64,256]{3,2,1,0:T(8,128)(2,1)S(1)}, bf16[1,2,64,256]{3,2,1,0:T(8,128)(2,1)S(1)}, u32[]{:S(2)}, u32[]{:S(2)}) %collective-permute-start.13) | collective-permute-done | bytes 65568 | tf_op jit(solution)/shard_map/ppermute | solution.py:32
  16.4 0.0 collective-permute-start.14
  16.4 0.0 collective-permute-done.8.refs_7_
  16.4 0.0 collective-permute-done.2.refs_2_
  16.4 1.0 %attend_early.1 = (f32[2,384,128]{2,1,0:T(8,128)S(1)}, f32[2,384,128]{2,1,0:T(8,128)S(1)}, f32[2,384,128]{2,1,0:T(8,128)S(1)}, f32[64,1536]{1,0:T(8,128)S(1)}, f32[1,64]{1,0:T(1,128)S(1)}) custom-call(bf16[2,384,128]{2,1,0:T(8,128)(2,1)S(1)} %get-tuple-element.18.rows_ref, f32[8,1024]{1,0:T(8,128)S(1)} %get-tuple-element.19.bias_ref, ...), custom_call_target="tpu_custom_call" | custom-call | tf_op jit(solution)/shard_map/attend_early/pallas_call | solution.py:259
  17.4 0.0 collective-permute-done.12.refs_6_
  17.4 0.2 collective-permute-done.14.refs_8_
  17.6 1.5 %collective-permute-start.15 = (f32[1,64]{1,0:T(1,128)S(1)}, f32[1,64]{1,0:T(1,128)S(1)}, u32[]{:S(2)}, u32[]{:S(2)}) collective-permute-start(f32[1,64]{1,0:T(1,128)S(1)} %get-tuple-element.28.own_ref), channel_id=1, source_target_pairs={{0,1},{1,0},{2,3},{3,2},{4,5},{5,4},{6,7},{7,6},{8,9},{9,8},{10,11... | collective-permute-start | bytes 776 | tf_op jit(solution)/shard_map/ppermute | solution.py:32
  19.2 2.0 %collective-permute-done.15.other_ref = f32[1,64]{1,0:T(1,128)S(1)} collective-permute-done((f32[1,64]{1,0:T(1,128)S(1)}, f32[1,64]{1,0:T(1,128)S(1)}, u32[]{:S(2)}, u32[]{:S(2)}) %collective-permute-start.15) | collective-permute-done | bytes 288 | tf_op jit(solution)/shard_map/ppermute | solution.py:32
  21.2 0.8 %finish.1 = bf16[1,64,1536]{2,1,0:T(8,128)(2,1)} custom-call(f32[64,1536]{1,0:T(8,128)S(1)} %get-tuple-element.27.attended_ref, f32[1,64]{1,0:T(1,128)S(1)} %get-tuple-element.28.own_ref, f32[1,64]{1,0:T(1,128)S(1)} %collective-permute-done.15.other_ref, f32[8,1536]{1,0:T(8,128)S(1)} %get-tuple-element.29.factor_ref, f32[64,128]{1,0:T(8,128)S(1)} %get-tuple-element.30.live_ref), custom_call_target="tpu_custom_call" | custom-call | tf_op jit(solution)/shard_map/finish/pallas_call | solution.py:269
  (6 shorter events, 0.0 us)
Async XLA Ops:
  0.0 8.8 %collective-permute-start = (bf16[1,2,64,256]{3,2,1,0:T(8,128)(2,1)}, bf16[1,2,64,256]{3,2,1,0:T(8,128)(2,1)S(1)}, u32[]{:S(2)}, u32[]{:S(2)}) collective-permute-start(bf16[1,2,64,256]{3,2,1,0:T(8,128)(2,1)} %bitcast.3), channel_id=1, source_target_pairs={{0,6},{2,4},{4,2},{6,0},{8,14},{10,12},{12,10},{14,8},{16,22},{18,... | collective-permute-start | bytes 196616 | tf_op jit(solution)/shard_map/ppermute | solution.py:32
  5.0 4.6 %collective-permute-start.3 = (bf16[1,2,64,256]{3,2,1,0:T(8,128)(2,1)}, bf16[1,2,64,256]{3,2,1,0:T(8,128)(2,1)S(1)}, u32[]{:S(2)}, u32[]{:S(2)}) collective-permute-start(bf16[1,2,64,256]{3,2,1,0:T(8,128)(2,1)} %bitcast.4), channel_id=1, source_target_pairs={{0,2},{2,0},{4,6},{6,4},{8,10},{10,8},{12,14},{14,12},{16,18},{18,... | collective-permute-start | bytes 196616 | tf_op jit(solution)/shard_map/ppermute | solution.py:32
  5.1 1.3 %copy-start = (bf16[2,1,64,256]{3,2,1,0:T(8,128)(2,1)S(1)}, bf16[2,1,64,256]{3,2,1,0:T(8,128)(2,1)}, u32[]{:S(2)}) copy-start(bf16[2,1,64,256]{3,2,1,0:T(8,128)(2,1)} %param.7) | copy-start | bytes 196612
  6.4 4.7 %collective-permute-start.4 = (bf16[1,2,64,256]{3,2,1,0:T(8,128)(2,1)S(1)}, bf16[1,2,64,256]{3,2,1,0:T(8,128)(2,1)S(1)}, u32[]{:S(2)}, u32[]{:S(2)}) collective-permute-start(bf16[1,2,64,256]{3,2,1,0:T(8,128)(2,1)S(1)} %bitcast.6), channel_id=1, source_target_pairs={{0,8},{2,10},{4,12},{6,14},{8,0},{10,2},{12,4},{14,6},{16,24},{18,... | collective-permute-start | bytes 196616 | tf_op jit(solution)/shard_map/ppermute | solution.py:32
  6.4 5.4 %collective-permute-start.6 = (bf16[1,2,64,256]{3,2,1,0:T(8,128)(2,1)S(1)}, bf16[1,2,64,256]{3,2,1,0:T(8,128)(2,1)S(1)}, u32[]{:S(2)}, u32[]{:S(2)}) collective-permute-start(bf16[1,2,64,256]{3,2,1,0:T(8,128)(2,1)S(1)} %bitcast.7), channel_id=1, source_target_pairs={{0,4},{2,6},{4,0},{6,2},{8,12},{10,14},{12,8},{14,10},{16,20},{18,... | collective-permute-start | bytes 196616 | tf_op jit(solution)/shard_map/ppermute | solution.py:32
  7.1 4.8 %collective-permute-start.1 = (bf16[1,2,64,256]{3,2,1,0:T(8,128)(2,1)S(1)}, bf16[1,2,64,256]{3,2,1,0:T(8,128)(2,1)S(1)}, u32[]{:S(2)}, u32[]{:S(2)}) collective-permute-start(bf16[1,2,64,256]{3,2,1,0:T(8,128)(2,1)S(1)} %bitcast.8), channel_id=1, source_target_pairs={{0,16},{2,18},{4,20},{6,22},{8,24},{10,26},{12,28},{14,30},{16,0},... | collective-permute-start | bytes 196616 | tf_op jit(solution)/shard_map/ppermute | solution.py:32
  8.8 4.9 %collective-permute-start.10 = (bf16[1,2,64,256]{3,2,1,0:T(8,128)(2,1)S(1)}, bf16[1,2,64,256]{3,2,1,0:T(8,128)(2,1)S(1)}, u32[]{:S(2)}, u32[]{:S(2)}) collective-permute-start(bf16[1,2,64,256]{3,2,1,0:T(8,128)(2,1)S(1)} %collective-permute-done.refs_1_), channel_id=1, source_target_pairs={{0,16},{2,18},{4,20},{6,22},{8,24},{10,26},{12,28},{14,30},{16,0},... | collective-permute-start | bytes 196616 | tf_op jit(solution)/shard_map/ppermute | solution.py:32
  9.7 4.5 %collective-permute-start.9 = (bf16[1,2,64,256]{3,2,1,0:T(8,128)(2,1)S(1)}, bf16[1,2,64,256]{3,2,1,0:T(8,128)(2,1)S(1)}, u32[]{:S(2)}, u32[]{:S(2)}) collective-permute-start(bf16[1,2,64,256]{3,2,1,0:T(8,128)(2,1)S(1)} %collective-permute-done.3.refs_3_), channel_id=1, source_target_pairs={{0,16},{2,18},{4,20},{6,22},{8,24},{10,26},{12,28},{14,30},{16,0},... | collective-permute-start | bytes 196616 | tf_op jit(solution)/shard_map/ppermute | solution.py:32
  11.0 3.2 %collective-permute-start.5 = (bf16[1,2,64,256]{3,2,1,0:T(8,128)(2,1)S(1)}, bf16[1,2,64,256]{3,2,1,0:T(8,128)(2,1)S(1)}, u32[]{:S(2)}, u32[]{:S(2)}) collective-permute-start(bf16[1,2,64,256]{3,2,1,0:T(8,128)(2,1)S(1)} %collective-permute-done.3.refs_3_), channel_id=1, source_target_pairs={{0,8},{2,10},{4,12},{6,14},{8,0},{10,2},{12,4},{14,6},{16,24},{18,... | collective-permute-start | bytes 196616 | tf_op jit(solution)/shard_map/ppermute | solution.py:32
  11.8 2.8 %collective-permute-start.7 = (bf16[1,2,64,256]{3,2,1,0:T(8,128)(2,1)S(1)}, bf16[1,2,64,256]{3,2,1,0:T(8,128)(2,1)S(1)}, u32[]{:S(2)}, u32[]{:S(2)}) collective-permute-start(bf16[1,2,64,256]{3,2,1,0:T(8,128)(2,1)S(1)} %collective-permute-done.6.refs_10_), channel_id=1, source_target_pairs={{0,8},{2,10},{4,12},{6,14},{8,0},{10,2},{12,4},{14,6},{16,24},{18,... | collective-permute-start | bytes 196616 | tf_op jit(solution)/shard_map/ppermute | solution.py:32
  11.8 4.5 %collective-permute-start.13 = (bf16[1,2,64,256]{3,2,1,0:T(8,128)(2,1)S(1)}, bf16[1,2,64,256]{3,2,1,0:T(8,128)(2,1)S(1)}, u32[]{:S(2)}, u32[]{:S(2)}) collective-permute-start(bf16[1,2,64,256]{3,2,1,0:T(8,128)(2,1)S(1)} %collective-permute-done.6.refs_10_), channel_id=1, source_target_pairs={{0,16},{2,18},{4,20},{6,22},{8,24},{10,26},{12,28},{14,30},{16,0},... | collective-permute-start | bytes 196616 | tf_op jit(solution)/shard_map/ppermute | solution.py:32
  13.7 2.6 %collective-permute-start.8 = (bf16[1,2,64,256]{3,2,1,0:T(8,128)(2,1)S(1)}, bf16[1,2,64,256]{3,2,1,0:T(8,128)(2,1)S(1)}, u32[]{:S(2)}, u32[]{:S(2)}) collective-permute-start(bf16[1,2,64,256]{3,2,1,0:T(8,128)(2,1)S(1)} %collective-permute-done.refs_1_), channel_id=1, source_target_pairs={{0,8},{2,10},{4,12},{6,14},{8,0},{10,2},{12,4},{14,6},{16,24},{18,... | collective-permute-start | bytes 196616 | tf_op jit(solution)/shard_map/ppermute | solution.py:32
  14.1 2.2 %collective-permute-start.2 = (bf16[1,2,64,256]{3,2,1,0:T(8,128)(2,1)S(1)}, bf16[1,2,64,256]{3,2,1,0:T(8,128)(2,1)S(1)}, u32[]{:S(2)}, u32[]{:S(2)}) collective-permute-start(bf16[1,2,64,256]{3,2,1,0:T(8,128)(2,1)S(1)} %collective-permute-done.1.refs_5_), channel_id=1, source_target_pairs={{0,8},{2,10},{4,12},{6,14},{8,0},{10,2},{12,4},{14,6},{16,24},{18,... | collective-permute-start | bytes 196616 | tf_op jit(solution)/shard_map/ppermute | solution.py:32
  14.2 2.1 %collective-permute-start.11 = (bf16[1,2,64,256]{3,2,1,0:T(8,128)(2,1)S(1)}, bf16[1,2,64,256]{3,2,1,0:T(8,128)(2,1)S(1)}, u32[]{:S(2)}, u32[]{:S(2)}) collective-permute-start(bf16[1,2,64,256]{3,2,1,0:T(8,128)(2,1)S(1)} %collective-permute-done.10.refs_9_), channel_id=1, source_target_pairs={{0,8},{2,10},{4,12},{6,14},{8,0},{10,2},{12,4},{14,6},{16,24},{18,... | collective-permute-start | bytes 196616 | tf_op jit(solution)/shard_map/ppermute | solution.py:32
  14.7 2.7 %collective-permute-start.12 = (bf16[1,2,64,256]{3,2,1,0:T(8,128)(2,1)S(1)}, bf16[1,2,64,256]{3,2,1,0:T(8,128)(2,1)S(1)}, u32[]{:S(2)}, u32[]{:S(2)}) collective-permute-start(bf16[1,2,64,256]{3,2,1,0:T(8,128)(2,1)S(1)} %collective-permute-done.9.refs_8_), channel_id=1, source_target_pairs={{0,8},{2,10},{4,12},{6,14},{8,0},{10,2},{12,4},{14,6},{16,24},{18,... | collective-permute-start | bytes 196616 | tf_op jit(solution)/shard_map/ppermute | solution.py:32
  16.4 1.3 %collective-permute-start.14 = (bf16[1,2,64,256]{3,2,1,0:T(8,128)(2,1)S(1)}, bf16[1,2,64,256]{3,2,1,0:T(8,128)(2,1)S(1)}, u32[]{:S(2)}, u32[]{:S(2)}) collective-permute-start(bf16[1,2,64,256]{3,2,1,0:T(8,128)(2,1)S(1)} %collective-permute-done.13.refs_7_), channel_id=1, source_target_pairs={{0,8},{2,10},{4,12},{6,14},{8,0},{10,2},{12,4},{14,6},{16,24},{18,... | collective-permute-start | bytes 196616 | tf_op jit(solution)/shard_map/ppermute | solution.py:32
  17.6 3.6 %collective-permute-start.15 = (f32[1,64]{1,0:T(1,128)S(1)}, f32[1,64]{1,0:T(1,128)S(1)}, u32[]{:S(2)}, u32[]{:S(2)}) collective-permute-start(f32[1,64]{1,0:T(1,128)S(1)} %get-tuple-element.28.own_ref), channel_id=1, source_target_pairs={{0,1},{1,0},{2,3},{3,2},{4,5},{5,4},{6,7},{7,6},{8,9},{9,8},{10,11... | collective-permute-start | bytes 776 | tf_op jit(solution)/shard_map/ppermute | solution.py:32

commit v6 on v5

--- a/solution.py
+++ b/solution.py
@@ -178,15 +178,20 @@
     pl.when(on_upper(True))(end)
 
 
-def finish_kernel(features, attended_ref, own_ref, other_ref, factor_ref, live_ref, out_ref):
-    rows = attended_ref.shape[0]
-    mean_square = (own_ref[...] + other_ref[...]) / features
-    scale = jnp.broadcast_to(lax.rsqrt(mean_square + 1e-06), (HD, rows)).T
+def gain_kernel(attended_ref, factor_ref, live_ref, out_ref):
     live = live_ref[...] > 0.0
     for h in range(attended_ref.shape[1] // HD):
         lanes = slice(h * HD, (h + 1) * HD)
-        block = attended_ref[:, lanes] * scale * factor_ref[0:1, lanes]
-        out_ref[0, :, lanes] = jnp.where(live, block, 0.0).astype(out_ref.dtype)
+        out_ref[:, lanes] = jnp.where(live, attended_ref[:, lanes] * factor_ref[0:1, lanes], 0.0)
+
+
+def finish_kernel(features, gained_ref, own_ref, other_ref, out_ref):
+    rows = gained_ref.shape[0]
+    mean_square = (own_ref[...] + other_ref[...]) / features
+    scale = jnp.broadcast_to(lax.rsqrt(mean_square + 1e-06), (HD, rows)).T
+    for h in range(gained_ref.shape[1] // HD):
+        lanes = slice(h * HD, (h + 1) * HD)
+        out_ref[0, :, lanes] = (gained_ref[:, lanes] * scale).astype(out_ref.dtype)
 
 
 def kernel(body, outs, count, megabytes, name, in_place={}):
@@ -266,11 +271,12 @@
         late_kernel, ends, 7 + len(late), 16, "attend_late", in_place={5: 0, 6: 1}
     )(rows, bias, *state, attended, squares, *[have[name] for name in late])
     others = [exchanged(squares, ("mp",), (by,)) for by in range(1, lax.axis_size("mp"))]
+    gained = kernel(gain_kernel, ends[0], 3, 4, "gain")(attended, factor, live)
     return kernel(
         functools.partial(finish_kernel, width * lax.axis_size("mp")),
         jax.ShapeDtypeStruct(queries.shape, queries.dtype),
-        5, 4, "finish",
-    )(attended, squares, sum(others), factor, live)
+        3, 4, "finish",
+    )(gained, squares, sum(others))
 
 
 def passed_along(shard, axis, by):

time: 22.1 us -> 22.1 us (level)
  transfers between devices with their start and end apart: 16 -> 16, of which waited for: 5 -> 5; matrix products, arithmetic and copies ran while one was open for 0% -> 0% of each run, Pallas kernels for 10% -> 11%
where the time goes in v6:
time: 22.1 us; the launch traced here: 22 us
  starting transfers between devices  13.7 us (62%)
  waiting for transfers between devices  5.07 us (23%)
  Pallas kernels  3.1 us (14%)
    ppermute x16, starting transfers between devices, exchanged(): lax.ppermute(shard, axes, [(i, places.index(there)) for i, there in enume...  13.7 us
    ppermute x16, waiting for transfers between devices, exchanged(): lax.ppermute(shard, axes, [(i, places.index(there)) for i, there in enume...  5.07 us
    pallas_call x1, Pallas kernels, by_exchange(): pl.pallas_call(functools.partial(prepare_kernel, offsets, len(outs)), out...  1.28 us
    pallas_call x1, Pallas kernels, by_exchange(): kernel(functools.partial(early_kernel, early_at), (f32(stacked),) * 3 + e...  1 us
    pallas_call x1, Pallas kernels, by_exchange(): kernel(functools.partial(finish_kernel, width * lax.axis_size('mp')), jax...  0.79 us
  transfers between devices with their start and end apart: 16, of which 5 were waited for; matrix products, arithmetic and copies ran while one was open for 0% of the time, Pallas kernels for 11%

profile of v6, /device:TPU:0, one launch (start us, length us, event | category | flops | bytes accessed | tf_op | source)
XLA Modules:
  0.0 22.0 jit_solution(2701846278590595901)
XLA Ops:
  0.0 5.0 %collective-permute-start = (bf16[1,2,64,256]{3,2,1,0:T(8,128)(2,1)}, bf16[1,2,64,256]{3,2,1,0:T(8,128)(2,1)S(1)}, u32[]{:S(2)}, u32[]{:S(2)}) collective-permute-start(bf16[1,2,64,256]{3,2,1,0:T(8,128)(2,1)} %bitcast.3), channel_id=1, source_target_pairs={{0,6},{2,4},{4,2},{6,0},{8,14},{10,12},{12,10},{14,8},{16,22},{18,... | collective-permute-start | bytes 196616 | tf_op jit(solution)/shard_map/ppermute | solution.py:32
  5.0 0.0 collective-permute-start.3
  5.1 1.3 %prepare.1 = (bf16[2,384,128]{2,1,0:T(8,128)(2,1)S(1)}, bf16[1,2,64,256]{3,2,1,0:T(8,128)(2,1)S(1)}, f32[8,1536]{1,0:T(8,128)S(1)}, f32[8,1024]{1,0:T(8,128)S(1)}, f32[64,128]{1,0:T(8,128)S(1)}) custom-call(bf16[64,1536]{1,0:T(8,128)(2,1)} %bitcast.2, bf16[64,1536]{1,0:T(8,128)(2,1)} %refs_1_.1, bf16[1536]{0:T(1024)(128)(2,1)} %refs_2_.1, s32[4]{0:T(128)} %refs_3_.1, ...), custom_call_target="tpu_custom_call" | custom-call | tf_op jit(solution)/shard_map/prepare/pallas_call | solution.py:252
  6.4 0.1 collective-permute-start.4
  6.4 0.6 %collective-permute-start.6 = (bf16[1,2,64,256]{3,2,1,0:T(8,128)(2,1)S(1)}, bf16[1,2,64,256]{3,2,1,0:T(8,128)(2,1)S(1)}, u32[]{:S(2)}, u32[]{:S(2)}) collective-permute-start(bf16[1,2,64,256]{3,2,1,0:T(8,128)(2,1)S(1)} %bitcast.7), channel_id=1, source_target_pairs={{0,4},{2,6},{4,0},{6,2},{8,12},{10,14},{12,8},{14,10},{16,20},{18,... | collective-permute-start | bytes 196616 | tf_op jit(solution)/shard_map/ppermute | solution.py:32
  7.1 1.7 %collective-permute-start.1 = (bf16[1,2,64,256]{3,2,1,0:T(8,128)(2,1)S(1)}, bf16[1,2,64,256]{3,2,1,0:T(8,128)(2,1)S(1)}, u32[]{:S(2)}, u32[]{:S(2)}) collective-permute-start(bf16[1,2,64,256]{3,2,1,0:T(8,128)(2,1)S(1)} %bitcast.8), channel_id=1, source_target_pairs={{0,16},{2,18},{4,20},{6,22},{8,24},{10,26},{12,28},{14,30},{16,0},... | collective-permute-start | bytes 196616 | tf_op jit(solution)/shard_map/ppermute | solution.py:32
  8.8 0.0 collective-permute-done.refs_1_
  8.8 0.9 %collective-permute-start.10 = (bf16[1,2,64,256]{3,2,1,0:T(8,128)(2,1)S(1)}, bf16[1,2,64,256]{3,2,1,0:T(8,128)(2,1)S(1)}, u32[]{:S(2)}, u32[]{:S(2)}) collective-permute-start(bf16[1,2,64,256]{3,2,1,0:T(8,128)(2,1)S(1)} %collective-permute-done.refs_1_), channel_id=1, source_target_pairs={{0,16},{2,18},{4,20},{6,22},{8,24},{10,26},{12,28},{14,30},{16,0},... | collective-permute-start | bytes 196616 | tf_op jit(solution)/shard_map/ppermute | solution.py:32
  9.7 0.0 collective-permute-done.3.refs_3_
  9.7 1.4 %collective-permute-start.9 = (bf16[1,2,64,256]{3,2,1,0:T(8,128)(2,1)S(1)}, bf16[1,2,64,256]{3,2,1,0:T(8,128)(2,1)S(1)}, u32[]{:S(2)}, u32[]{:S(2)}) collective-permute-start(bf16[1,2,64,256]{3,2,1,0:T(8,128)(2,1)S(1)} %collective-permute-done.3.refs_3_), channel_id=1, source_target_pairs={{0,16},{2,18},{4,20},{6,22},{8,24},{10,26},{12,28},{14,30},{16,0},... | collective-permute-start | bytes 196616 | tf_op jit(solution)/shard_map/ppermute | solution.py:32
  11.0 0.0 collective-permute-done.4.refs_4_
  11.0 0.0 collective-permute-start.5
  11.0 0.8 %collective-permute-done.6.refs_10_ = bf16[1,2,64,256]{3,2,1,0:T(8,128)(2,1)S(1)} collective-permute-done((bf16[1,2,64,256]{3,2,1,0:T(8,128)(2,1)S(1)}, bf16[1,2,64,256]{3,2,1,0:T(8,128)(2,1)S(1)}, u32[]{:S(2)}, u32[]{:S(2)}) %collective-permute-start.6) | collective-permute-done | bytes 65568 | tf_op jit(solution)/shard_map/ppermute | solution.py:32
  11.8 1.9 %collective-permute-start.13 = (bf16[1,2,64,256]{3,2,1,0:T(8,128)(2,1)S(1)}, bf16[1,2,64,256]{3,2,1,0:T(8,128)(2,1)S(1)}, u32[]{:S(2)}, u32[]{:S(2)}) collective-permute-start(bf16[1,2,64,256]{3,2,1,0:T(8,128)(2,1)S(1)} %collective-permute-done.6.refs_10_), channel_id=1, source_target_pairs={{0,16},{2,18},{4,20},{6,22},{8,24},{10,26},{12,28},{14,30},{16,0},... | collective-permute-start | bytes 196616 | tf_op jit(solution)/shard_map/ppermute | solution.py:32
  13.7 0.0 collective-permute-done.10.refs_9_
  13.7 0.0 collective-permute-start.8
  13.7 0.4 %collective-permute-done.9.refs_8_ = bf16[1,2,64,256]{3,2,1,0:T(8,128)(2,1)S(1)} collective-permute-done((bf16[1,2,64,256]{3,2,1,0:T(8,128)(2,1)S(1)}, bf16[1,2,64,256]{3,2,1,0:T(8,128)(2,1)S(1)}, u32[]{:S(2)}, u32[]{:S(2)}) %collective-permute-start.9) | collective-permute-done | bytes 65568 | tf_op jit(solution)/shard_map/ppermute | solution.py:32
  14.1 0.1 collective-permute-start.2
  14.2 0.0 collective-permute-done.5.refs_5_
  14.2 0.4 %collective-permute-start.11 = (bf16[1,2,64,256]{3,2,1,0:T(8,128)(2,1)S(1)}, bf16[1,2,64,256]{3,2,1,0:T(8,128)(2,1)S(1)}, u32[]{:S(2)}, u32[]{:S(2)}) collective-permute-start(bf16[1,2,64,256]{3,2,1,0:T(8,128)(2,1)S(1)} %collective-permute-done.10.refs_9_), channel_id=1, source_target_pairs={{0,8},{2,10},{4,12},{6,14},{8,0},{10,2},{12,4},{14,6},{16,24},{18,... | collective-permute-start | bytes 196616 | tf_op jit(solution)/shard_map/ppermute | solution.py:32
  14.7 0.0 collective-permute-done.7.refs_6_
  14.7 0.1 collective-permute-start.12
  14.7 1.6 %collective-permute-done.13.refs_7_ = bf16[1,2,64,256]{3,2,1,0:T(8,128)(2,1)S(1)} collective-permute-done((bf16[1,2,64,256]{3,2,1,0:T(8,128)(2,1)S(1)}, bf16[1,2,64,256]{3,2,1,0:T(8,128)(2,1)S(1)}, u32[]{:S(2)}, u32[]{:S(2)}) %collective-permute-start.13) | collective-permute-done | bytes 65568 | tf_op jit(solution)/shard_map/ppermute | solution.py:32
  16.4 0.0 collective-permute-start.14
  16.4 0.0 collective-permute-done.8.refs_7_
  16.4 0.0 collective-permute-done.2.refs_2_
  16.4 1.0 %attend_early.1 = (f32[2,384,128]{2,1,0:T(8,128)S(1)}, f32[2,384,128]{2,1,0:T(8,128)S(1)}, f32[2,384,128]{2,1,0:T(8,128)S(1)}, f32[64,1536]{1,0:T(8,128)S(1)}, f32[1,64]{1,0:T(1,128)S(1)}) custom-call(bf16[2,384,128]{2,1,0:T(8,128)(2,1)S(1)} %get-tuple-element.18.rows_ref, f32[8,1024]{1,0:T(8,128)S(1)} %get-tuple-element.19.bias_ref, ...), custom_call_target="tpu_custom_call" | custom-call | tf_op jit(solution)/shard_map/attend_early/pallas_call | solution.py:264
  17.4 0.0 collective-permute-done.12.refs_6_
  17.4 0.2 collective-permute-done.14.refs_8_
  17.6 1.5 %collective-permute-start.15 = (f32[1,64]{1,0:T(1,128)S(1)}, f32[1,64]{1,0:T(1,128)S(1)}, u32[]{:S(2)}, u32[]{:S(2)}) collective-permute-start(f32[1,64]{1,0:T(1,128)S(1)} %get-tuple-element.30.own_ref), channel_id=1, source_target_pairs={{0,1},{1,0},{2,3},{3,2},{4,5},{5,4},{6,7},{7,6},{8,9},{9,8},{10,11... | collective-permute-start | bytes 776 | tf_op jit(solution)/shard_map/ppermute | solution.py:32
  19.2 2.0 %collective-permute-done.15.other_ref = f32[1,64]{1,0:T(1,128)S(1)} collective-permute-done((f32[1,64]{1,0:T(1,128)S(1)}, f32[1,64]{1,0:T(1,128)S(1)}, u32[]{:S(2)}, u32[]{:S(2)}) %collective-permute-start.15) | collective-permute-done | bytes 288 | tf_op jit(solution)/shard_map/ppermute | solution.py:32
  21.2 0.8 %finish.1 = bf16[1,64,1536]{2,1,0:T(8,128)(2,1)} custom-call(f32[64,1536]{1,0:T(8,128)S(1)} %gain.1.gained_ref, f32[1,64]{1,0:T(1,128)S(1)} %get-tuple-element.30.own_ref, f32[1,64]{1,0:T(1,128)S(1)} %collective-permute-done.15.other_ref), custom_call_target="tpu_custom_call" | custom-call | tf_op jit(solution)/shard_map/finish/pallas_call | solution.py:275
  (7 shorter events, 0.0 us)
Async XLA Ops:
  0.0 8.8 %collective-permute-start = (bf16[1,2,64,256]{3,2,1,0:T(8,128)(2,1)}, bf16[1,2,64,256]{3,2,1,0:T(8,128)(2,1)S(1)}, u32[]{:S(2)}, u32[]{:S(2)}) collective-permute-start(bf16[1,2,64,256]{3,2,1,0:T(8,128)(2,1)} %bitcast.3), channel_id=1, source_target_pairs={{0,6},{2,4},{4,2},{6,0},{8,14},{10,12},{12,10},{14,8},{16,22},{18,... | collective-permute-start | bytes 196616 | tf_op jit(solution)/shard_map/ppermute | solution.py:32
  5.0 4.6 %collective-permute-start.3 = (bf16[1,2,64,256]{3,2,1,0:T(8,128)(2,1)}, bf16[1,2,64,256]{3,2,1,0:T(8,128)(2,1)S(1)}, u32[]{:S(2)}, u32[]{:S(2)}) collective-permute-start(bf16[1,2,64,256]{3,2,1,0:T(8,128)(2,1)} %bitcast.4), channel_id=1, source_target_pairs={{0,2},{2,0},{4,6},{6,4},{8,10},{10,8},{12,14},{14,12},{16,18},{18,... | collective-permute-start | bytes 196616 | tf_op jit(solution)/shard_map/ppermute | solution.py:32
  5.1 1.3 %copy-start = (bf16[2,1,64,256]{3,2,1,0:T(8,128)(2,1)S(1)}, bf16[2,1,64,256]{3,2,1,0:T(8,128)(2,1)}, u32[]{:S(2)}) copy-start(bf16[2,1,64,256]{3,2,1,0:T(8,128)(2,1)} %param.7) | copy-start | bytes 196612
  6.4 4.7 %collective-permute-start.4 = (bf16[1,2,64,256]{3,2,1,0:T(8,128)(2,1)S(1)}, bf16[1,2,64,256]{3,2,1,0:T(8,128)(2,1)S(1)}, u32[]{:S(2)}, u32[]{:S(2)}) collective-permute-start(bf16[1,2,64,256]{3,2,1,0:T(8,128)(2,1)S(1)} %bitcast.6), channel_id=1, source_target_pairs={{0,8},{2,10},{4,12},{6,14},{8,0},{10,2},{12,4},{14,6},{16,24},{18,... | collective-permute-start | bytes 196616 | tf_op jit(solution)/shard_map/ppermute | solution.py:32
  6.4 5.4 %collective-permute-start.6 = (bf16[1,2,64,256]{3,2,1,0:T(8,128)(2,1)S(1)}, bf16[1,2,64,256]{3,2,1,0:T(8,128)(2,1)S(1)}, u32[]{:S(2)}, u32[]{:S(2)}) collective-permute-start(bf16[1,2,64,256]{3,2,1,0:T(8,128)(2,1)S(1)} %bitcast.7), channel_id=1, source_target_pairs={{0,4},{2,6},{4,0},{6,2},{8,12},{10,14},{12,8},{14,10},{16,20},{18,... | collective-permute-start | bytes 196616 | tf_op jit(solution)/shard_map/ppermute | solution.py:32
  7.1 4.8 %collective-permute-start.1 = (bf16[1,2,64,256]{3,2,1,0:T(8,128)(2,1)S(1)}, bf16[1,2,64,256]{3,2,1,0:T(8,128)(2,1)S(1)}, u32[]{:S(2)}, u32[]{:S(2)}) collective-permute-start(bf16[1,2,64,256]{3,2,1,0:T(8,128)(2,1)S(1)} %bitcast.8), channel_id=1, source_target_pairs={{0,16},{2,18},{4,20},{6,22},{8,24},{10,26},{12,28},{14,30},{16,0},... | collective-permute-start | bytes 196616 | tf_op jit(solution)/shard_map/ppermute | solution.py:32
  8.8 4.9 %collective-permute-start.10 = (bf16[1,2,64,256]{3,2,1,0:T(8,128)(2,1)S(1)}, bf16[1,2,64,256]{3,2,1,0:T(8,128)(2,1)S(1)}, u32[]{:S(2)}, u32[]{:S(2)}) collective-permute-start(bf16[1,2,64,256]{3,2,1,0:T(8,128)(2,1)S(1)} %collective-permute-done.refs_1_), channel_id=1, source_target_pairs={{0,16},{2,18},{4,20},{6,22},{8,24},{10,26},{12,28},{14,30},{16,0},... | collective-permute-start | bytes 196616 | tf_op jit(solution)/shard_map/ppermute | solution.py:32
  9.7 4.5 %collective-permute-start.9 = (bf16[1,2,64,256]{3,2,1,0:T(8,128)(2,1)S(1)}, bf16[1,2,64,256]{3,2,1,0:T(8,128)(2,1)S(1)}, u32[]{:S(2)}, u32[]{:S(2)}) collective-permute-start(bf16[1,2,64,256]{3,2,1,0:T(8,128)(2,1)S(1)} %collective-permute-done.3.refs_3_), channel_id=1, source_target_pairs={{0,16},{2,18},{4,20},{6,22},{8,24},{10,26},{12,28},{14,30},{16,0},... | collective-permute-start | bytes 196616 | tf_op jit(solution)/shard_map/ppermute | solution.py:32
  11.0 3.2 %collective-permute-start.5 = (bf16[1,2,64,256]{3,2,1,0:T(8,128)(2,1)S(1)}, bf16[1,2,64,256]{3,2,1,0:T(8,128)(2,1)S(1)}, u32[]{:S(2)}, u32[]{:S(2)}) collective-permute-start(bf16[1,2,64,256]{3,2,1,0:T(8,128)(2,1)S(1)} %collective-permute-done.3.refs_3_), channel_id=1, source_target_pairs={{0,8},{2,10},{4,12},{6,14},{8,0},{10,2},{12,4},{14,6},{16,24},{18,... | collective-permute-start | bytes 196616 | tf_op jit(solution)/shard_map/ppermute | solution.py:32
  11.8 2.8 %collective-permute-start.7 = (bf16[1,2,64,256]{3,2,1,0:T(8,128)(2,1)S(1)}, bf16[1,2,64,256]{3,2,1,0:T(8,128)(2,1)S(1)}, u32[]{:S(2)}, u32[]{:S(2)}) collective-permute-start(bf16[1,2,64,256]{3,2,1,0:T(8,128)(2,1)S(1)} %collective-permute-done.6.refs_10_), channel_id=1, source_target_pairs={{0,8},{2,10},{4,12},{6,14},{8,0},{10,2},{12,4},{14,6},{16,24},{18,... | collective-permute-start | bytes 196616 | tf_op jit(solution)/shard_map/ppermute | solution.py:32
  11.8 4.5 %collective-permute-start.13 = (bf16[1,2,64,256]{3,2,1,0:T(8,128)(2,1)S(1)}, bf16[1,2,64,256]{3,2,1,0:T(8,128)(2,1)S(1)}, u32[]{:S(2)}, u32[]{:S(2)}) collective-permute-start(bf16[1,2,64,256]{3,2,1,0:T(8,128)(2,1)S(1)} %collective-permute-done.6.refs_10_), channel_id=1, source_target_pairs={{0,16},{2,18},{4,20},{6,22},{8,24},{10,26},{12,28},{14,30},{16,0},... | collective-permute-start | bytes 196616 | tf_op jit(solution)/shard_map/ppermute | solution.py:32
  13.7 2.6 %collective-permute-start.8 = (bf16[1,2,64,256]{3,2,1,0:T(8,128)(2,1)S(1)}, bf16[1,2,64,256]{3,2,1,0:T(8,128)(2,1)S(1)}, u32[]{:S(2)}, u32[]{:S(2)}) collective-permute-start(bf16[1,2,64,256]{3,2,1,0:T(8,128)(2,1)S(1)} %collective-permute-done.refs_1_), channel_id=1, source_target_pairs={{0,8},{2,10},{4,12},{6,14},{8,0},{10,2},{12,4},{14,6},{16,24},{18,... | collective-permute-start | bytes 196616 | tf_op jit(solution)/shard_map/ppermute | solution.py:32
  14.1 2.2 %collective-permute-start.2 = (bf16[1,2,64,256]{3,2,1,0:T(8,128)(2,1)S(1)}, bf16[1,2,64,256]{3,2,1,0:T(8,128)(2,1)S(1)}, u32[]{:S(2)}, u32[]{:S(2)}) collective-permute-start(bf16[1,2,64,256]{3,2,1,0:T(8,128)(2,1)S(1)} %collective-permute-done.1.refs_5_), channel_id=1, source_target_pairs={{0,8},{2,10},{4,12},{6,14},{8,0},{10,2},{12,4},{14,6},{16,24},{18,... | collective-permute-start | bytes 196616 | tf_op jit(solution)/shard_map/ppermute | solution.py:32
  14.2 2.1 %collective-permute-start.11 = (bf16[1,2,64,256]{3,2,1,0:T(8,128)(2,1)S(1)}, bf16[1,2,64,256]{3,2,1,0:T(8,128)(2,1)S(1)}, u32[]{:S(2)}, u32[]{:S(2)}) collective-permute-start(bf16[1,2,64,256]{3,2,1,0:T(8,128)(2,1)S(1)} %collective-permute-done.10.refs_9_), channel_id=1, source_target_pairs={{0,8},{2,10},{4,12},{6,14},{8,0},{10,2},{12,4},{14,6},{16,24},{18,... | collective-permute-start | bytes 196616 | tf_op jit(solution)/shard_map/ppermute | solution.py:32
  14.7 2.7 %collective-permute-start.12 = (bf16[1,2,64,256]{3,2,1,0:T(8,128)(2,1)S(1)}, bf16[1,2,64,256]{3,2,1,0:T(8,128)(2,1)S(1)}, u32[]{:S(2)}, u32[]{:S(2)}) collective-permute-start(bf16[1,2,64,256]{3,2,1,0:T(8,128)(2,1)S(1)} %collective-permute-done.9.refs_8_), channel_id=1, source_target_pairs={{0,8},{2,10},{4,12},{6,14},{8,0},{10,2},{12,4},{14,6},{16,24},{18,... | collective-permute-start | bytes 196616 | tf_op jit(solution)/shard_map/ppermute | solution.py:32
  16.4 1.3 %collective-permute-start.14 = (bf16[1,2,64,256]{3,2,1,0:T(8,128)(2,1)S(1)}, bf16[1,2,64,256]{3,2,1,0:T(8,128)(2,1)S(1)}, u32[]{:S(2)}, u32[]{:S(2)}) collective-permute-start(bf16[1,2,64,256]{3,2,1,0:T(8,128)(2,1)S(1)} %collective-permute-done.13.refs_7_), channel_id=1, source_target_pairs={{0,8},{2,10},{4,12},{6,14},{8,0},{10,2},{12,4},{14,6},{16,24},{18,... | collective-permute-start | bytes 196616 | tf_op jit(solution)/shard_map/ppermute | solution.py:32
  17.6 3.6 %collective-permute-start.15 = (f32[1,64]{1,0:T(1,128)S(1)}, f32[1,64]{1,0:T(1,128)S(1)}, u32[]{:S(2)}, u32[]{:S(2)}) collective-permute-start(f32[1,64]{1,0:T(1,128)S(1)} %get-tuple-element.30.own_ref), channel_id=1, source_target_pairs={{0,1},{1,0},{2,3},{3,2},{4,5},{5,4},{6,7},{7,6},{8,9},{9,8},{10,11... | collective-permute-start | bytes 776 | tf_op jit(solution)/shard_map/ppermute | solution.py:32

commit v7 on v6

--- a/solution.py
+++ b/solution.py
@@ -108,14 +108,12 @@
     return new_max, weight_sums, mixed
 
 
-def on_upper(upper):
-    across = lax.axis_size("span") // 2
-    return (lax.axis_index("span") >= across) == upper
-
-
-def usable_on_lower(offsets):
-    across = lax.axis_size("span") // 2
-    chosen = [i for i, (by, _) in enumerate(offsets) if by < across]
+def on_upper():
+    return lax.axis_index("span") >= lax.axis_size("span") // 2
+
+
+def usable_below(clips, offsets):
+    chosen = [i for i, (by, _) in enumerate(offsets) if by < clips]
     others = [i for i in range(len(offsets)) if i not in chosen]
     return sorted(chosen + others[: len(chosen) % 2])
 
@@ -157,8 +155,12 @@
         if is_all:
             squares_ref[...] = jnp.sum(sum(squares).T, axis=0, keepdims=True)
 
-    pl.when(on_upper(True))(lambda: fold_in(range(len(kv_refs)), False))
-    pl.when(on_upper(False))(lambda: fold_in(usable_on_lower(offsets), True))
+    pl.when(on_upper())(lambda: fold_in(range(len(kv_refs)), False))
+    across = lax.axis_size("span") // 2
+    own_clip = lax.axis_index("span")
+    middle = jnp.logical_and(own_clip >= 1, own_clip < across)
+    pl.when(middle)(lambda: fold_in(usable_below(across, offsets), True))
+    pl.when(own_clip == 0)(lambda: fold_in(usable_below(1, offsets), True))
 
 
 def late_kernel(rows_ref, bias_ref, *refs):
@@ -175,7 +177,7 @@
             squares.append(put_attended(attended_ref, g, state))
         squares_ref[...] = jnp.sum(sum(squares).T, axis=0, keepdims=True)
 
-    pl.when(on_upper(True))(end)
+    pl.when(on_upper())(end)
 
 
 def gain_kernel(attended_ref, factor_ref, live_ref, out_ref):
@@ -266,7 +268,7 @@
         (f32(stacked),) * 3 + ends,
         2 + len(early), 16, "attend_early",
     )(rows, bias, *[have[name] for name in early])
-    assert not usable_on_lower(late_at)
+    assert not usable_below(lax.axis_size("span") // 2, late_at)
     attended, squares = kernel(
         late_kernel, ends, 7 + len(late), 16, "attend_late", in_place={5: 0, 6: 1}
     )(rows, bias, *state, attended, squares, *[have[name] for name in late])

time: 22.1 us -> 22.1 us (level)
  waiting for transfers between devices: 5.07 us -> 5.4 us
  Pallas kernels: 3.1 us -> 2.78 us
    pallas_call x1, Pallas kernels: 1 us -> 0.68 us  [by_exchange(): kernel(functools.partial(early_kernel, early_at), (f32(stacked),) * 3 + e...]
    ppermute x16, waiting for transfers between devices: 5.07 us -> 5.4 us  [exchanged(): lax.ppermute(shard, axes, [(i, places.index(there)) for i, there in enume...]
  transfers between devices with their start and end apart: 16 -> 16, of which waited for: 5 -> 5; matrix products, arithmetic and copies ran while one was open for 0% -> 0% of each run, Pallas kernels for 11% -> 9%
where the time goes in v7:
time: 22.1 us; the launch traced here: 22 us
  starting transfers between devices  13.7 us (62%)
  waiting for transfers between devices  5.4 us (24%)
  Pallas kernels  2.78 us (13%)
    ppermute x16, starting transfers between devices, exchanged(): lax.ppermute(shard, axes, [(i, places.index(there)) for i, there in enume...  13.7 us
    ppermute x16, waiting for transfers between devices, exchanged(): lax.ppermute(shard, axes, [(i, places.index(there)) for i, there in enume...  5.4 us
    pallas_call x1, Pallas kernels, by_exchange(): pl.pallas_call(functools.partial(prepare_kernel, offsets, len(outs)), out...  1.28 us
    pallas_call x1, Pallas kernels, by_exchange(): kernel(functools.partial(finish_kernel, width * lax.axis_size('mp')), jax...  0.79 us
    pallas_call x1, Pallas kernels, by_exchange(): kernel(functools.partial(early_kernel, early_at), (f32(stacked),) * 3 + e...  0.68 us
  transfers between devices with their start and end apart: 16, of which 5 were waited for; matrix products, arithmetic and copies ran while one was open for 0% of the time, Pallas kernels for 9%

profile of v7, /device:TPU:0, one launch (start us, length us, event | category | flops | bytes accessed | tf_op | source)
XLA Modules:
  0.0 22.0 jit_solution(7926916808433223810)
XLA Ops:
  0.0 5.0 %collective-permute-start = (bf16[1,2,64,256]{3,2,1,0:T(8,128)(2,1)}, bf16[1,2,64,256]{3,2,1,0:T(8,128)(2,1)S(1)}, u32[]{:S(2)}, u32[]{:S(2)}) collective-permute-start(bf16[1,2,64,256]{3,2,1,0:T(8,128)(2,1)} %bitcast.3), channel_id=1, source_target_pairs={{0,6},{2,4},{4,2},{6,0},{8,14},{10,12},{12,10},{14,8},{16,22},{18,... | collective-permute-start | bytes 196616 | tf_op jit(solution)/shard_map/ppermute | solution.py:32
  5.0 0.0 collective-permute-start.3
  5.1 1.3 %prepare.1 = (bf16[2,384,128]{2,1,0:T(8,128)(2,1)S(1)}, bf16[1,2,64,256]{3,2,1,0:T(8,128)(2,1)S(1)}, f32[8,1536]{1,0:T(8,128)S(1)}, f32[8,1024]{1,0:T(8,128)S(1)}, f32[64,128]{1,0:T(8,128)S(1)}) custom-call(bf16[64,1536]{1,0:T(8,128)(2,1)} %bitcast.2, bf16[64,1536]{1,0:T(8,128)(2,1)} %refs_1_.1, bf16[1536]{0:T(1024)(128)(2,1)} %refs_2_.1, s32[4]{0:T(128)} %refs_3_.1, ...), custom_call_target="tpu_custom_call" | custom-call | tf_op jit(solution)/shard_map/prepare/pallas_call | solution.py:254
  6.4 0.1 collective-permute-start.4
  6.4 0.6 %collective-permute-start.6 = (bf16[1,2,64,256]{3,2,1,0:T(8,128)(2,1)S(1)}, bf16[1,2,64,256]{3,2,1,0:T(8,128)(2,1)S(1)}, u32[]{:S(2)}, u32[]{:S(2)}) collective-permute-start(bf16[1,2,64,256]{3,2,1,0:T(8,128)(2,1)S(1)} %bitcast.7), channel_id=1, source_target_pairs={{0,4},{2,6},{4,0},{6,2},{8,12},{10,14},{12,8},{14,10},{16,20},{18,... | collective-permute-start | bytes 196616 | tf_op jit(solution)/shard_map/ppermute | solution.py:32
  7.1 1.7 %collective-permute-start.1 = (bf16[1,2,64,256]{3,2,1,0:T(8,128)(2,1)S(1)}, bf16[1,2,64,256]{3,2,1,0:T(8,128)(2,1)S(1)}, u32[]{:S(2)}, u32[]{:S(2)}) collective-permute-start(bf16[1,2,64,256]{3,2,1,0:T(8,128)(2,1)S(1)} %bitcast.8), channel_id=1, source_target_pairs={{0,16},{2,18},{4,20},{6,22},{8,24},{10,26},{12,28},{14,30},{16,0},... | collective-permute-start | bytes 196616 | tf_op jit(solution)/shard_map/ppermute | solution.py:32
  8.8 0.0 collective-permute-done.refs_1_
  8.8 0.9 %collective-permute-start.10 = (bf16[1,2,64,256]{3,2,1,0:T(8,128)(2,1)S(1)}, bf16[1,2,64,256]{3,2,1,0:T(8,128)(2,1)S(1)}, u32[]{:S(2)}, u32[]{:S(2)}) collective-permute-start(bf16[1,2,64,256]{3,2,1,0:T(8,128)(2,1)S(1)} %collective-permute-done.refs_1_), channel_id=1, source_target_pairs={{0,16},{2,18},{4,20},{6,22},{8,24},{10,26},{12,28},{14,30},{16,0},... | collective-permute-start | bytes 196616 | tf_op jit(solution)/shard_map/ppermute | solution.py:32
  9.7 0.0 collective-permute-done.3.refs_3_
  9.7 1.4 %collective-permute-start.9 = (bf16[1,2,64,256]{3,2,1,0:T(8,128)(2,1)S(1)}, bf16[1,2,64,256]{3,2,1,0:T(8,128)(2,1)S(1)}, u32[]{:S(2)}, u32[]{:S(2)}) collective-permute-start(bf16[1,2,64,256]{3,2,1,0:T(8,128)(2,1)S(1)} %collective-permute-done.3.refs_3_), channel_id=1, source_target_pairs={{0,16},{2,18},{4,20},{6,22},{8,24},{10,26},{12,28},{14,30},{16,0},... | collective-permute-start | bytes 196616 | tf_op jit(solution)/shard_map/ppermute | solution.py:32
  11.0 0.0 collective-permute-done.4.refs_4_
  11.0 0.0 collective-permute-start.5
  11.0 0.8 %collective-permute-done.6.refs_10_ = bf16[1,2,64,256]{3,2,1,0:T(8,128)(2,1)S(1)} collective-permute-done((bf16[1,2,64,256]{3,2,1,0:T(8,128)(2,1)S(1)}, bf16[1,2,64,256]{3,2,1,0:T(8,128)(2,1)S(1)}, u32[]{:S(2)}, u32[]{:S(2)}) %collective-permute-start.6) | collective-permute-done | bytes 65568 | tf_op jit(solution)/shard_map/ppermute | solution.py:32
  11.8 0.0 collective-permute-start.7
  11.8 0.0 collective-permute-done.1.refs_5_
  11.8 1.9 %collective-permute-start.13 = (bf16[1,2,64,256]{3,2,1,0:T(8,128)(2,1)S(1)}, bf16[1,2,64,256]{3,2,1,0:T(8,128)(2,1)S(1)}, u32[]{:S(2)}, u32[]{:S(2)}) collective-permute-start(bf16[1,2,64,256]{3,2,1,0:T(8,128)(2,1)S(1)} %collective-permute-done.6.refs_10_), channel_id=1, source_target_pairs={{0,16},{2,18},{4,20},{6,22},{8,24},{10,26},{12,28},{14,30},{16,0},... | collective-permute-start | bytes 196616 | tf_op jit(solution)/shard_map/ppermute | solution.py:32
  13.7 0.0 collective-permute-done.10.refs_9_
  13.7 0.0 collective-permute-start.8
  13.7 0.4 %collective-permute-done.9.refs_8_ = bf16[1,2,64,256]{3,2,1,0:T(8,128)(2,1)S(1)} collective-permute-done((bf16[1,2,64,256]{3,2,1,0:T(8,128)(2,1)S(1)}, bf16[1,2,64,256]{3,2,1,0:T(8,128)(2,1)S(1)}, u32[]{:S(2)}, u32[]{:S(2)}) %collective-permute-start.9) | collective-permute-done | bytes 65568 | tf_op jit(solution)/shard_map/ppermute | solution.py:32
  14.1 0.1 collective-permute-start.2
  14.2 0.4 %collective-permute-start.11 = (bf16[1,2,64,256]{3,2,1,0:T(8,128)(2,1)S(1)}, bf16[1,2,64,256]{3,2,1,0:T(8,128)(2,1)S(1)}, u32[]{:S(2)}, u32[]{:S(2)}) collective-permute-start(bf16[1,2,64,256]{3,2,1,0:T(8,128)(2,1)S(1)} %collective-permute-done.10.refs_9_), channel_id=1, source_target_pairs={{0,8},{2,10},{4,12},{6,14},{8,0},{10,2},{12,4},{14,6},{16,24},{18,... | collective-permute-start | bytes 196616 | tf_op jit(solution)/shard_map/ppermute | solution.py:32
  14.7 0.0 collective-permute-done.7.refs_6_
  14.7 0.1 collective-permute-start.12
  14.7 1.6 %collective-permute-done.13.refs_7_ = bf16[1,2,64,256]{3,2,1,0:T(8,128)(2,1)S(1)} collective-permute-done((bf16[1,2,64,256]{3,2,1,0:T(8,128)(2,1)S(1)}, bf16[1,2,64,256]{3,2,1,0:T(8,128)(2,1)S(1)}, u32[]{:S(2)}, u32[]{:S(2)}) %collective-permute-start.13) | collective-permute-done | bytes 65568 | tf_op jit(solution)/shard_map/ppermute | solution.py:32
  16.4 0.0 collective-permute-done.2.refs_2_
  16.4 0.0 collective-permute-done.11.refs_11_
  16.4 0.7 %attend_early.1 = (f32[2,384,128]{2,1,0:T(8,128)S(1)}, f32[2,384,128]{2,1,0:T(8,128)S(1)}, f32[2,384,128]{2,1,0:T(8,128)S(1)}, f32[64,1536]{1,0:T(8,128)S(1)}, f32[1,64]{1,0:T(1,128)S(1)}) custom-call(bf16[2,384,128]{2,1,0:T(8,128)(2,1)S(1)} %get-tuple-element.18.rows_ref, f32[8,1024]{1,0:T(8,128)S(1)} %get-tuple-element.19.bias_ref, ...), custom_call_target="tpu_custom_call" | custom-call | tf_op jit(solution)/shard_map/attend_early/pallas_call | solution.py:266
  17.1 0.0 collective-permute-done.12.refs_6_
  17.1 0.5 %collective-permute-done.14.refs_8_ = bf16[1,2,64,256]{3,2,1,0:T(8,128)(2,1)S(1)} collective-permute-done((bf16[1,2,64,256]{3,2,1,0:T(8,128)(2,1)S(1)}, bf16[1,2,64,256]{3,2,1,0:T(8,128)(2,1)S(1)}, u32[]{:S(2)}, u32[]{:S(2)}) %collective-permute-start.14) | collective-permute-done | bytes 65568 | tf_op jit(solution)/shard_map/ppermute | solution.py:32
  17.6 1.5 %collective-permute-start.15 = (f32[1,64]{1,0:T(1,128)S(1)}, f32[1,64]{1,0:T(1,128)S(1)}, u32[]{:S(2)}, u32[]{:S(2)}) collective-permute-start(f32[1,64]{1,0:T(1,128)S(1)} %get-tuple-element.30.own_ref), channel_id=1, source_target_pairs={{0,1},{1,0},{2,3},{3,2},{4,5},{5,4},{6,7},{7,6},{8,9},{9,8},{10,11... | collective-permute-start | bytes 776 | tf_op jit(solution)/shard_map/ppermute | solution.py:32
  19.2 2.0 %collective-permute-done.15.other_ref = f32[1,64]{1,0:T(1,128)S(1)} collective-permute-done((f32[1,64]{1,0:T(1,128)S(1)}, f32[1,64]{1,0:T(1,128)S(1)}, u32[]{:S(2)}, u32[]{:S(2)}) %collective-permute-start.15) | collective-permute-done | bytes 288 | tf_op jit(solution)/shard_map/ppermute | solution.py:32
  21.2 0.8 %finish.1 = bf16[1,64,1536]{2,1,0:T(8,128)(2,1)} custom-call(f32[64,1536]{1,0:T(8,128)S(1)} %gain.1.gained_ref, f32[1,64]{1,0:T(1,128)S(1)} %get-tuple-element.30.own_ref, f32[1,64]{1,0:T(1,128)S(1)} %collective-permute-done.15.other_ref), custom_call_target="tpu_custom_call" | custom-call | tf_op jit(solution)/shard_map/finish/pallas_call | solution.py:277
  (7 shorter events, 0.0 us)
Async XLA Ops:
  0.0 8.8 %collective-permute-start = (bf16[1,2,64,256]{3,2,1,0:T(8,128)(2,1)}, bf16[1,2,64,256]{3,2,1,0:T(8,128)(2,1)S(1)}, u32[]{:S(2)}, u32[]{:S(2)}) collective-permute-start(bf16[1,2,64,256]{3,2,1,0:T(8,128)(2,1)} %bitcast.3), channel_id=1, source_target_pairs={{0,6},{2,4},{4,2},{6,0},{8,14},{10,12},{12,10},{14,8},{16,22},{18,... | collective-permute-start | bytes 196616 | tf_op jit(solution)/shard_map/ppermute | solution.py:32
  5.0 4.6 %collective-permute-start.3 = (bf16[1,2,64,256]{3,2,1,0:T(8,128)(2,1)}, bf16[1,2,64,256]{3,2,1,0:T(8,128)(2,1)S(1)}, u32[]{:S(2)}, u32[]{:S(2)}) collective-permute-start(bf16[1,2,64,256]{3,2,1,0:T(8,128)(2,1)} %bitcast.4), channel_id=1, source_target_pairs={{0,2},{2,0},{4,6},{6,4},{8,10},{10,8},{12,14},{14,12},{16,18},{18,... | collective-permute-start | bytes 196616 | tf_op jit(solution)/shard_map/ppermute | solution.py:32
  5.1 1.3 %copy-start = (bf16[2,1,64,256]{3,2,1,0:T(8,128)(2,1)S(1)}, bf16[2,1,64,256]{3,2,1,0:T(8,128)(2,1)}, u32[]{:S(2)}) copy-start(bf16[2,1,64,256]{3,2,1,0:T(8,128)(2,1)} %param.7) | copy-start | bytes 196612
  6.4 4.7 %collective-permute-start.4 = (bf16[1,2,64,256]{3,2,1,0:T(8,128)(2,1)S(1)}, bf16[1,2,64,256]{3,2,1,0:T(8,128)(2,1)S(1)}, u32[]{:S(2)}, u32[]{:S(2)}) collective-permute-start(bf16[1,2,64,256]{3,2,1,0:T(8,128)(2,1)S(1)} %bitcast.6), channel_id=1, source_target_pairs={{0,8},{2,10},{4,12},{6,14},{8,0},{10,2},{12,4},{14,6},{16,24},{18,... | collective-permute-start | bytes 196616 | tf_op jit(solution)/shard_map/ppermute | solution.py:32
  6.4 5.4 %collective-permute-start.6 = (bf16[1,2,64,256]{3,2,1,0:T(8,128)(2,1)S(1)}, bf16[1,2,64,256]{3,2,1,0:T(8,128)(2,1)S(1)}, u32[]{:S(2)}, u32[]{:S(2)}) collective-permute-start(bf16[1,2,64,256]{3,2,1,0:T(8,128)(2,1)S(1)} %bitcast.7), channel_id=1, source_target_pairs={{0,4},{2,6},{4,0},{6,2},{8,12},{10,14},{12,8},{14,10},{16,20},{18,... | collective-permute-start | bytes 196616 | tf_op jit(solution)/shard_map/ppermute | solution.py:32
  7.1 4.8 %collective-permute-start.1 = (bf16[1,2,64,256]{3,2,1,0:T(8,128)(2,1)S(1)}, bf16[1,2,64,256]{3,2,1,0:T(8,128)(2,1)S(1)}, u32[]{:S(2)}, u32[]{:S(2)}) collective-permute-start(bf16[1,2,64,256]{3,2,1,0:T(8,128)(2,1)S(1)} %bitcast.8), channel_id=1, source_target_pairs={{0,16},{2,18},{4,20},{6,22},{8,24},{10,26},{12,28},{14,30},{16,0},... | collective-permute-start | bytes 196616 | tf_op jit(solution)/shard_map/ppermute | solution.py:32
  8.8 4.9 %collective-permute-start.10 = (bf16[1,2,64,256]{3,2,1,0:T(8,128)(2,1)S(1)}, bf16[1,2,64,256]{3,2,1,0:T(8,128)(2,1)S(1)}, u32[]{:S(2)}, u32[]{:S(2)}) collective-permute-start(bf16[1,2,64,256]{3,2,1,0:T(8,128)(2,1)S(1)} %collective-permute-done.refs_1_), channel_id=1, source_target_pairs={{0,16},{2,18},{4,20},{6,22},{8,24},{10,26},{12,28},{14,30},{16,0},... | collective-permute-start | bytes 196616 | tf_op jit(solution)/shard_map/ppermute | solution.py:32
  9.7 4.5 %collective-permute-start.9 = (bf16[1,2,64,256]{3,2,1,0:T(8,128)(2,1)S(1)}, bf16[1,2,64,256]{3,2,1,0:T(8,128)(2,1)S(1)}, u32[]{:S(2)}, u32[]{:S(2)}) collective-permute-start(bf16[1,2,64,256]{3,2,1,0:T(8,128)(2,1)S(1)} %collective-permute-done.3.refs_3_), channel_id=1, source_target_pairs={{0,16},{2,18},{4,20},{6,22},{8,24},{10,26},{12,28},{14,30},{16,0},... | collective-permute-start | bytes 196616 | tf_op jit(solution)/shard_map/ppermute | solution.py:32
  11.0 3.2 %collective-permute-start.5 = (bf16[1,2,64,256]{3,2,1,0:T(8,128)(2,1)S(1)}, bf16[1,2,64,256]{3,2,1,0:T(8,128)(2,1)S(1)}, u32[]{:S(2)}, u32[]{:S(2)}) collective-permute-start(bf16[1,2,64,256]{3,2,1,0:T(8,128)(2,1)S(1)} %collective-permute-done.3.refs_3_), channel_id=1, source_target_pairs={{0,8},{2,10},{4,12},{6,14},{8,0},{10,2},{12,4},{14,6},{16,24},{18,... | collective-permute-start | bytes 196616 | tf_op jit(solution)/shard_map/ppermute | solution.py:32
  11.8 2.8 %collective-permute-start.7 = (bf16[1,2,64,256]{3,2,1,0:T(8,128)(2,1)S(1)}, bf16[1,2,64,256]{3,2,1,0:T(8,128)(2,1)S(1)}, u32[]{:S(2)}, u32[]{:S(2)}) collective-permute-start(bf16[1,2,64,256]{3,2,1,0:T(8,128)(2,1)S(1)} %collective-permute-done.6.refs_10_), channel_id=1, source_target_pairs={{0,8},{2,10},{4,12},{6,14},{8,0},{10,2},{12,4},{14,6},{16,24},{18,... | collective-permute-start | bytes 196616 | tf_op jit(solution)/shard_map/ppermute | solution.py:32
  11.8 4.5 %collective-permute-start.13 = (bf16[1,2,64,256]{3,2,1,0:T(8,128)(2,1)S(1)}, bf16[1,2,64,256]{3,2,1,0:T(8,128)(2,1)S(1)}, u32[]{:S(2)}, u32[]{:S(2)}) collective-permute-start(bf16[1,2,64,256]{3,2,1,0:T(8,128)(2,1)S(1)} %collective-permute-done.6.refs_10_), channel_id=1, source_target_pairs={{0,16},{2,18},{4,20},{6,22},{8,24},{10,26},{12,28},{14,30},{16,0},... | collective-permute-start | bytes 196616 | tf_op jit(solution)/shard_map/ppermute | solution.py:32
  13.7 2.6 %collective-permute-start.8 = (bf16[1,2,64,256]{3,2,1,0:T(8,128)(2,1)S(1)}, bf16[1,2,64,256]{3,2,1,0:T(8,128)(2,1)S(1)}, u32[]{:S(2)}, u32[]{:S(2)}) collective-permute-start(bf16[1,2,64,256]{3,2,1,0:T(8,128)(2,1)S(1)} %collective-permute-done.refs_1_), channel_id=1, source_target_pairs={{0,8},{2,10},{4,12},{6,14},{8,0},{10,2},{12,4},{14,6},{16,24},{18,... | collective-permute-start | bytes 196616 | tf_op jit(solution)/shard_map/ppermute | solution.py:32
  14.1 2.2 %collective-permute-start.2 = (bf16[1,2,64,256]{3,2,1,0:T(8,128)(2,1)S(1)}, bf16[1,2,64,256]{3,2,1,0:T(8,128)(2,1)S(1)}, u32[]{:S(2)}, u32[]{:S(2)}) collective-permute-start(bf16[1,2,64,256]{3,2,1,0:T(8,128)(2,1)S(1)} %collective-permute-done.1.refs_5_), channel_id=1, source_target_pairs={{0,8},{2,10},{4,12},{6,14},{8,0},{10,2},{12,4},{14,6},{16,24},{18,... | collective-permute-start | bytes 196616 | tf_op jit(solution)/shard_map/ppermute | solution.py:32
  14.2 2.1 %collective-permute-start.11 = (bf16[1,2,64,256]{3,2,1,0:T(8,128)(2,1)S(1)}, bf16[1,2,64,256]{3,2,1,0:T(8,128)(2,1)S(1)}, u32[]{:S(2)}, u32[]{:S(2)}) collective-permute-start(bf16[1,2,64,256]{3,2,1,0:T(8,128)(2,1)S(1)} %collective-permute-done.10.refs_9_), channel_id=1, source_target_pairs={{0,8},{2,10},{4,12},{6,14},{8,0},{10,2},{12,4},{14,6},{16,24},{18,... | collective-permute-start | bytes 196616 | tf_op jit(solution)/shard_map/ppermute | solution.py:32
  14.7 2.4 %collective-permute-start.12 = (bf16[1,2,64,256]{3,2,1,0:T(8,128)(2,1)S(1)}, bf16[1,2,64,256]{3,2,1,0:T(8,128)(2,1)S(1)}, u32[]{:S(2)}, u32[]{:S(2)}) collective-permute-start(bf16[1,2,64,256]{3,2,1,0:T(8,128)(2,1)S(1)} %collective-permute-done.9.refs_8_), channel_id=1, source_target_pairs={{0,8},{2,10},{4,12},{6,14},{8,0},{10,2},{12,4},{14,6},{16,24},{18,... | collective-permute-start | bytes 196616 | tf_op jit(solution)/shard_map/ppermute | solution.py:32
  16.4 1.3 %collective-permute-start.14 = (bf16[1,2,64,256]{3,2,1,0:T(8,128)(2,1)S(1)}, bf16[1,2,64,256]{3,2,1,0:T(8,128)(2,1)S(1)}, u32[]{:S(2)}, u32[]{:S(2)}) collective-permute-start(bf16[1,2,64,256]{3,2,1,0:T(8,128)(2,1)S(1)} %collective-permute-done.13.refs_7_), channel_id=1, source_target_pairs={{0,8},{2,10},{4,12},{6,14},{8,0},{10,2},{12,4},{14,6},{16,24},{18,... | collective-permute-start | bytes 196616 | tf_op jit(solution)/shard_map/ppermute | solution.py:32
  17.6 3.6 %collective-permute-start.15 = (f32[1,64]{1,0:T(1,128)S(1)}, f32[1,64]{1,0:T(1,128)S(1)}, u32[]{:S(2)}, u32[]{:S(2)}) collective-permute-start(f32[1,64]{1,0:T(1,128)S(1)} %get-tuple-element.30.own_ref), channel_id=1, source_target_pairs={{0,1},{1,0},{2,3},{3,2},{4,5},{5,4},{6,7},{7,6},{8,9},{9,8},{10,11... | collective-permute-start | bytes 776 | tf_op jit(solution)/shard_map/ppermute | solution.py:32
